TPU v7x, 32 devices: a whole 2x2x4 slice. The times are simulated.
32 devices in a mesh: dp: 8 (over z, x), tensor: 4 (over y, core).
Axes of the slice: x: 2, y: 2, z: 4, core: 2. Of those that a mesh axis runs over, the one named last changes fastest.
Arguments:
- tokens: bfloat16 [256, 6144], P('dp', 'tensor'), may hold values from -32 to 32
- gain_in: float32 [6144], P('tensor'), may hold values from 0.1 to 1.9
- shift_in: float32 [6144], P('tensor'), may hold values from -3 to 3
- up_weight: bfloat16 [6144, 24576], P('tensor', 'dp'), may hold values from -0.078125 to 0.078125
- up_bias: float32 [24576], P('dp'), may hold values from -3 to 3
- down_weight: bfloat16 [24576, 6144], P('dp', 'tensor'), may hold values from -1 to 1
- gain_out: float32 [6144], P('tensor'), may hold values from 0.1 to 1.9
- curvature: float32 [256, 6144], P('dp', 'tensor'), may hold values from 0.5 to 12
- up_tangent: bfloat16 [6144, 24576], P('tensor', 'dp'), may hold values from -0.078125 to 0.078125
- down_tangent: bfloat16 [24576, 6144], P('dp', 'tensor'), may hold values from -1 to 1
Outputs:
- up_product: float32 [6144, 24576], P('tensor', 'dp')
- down_product: float32 [24576, 6144], P('dp', 'tensor')
All inputs are finite; a program needn't handle non-finite values.
Results may differ from a plain program's by a relative error of at most 0.003.
Values may be sent and summed in bfloat16 or wider, within the bound.
No kernel may reach another device: no remote copies, remote signals or barrier semaphores. Data moves between devices by JAX's collectives and lax.ppermute only.
A program may use at most 128 MiB of HBM per device.

v0:
```python
import jax
import jax.numpy as jnp
from jax import lax
from jax.sharding import PartitionSpec as P

D = 6144


epsilon = 1e-05
root_half = 0.7071067811865476
inv_root_two_pi = 0.3989422804014327


def gelu_value(values):
    return 0.5 * values * (1.0 + lax.erf(values * root_half))


def gelu_slope(values):
    return (
        0.5 * (1.0 + lax.erf(values * root_half))
        + values * jnp.exp(-0.5 * values * values) * inv_root_two_pi
    )


def row_total(values):
    return jnp.sum(values, axis=1)


def on_device(
    tokens,
    gain_in,
    shift_in,
    up_weight,
    up_bias,
    down_weight,
    gain_out,
    curvature,
    up_tangent,
    down_tangent,
):
    model_width = float(D)
    source = tokens.astype(jnp.float32)
    sum_in, square_in = lax.psum((row_total(source), row_total(source * source)), "tensor")
    center_in = sum_in / model_width
    spread_in = square_in / model_width - center_in * center_in
    inverse_in = lax.rsqrt(spread_in + epsilon)[:, None]
    normed = ((source - center_in[:, None]) * inverse_in * gain_in + shift_in).astype(jnp.bfloat16)
    all_normed = lax.all_gather(normed, "dp", axis=0, tiled=True)
    pre_part = jnp.dot(all_normed, up_weight, preferred_element_type=jnp.float32)
    tangent_part = jnp.dot(all_normed, up_tangent, preferred_element_type=jnp.float32)
    share_rows = all_normed.shape[0] // lax.axis_size("tensor")
    pre_total, tangent_total = lax.psum((pre_part, tangent_part), "tensor")
    pre_full = pre_total + up_bias
    slope_full = gelu_slope(pre_full)
    hidden = gelu_value(pre_full).astype(jnp.bfloat16)
    hidden_tangent = (slope_full * tangent_total).astype(jnp.bfloat16)
    slope_rows = lax.dynamic_slice_in_dim(
        slope_full, lax.axis_index("tensor") * share_rows, share_rows, 0
    )
    slope_kept = lax.optimization_barrier(slope_rows.astype(jnp.bfloat16))
    primal = jnp.dot(hidden, down_weight, preferred_element_type=jnp.float32)
    tangent = jnp.dot(hidden_tangent, down_weight, preferred_element_type=jnp.float32) + jnp.dot(
        hidden, down_tangent, preferred_element_type=jnp.float32
    )
    both_outputs = lax.psum_scatter(
        jnp.concatenate([primal, tangent], axis=1), "dp", scatter_dimension=0, tiled=True
    )
    local_width = down_weight.shape[1]
    output = source + both_outputs[:, :local_width]
    output_tangent = both_outputs[:, local_width:]
    factor = gain_out * gain_out * curvature
    sum_out, square_out = lax.psum((row_total(output), row_total(output * output)), "tensor")
    center_out = sum_out / model_width
    inverse_out = lax.rsqrt(square_out / model_width - center_out * center_out + epsilon)[:, None]
    normal_out = (output - center_out[:, None]) * inverse_out
    tangent_sum, tangent_dot = lax.psum(
        (row_total(output_tangent), row_total(normal_out * output_tangent)), "tensor"
    )
    normal_tangent = (
        output_tangent
        - (tangent_sum / model_width)[:, None]
        - normal_out * (tangent_dot / model_width)[:, None]
    ) * inverse_out
    weighted = factor * normal_tangent
    weight_sum, weight_dot = lax.psum(
        (row_total(weighted), row_total(normal_out * weighted)), "tensor"
    )
    cotangent = (
        (
            weighted
            - (weight_sum / model_width)[:, None]
            - normal_out * (weight_dot / model_width)[:, None]
        )
        * inverse_out
    ).astype(jnp.bfloat16)
    all_cotangent = lax.all_gather(cotangent, "dp", axis=0, tiled=True)
    back_part = lax.dot_general(
        all_cotangent, down_weight, (((1,), (1,)), ((), ())), preferred_element_type=jnp.float32
    )
    down_product = lax.dot_general(
        hidden, all_cotangent, (((0,), (0,)), ((), ())), preferred_element_type=jnp.float32
    )
    back_share = lax.psum_scatter(back_part, "tensor", scatter_dimension=0, tiled=True)
    grad_share = (back_share * slope_kept.astype(jnp.float32)).astype(jnp.bfloat16)
    grad_pre = lax.all_gather(grad_share, "tensor", axis=0, tiled=True)
    up_product = lax.dot_general(
        all_normed, grad_pre, (((0,), (0,)), ((), ())), preferred_element_type=jnp.float32
    )
    return (up_product, down_product)


def solution(mesh):
    return jax.shard_map(
        on_device,
        mesh=mesh,
        in_specs=(
            P("dp", "tensor"),
            P("tensor"),
            P("tensor"),
            P("tensor", "dp"),
            P("dp"),
            P("dp", "tensor"),
            P("tensor"),
            P("dp", "tensor"),
            P("tensor", "dp"),
            P("dp", "tensor"),
        ),
        out_specs=(P("tensor", "dp"), P("dp", "tensor")),
        check_vma=False,
    )
```

profile of v0, /device:TPU:0, one launch (start us, length us, event | category | flops | bytes accessed | tf_op | source)
XLA Modules:
  0.0 411.7 jit_solution(12184081527667012065)
XLA Ops:
  7.2 0.0 all-reduce.7.cloned.1.call-start
  7.2 1.0 convert_reduce_fusion
  8.2 8.4 %all-reduce.3 = (f32[32]{0:T(128)S(1)}, f32[32]{0:T(128)S(1)}) all-reduce(f32[32]{0:T(128)S(1)} %get-tuple-element.9, f32[32]{0:T(128)S(1)} %get-tuple-element.8), channel_id=1, replica_groups=mesh['dp'=8,'tensor'=4] {'tensor'}, use_global_device_ids=true, to_apply=%region_3.0 | all-reduce | flops 64 | bytes 512 | tf_op jit(solution)/shard_map/psum | solution.py:43
  16.6 1.0 fusion.8
  17.6 0.0 slice-start
  17.6 32.7 %all_gather.9 = bf16[256,1536]{1,0:T(8,128)(2,1)S(1)} all-gather(bf16[32,1536]{1,0:T(8,128)(2,1)S(1)} %fusion.8), channel_id=1, replica_groups=mesh['dp'=8,'tensor'=4] {'dp'}, dimensions={0}, use_global_device_ids=true | all-gather | bytes 884736 | tf_op jit(solution)/shard_map/all_gather | solution.py:48
  50.4 8.1 %fusion.14 = f32[256,3072]{1,0:T(8,128)} fusion(bf16[256,1536]{1,0:T(8,128)(2,1)S(1)} %all_gather.9, bf16[1536,3072]{1,0:T(8,128)(2,1)} %param.18), kind=kOutput, calls=%fused_computation.41 | convolution fusion | flops 2415919104 | bytes 13369344 | tf_op jit(solution)/shard_map/dot_general | solution.py:50
  58.5 0.0 slice-done
  58.5 4.3 %fusion.12 = f32[256,3072]{1,0:T(8,128)} fusion(bf16[256,1536]{1,0:T(8,128)(2,1)S(1)} %all_gather.9, bf16[1536,3072]{1,0:T(8,128)(2,1)S(1)} %bitcast.16), kind=kOutput, calls=%fused_computation.39 | convolution fusion | flops 2415919104 | bytes 13369344 | tf_op jit(solution)/shard_map/dot_general | solution.py:49
  62.8 0.0 all-reduce.7.cloned.1.call-update
  62.8 0.0 reduce-scatter.3.cloned.1.call-start
  62.8 119.7 %all-reduce.7.cloned.1.call-done = (f32[256,3072]{1,0:T(8,128)}, f32[256,3072]{1,0:T(8,128)}) async-done(((f32[256,3072]{1,0:T(8,128)}, f32[256,3072]{1,0:T(8,128)}), (f32[256,3072]{1,0:T(8,128)}, f32[256,3072]{1,0:T(8,128)})) %all-reduce.7.cloned.1.call-update) | async-done | bytes 6291472 | tf_op jit(solution)/shard_map/psum | solution.py:52
  182.5 0.0 copy-done.4
  182.5 3.1 multiply_convert_fusion.1
  185.6 0.0 copy-start
  185.6 0.0 slice-start.7
  185.7 0.0 slice-start.8
  185.7 0.0 copy-start.5
  185.7 0.0 slice-start.3
  185.7 0.0 slice-start.4
  185.7 6.3 %fusion.13 = f32[256,1536]{1,0:T(8,128)S(1)} fusion(bf16[256,3072]{1,0:T(8,128)(2,1)S(1)} %get-tuple-element.22, bf16[3072,1536]{1,0:T(8,128)(2,1)} %param.15), kind=kOutput, calls=%fused_computation.40 | convolution fusion | flops 2415919104 | bytes 12582912 | tf_op jit(solution)/shard_map/dot_general | solution.py:61
  192.1 0.9 copy-done.5
  192.9 2.6 fusion.4
  195.6 0.2 slice-done.5
  195.8 2.7 convolution_add_fusion
  198.4 1.9 pad_maximum_fusion
  200.4 0.0 reduce-scatter.3.cloned.1.call-update
  200.4 0.0 reduce-scatter.5.cloned.1.call-start
  200.5 0.6 copy-done.3
  201.1 74.0 %reduce-scatter.3.cloned.1.call-done = f32[32,3072]{1,0:T(8,128)} async-done(((f32[256,3072]{1,0:T(8,128)}), f32[32,3072]{1,0:T(8,128)}) %reduce-scatter.3.cloned.1.call-update) | async-done | bytes 393232 | tf_op jit(solution)/shard_map/reduce_scatter | solution.py:65
  275.0 1.1 fusion.11
  276.1 6.0 %all-reduce.2 = (f32[32]{0:T(128)S(1)}, f32[32]{0:T(128)S(1)}) all-reduce(f32[32]{0:T(128)S(1)} %get-tuple-element.7, f32[32]{0:T(128)S(1)} %get-tuple-element.6), channel_id=1, replica_groups=mesh['dp'=8,'tensor'=4] {'tensor'}, use_global_device_ids=true, to_apply=%region_12.0 | all-reduce | flops 64 | bytes 512 | tf_op jit(solution)/shard_map/psum | solution.py:72
  282.1 1.1 slice_reduce_fusion
  283.2 6.3 %all-reduce.1 = (f32[32]{0:T(128)S(1)}, f32[32]{0:T(128)S(1)}) all-reduce(f32[32]{0:T(128)S(1)} %get-tuple-element.3, f32[32]{0:T(128)S(1)} %get-tuple-element.2), channel_id=1, replica_groups=mesh['dp'=8,'tensor'=4] {'tensor'}, use_global_device_ids=true, to_apply=%region_14.0 | all-reduce | flops 64 | bytes 512 | tf_op jit(solution)/shard_map/psum | solution.py:76
  289.5 1.2 fusion.10
  290.7 5.9 %all-reduce = (f32[32]{0:T(128)S(1)}, f32[32]{0:T(128)S(1)}) all-reduce(f32[32]{0:T(128)S(1)} %get-tuple-element.5, f32[32]{0:T(128)S(1)} %get-tuple-element.4), channel_id=1, replica_groups=mesh['dp'=8,'tensor'=4] {'tensor'}, use_global_device_ids=true, to_apply=%region_18.0 | all-reduce | flops 64 | bytes 512 | tf_op jit(solution)/shard_map/psum | solution.py:85
  296.6 0.1 multiply_convert_fusion.4
  296.8 32.3 %all_gather.10 = bf16[256,1536]{1,0:T(8,128)(2,1)S(1)} all-gather(bf16[32,1536]{1,0:T(8,128)(2,1)S(1)} %multiply_convert_fusion.4), channel_id=1, replica_groups=mesh['dp'=8,'tensor'=4] {'dp'}, dimensions={0}, use_global_device_ids=true | all-gather | bytes 884736 | tf_op jit(solution)/shard_map/all_gather | solution.py:96
  329.0 8.0 %fusion.15 = f32[256,3072]{1,0:T(8,128)} fusion(bf16[256,1536]{1,0:T(8,128)(2,1)S(1)} %all_gather.10, bf16[3072,1536]{1,0:T(8,128)(2,1)} %param.15), kind=kOutput, calls=%fused_computation.42 | convolution fusion | flops 2415919104 | bytes 13369344 | tf_op jit(solution)/shard_map/dot_general | solution.py:97
  337.0 0.0 reduce-scatter.5.cloned.1.call-update
  337.0 0.0 all-gather.2.cloned.1.call-start
  337.1 1.2 dynamic-slice_convert_fusion
  338.3 35.4 %reduce-scatter.5.cloned.1.call-done = f32[64,3072]{1,0:T(8,128)} async-done(((f32[256,3072]{1,0:T(8,128)}), f32[64,3072]{1,0:T(8,128)}) %reduce-scatter.5.cloned.1.call-update) | async-done | bytes 786448 | tf_op jit(solution)/shard_map/reduce_scatter | solution.py:103
  373.7 1.9 multiply_convert_fusion.3
  375.7 0.0 all-gather.2.cloned.1.call-update
  375.7 8.3 %fusion.17 = f32[3072,1536]{1,0:T(8,128)} fusion(bf16[256,3072]{1,0:T(8,128)(2,1)S(1)} %get-tuple-element.22, bf16[256,1536]{1,0:T(8,128)(2,1)S(1)} %all_gather.10), kind=kOutput, calls=%fused_computation.44 | convolution fusion | flops 2415919104 | bytes 21233664 | tf_op jit(solution)/shard_map/dot_general | solution.py:100
  384.0 11.5 %all-gather.2.cloned.1.call-done = bf16[256,3072]{1,0:T(8,128)(2,1)} async-done(((bf16[64,3072]{1,0:T(8,128)(2,1)}), bf16[256,3072]{1,0:T(8,128)(2,1)}) %all-gather.2.cloned.1.call-update) | async-done | bytes 1572880 | tf_op jit(solution)/shard_map/all_gather | solution.py:105
  395.5 9.7 %fusion.16 = f32[1536,3072]{1,0:T(8,128)} fusion(bf16[256,1536]{1,0:T(8,128)(2,1)S(1)} %all_gather.9, bf16[256,3072]{1,0:T(8,128)(2,1)} %all-gather.2.cloned.1.call-done), kind=kOutput, calls=%fused_computation.43 | convolution fusion | flops 2415919104 | bytes 21233664 | tf_op jit(solution)/shard_map/dot_general | solution.py:106
  (27 shorter events, 0.1 us)
Async XLA Ops:
  7.2 175.4 %all-reduce.7.cloned.1.call-start = ((), (), s32[]{:S(2)}) async-start(), calls=%async_computation.5 | async-start | bytes 12582912 | tf_op jit(solution)/shard_map/psum | solution.py:52
  17.6 40.8 %slice-start = ((s8[9437184]{0:T(1024)(128)(4,1)}), s8[4194304]{0:T(1024)(128)(4,1)S(1)}, s32[]{:S(2)}) async-start(s8[9437184]{0:T(1024)(128)(4,1)} %bitcast.15), calls=%async_computation.6 | async-start | bytes 8388608
  50.4 8.1 %slice-start.1 = ((s8[9437184]{0:T(1024)(128)(4,1)}), s8[4194304]{0:T(1024)(128)(4,1)S(1)}, s32[]{:S(2)}) async-start(s8[9437184]{0:T(1024)(128)(4,1)} %bitcast.15), calls=%async_computation.7 | async-start | bytes 8388608
  50.4 8.1 %slice-start.2 = ((s8[9437184]{0:T(1024)(128)(4,1)}), s8[1048576]{0:T(1024)(128)(4,1)S(1)}, s32[]{:S(2)}) async-start(s8[9437184]{0:T(1024)(128)(4,1)} %bitcast.15), calls=%async_computation.8 | async-start | bytes 2097152
  62.8 119.8 %copy-start.4 = (f32[3072]{0:T(1024)S(1)}, f32[3072]{0:T(1024)}, u32[]{:S(2)}) copy-start(f32[3072]{0:T(1024)} %param.14) | copy-start | bytes 36868
  62.8 212.2 %reduce-scatter.3.cloned.1.call-start = ((), (), s32[]{:S(2)}) async-start(), calls=%async_computation.2 | async-start | bytes 3538944 | tf_op jit(solution)/shard_map/reduce_scatter | solution.py:65
  182.5 9.5 %slice-start.6 = ((s8[9437184]{0:T(1024)(128)(4,1)}), s8[4194304]{0:T(1024)(128)(4,1)S(1)}, s32[]{:S(2)}) async-start(s8[9437184]{0:T(1024)(128)(4,1)} %bitcast.19), calls=%async_computation.12 | async-start | bytes 8388608
  185.6 6.4 %copy-start = (f32[256,3072]{1,0:T(8,128)}, f32[256,3072]{1,0:T(8,128)S(1)}, u32[]{:S(2)}) copy-start(f32[256,3072]{1,0:T(8,128)S(1)} %get-tuple-element.23) | copy-start | bytes 9437188
  185.6 6.4 %slice-start.7 = ((s8[9437184]{0:T(1024)(128)(4,1)}), s8[4194304]{0:T(1024)(128)(4,1)S(1)}, s32[]{:S(2)}) async-start(s8[9437184]{0:T(1024)(128)(4,1)} %bitcast.19), calls=%async_computation.13 | async-start | bytes 8388608
  185.7 6.4 %slice-start.8 = ((s8[9437184]{0:T(1024)(128)(4,1)}), s8[1048576]{0:T(1024)(128)(4,1)S(1)}, s32[]{:S(2)}) async-start(s8[9437184]{0:T(1024)(128)(4,1)} %bitcast.19), calls=%async_computation.14 | async-start | bytes 2097152
  185.7 7.3 %copy-start.5 = (f32[256,3072]{1,0:T(8,128)S(1)}, f32[256,3072]{1,0:T(8,128)}, u32[]{:S(2)}) copy-start(f32[256,3072]{1,0:T(8,128)} %get-tuple-element.19) | copy-start | bytes 9437188
  185.7 9.9 %slice-start.3 = ((s8[9437184]{0:T(1024)(128)(4,1)}), s8[4194304]{0:T(1024)(128)(4,1)S(1)}, s32[]{:S(2)}) async-start(s8[9437184]{0:T(1024)(128)(4,1)} %bitcast.17), calls=%async_computation.9 | async-start | bytes 8388608
  185.7 9.9 %slice-start.4 = ((s8[9437184]{0:T(1024)(128)(4,1)}), s8[4194304]{0:T(1024)(128)(4,1)S(1)}, s32[]{:S(2)}) async-start(s8[9437184]{0:T(1024)(128)(4,1)} %bitcast.17), calls=%async_computation.10 | async-start | bytes 8388608
  192.9 2.8 slice-start.5
  200.4 0.7 copy-start.3
  200.4 74.7 %copy-start.1 = (bf16[32,1536]{1,0:T(8,128)(2,1)S(1)}, bf16[32,1536]{1,0:T(8,128)(2,1)}, u32[]{:S(2)}) copy-start(bf16[32,1536]{1,0:T(8,128)(2,1)} %param.10) | copy-start | bytes 294916
  200.4 89.2 %copy-start.2 = (f32[32,1536]{1,0:T(8,128)S(1)}, f32[32,1536]{1,0:T(8,128)}, u32[]{:S(2)}) copy-start(f32[32,1536]{1,0:T(8,128)} %param.17) | copy-start | bytes 589828
  200.4 173.3 %reduce-scatter.5.cloned.1.call-start = ((), (), s32[]{:S(2)}) async-start(), calls=%async_computation.3 | async-start | bytes 3932160 | tf_op jit(solution)/shard_map/reduce_scatter | solution.py:103
  337.0 58.4 %all-gather.2.cloned.1.call-start = ((), (), s32[]{:S(2)}) async-start(), calls=%async_computation.4 | async-start | bytes 1966080 | tf_op jit(solution)/shard_map/all_gather | solution.py:105
Sparse Core Ops, SparseCore 0:
  62.9 119.5 all-reduce.6
  200.5 74.4 reduce-scatter.2
  337.2 36.4 reduce-scatter.4
  375.8 19.6 all-gather.1
where the time goes:
time: 412 us
  waiting for transfers between devices  241 us (58%)
  blocking collectives  91.6 us (22%)
  matrix products  49.9 us (12%)
  between operations  13.9 us (3%)
  other arithmetic  12.5 us (3%)
    psum x1, waiting for transfers between devices, on_device(): pre_total, tangent_total = lax.psum((pre_part, tangent_part), 'tensor')  120 us
    reduce_scatter x1, waiting for transfers between devices, on_device(): lax.psum_scatter(jnp.concatenate([primal, tangent], axis=1), 'dp', scatte...  74 us
    reduce_scatter x1, waiting for transfers between devices, on_device(): lax.psum_scatter(back_part, 'tensor', scatter_dimension=0, tiled=True)  35.4 us
    all_gather x1, blocking collectives, on_device(): all_normed = lax.all_gather(normed, 'dp', axis=0, tiled=True)  32.7 us
    all_gather x1, blocking collectives, on_device(): all_cotangent = lax.all_gather(cotangent, 'dp', axis=0, tiled=True)  32.3 us
    all_gather x1, waiting for transfers between devices, on_device(): grad_pre = lax.all_gather(grad_share, 'tensor', axis=0, tiled=True)  11.5 us
    dot_general x1, matrix products, on_device(): lax.dot_general(all_normed, grad_pre, (((0,), (0,)), ((), ())), preferred...  9.68 us
    psum x1, blocking collectives, on_device(): lax.psum((row_total(source), row_total(source * source)), 'tensor')  8.37 us
  transfers between devices with their start and end apart: 4, of which 4 were waited for; matrix products, arithmetic and copies ran while one was open for 2% of the time, Pallas kernels for 0%

commit v1 on v0

v1 whole, which is shorter than its diff:
```python
import functools

import jax
import jax.numpy as jnp
from jax import lax
from jax.experimental import pallas as pl
from jax.experimental.pallas import tpu as pltpu
from jax.sharding import PartitionSpec as P

D = 6144
TILE = 256
LANES = 128
LOADS = 4
SLOTS = 6
SCALE = 1000
BF16 = jnp.bfloat16
F32 = jnp.float32
PARAMS = pltpu.CompilerParams(vmem_limit_bytes=20 * 1024 * 1024)


epsilon = 1e-05
root_half = 0.7071067811865476
inv_root_two_pi = 0.3989422804014327


def swap_tensor(value, flip):
    size = lax.axis_size("tensor")
    return lax.ppermute(value, "tensor", [(t, t ^ flip) for t in range(size)])


def swap_dp(value, flip):
    size = lax.axis_size("dp")
    return lax.ppermute(value, "dp", [(i, i ^ flip) for i in range(size)])


def after(value, *earlier):
    return lax.optimization_barrier((value, *earlier))[0]


def swap_rows(values):
    half = values.shape[0] // 2
    return jnp.concatenate([values[half:], values[:half]], axis=0)


def far_bits():
    return [1 << k for k in range(1, lax.axis_size("dp").bit_length() - 1)]


def gather_rows(value, beside=None):
    half = value.shape[0] // 2
    count = lax.axis_size("dp")
    held = {0: value}
    for bit in reversed(far_bits()):
        held |= {far | bit: swap_dp(block, bit) for far, block in held.items()}
    held |= {far | 1: swap_dp(block, 1) for far, block in held.items()}
    made = beside(held[count - 2]) if beside else ()
    blocks = [held[place] for place in range(count - 1)] + [after(held[count - 1], *made)]
    rows = jnp.concatenate(
        [block[:half] for block in blocks] + [block[half:] for block in blocks], axis=0
    )
    return rows, made


def scatter_rows(parts, rows):
    half = rows // 2
    count = lax.axis_size("dp")

    def block(place):
        cuts = [
            part[k * count * half + place * half : k * count * half + (place + 1) * half]
            for part in parts
            for k in (0, 1)
        ]
        return jnp.concatenate(cuts, axis=0)

    order = list(range(count - 2, -1, -2))
    terms = {}
    for k, far in enumerate(order):
        sent = block(far + 1).astype(BF16)
        if k >= 1:
            sent = after(sent, *[terms[o][1] for o in order[: max(1, k - 1)]])
        terms[far] = [block(far), swap_dp(sent, 1)]
    pending = [(far, bit) for bit in far_bits() for far in order if far & bit and far & (bit - 1) < 2]
    pending.sort(key=lambda step: [-step[0], step[1]])
    last = []
    for far, bit in pending:
        total = sum(term.astype(F32) for term in terms[far]).astype(BF16)
        total = after(total, *last) if last else total
        last = [total]
        terms[far ^ bit].append(swap_dp(total, bit))
    return terms[0]


def whole(array):
    return pl.BlockSpec(array.shape, lambda *_: (0,) * array.ndim)


def cost(flops, *arrays):
    moved = sum(a.size * a.dtype.itemsize for a in arrays)
    return pl.CostEstimate(
        flops=int(flops) // SCALE, bytes_accessed=int(moved) // SCALE, transcendentals=0
    )


def load_kernel(start, count, *refs):
    refs, sems = refs[:count] + refs[-1 - count : -1], refs[-1]
    copies = []
    for k in range(count):
        given, held = refs[k], refs[count + k]
        rows, width = held.shape
        step = rows // LOADS
        for n in range(LOADS):
            cut = pl.ds(n * step, step)
            place = given.at[cut, pl.ds(start, width)]
            copies.append(pltpu.make_async_copy(place, held.at[cut], sems.at[k * LOADS + n]))
            copies[-1].start()
    for copy in copies:
        copy.wait()


def load_columns(arrays, start, width, *earlier):
    rows = arrays[0].shape[0]
    parts = [jax.ShapeDtypeStruct((rows, width), a.dtype) for a in arrays]
    return pl.pallas_call(
        functools.partial(load_kernel, start, len(arrays)),
        in_specs=[pl.BlockSpec(memory_space=pl.ANY)] * (len(arrays) + len(earlier)),
        out_specs=[pl.BlockSpec(memory_space=pltpu.VMEM)] * len(arrays),
        out_shape=[pltpu.VMEM(p.shape, p.dtype) for p in parts],
        scratch_shapes=[pltpu.SemaphoreType.DMA((LOADS * len(arrays),))],
        compiler_params=PARAMS,
        cost_estimate=cost(0, *parts),
        name="load_columns",
    )(*[pltpu.with_memory_space_constraint(a, pltpu.HBM) for a in arrays], *earlier)


def up_kernel(rows_ref, weight_ref, tangent_ref, own_ref, other_ref):
    half = own_ref.shape[1]
    for start in range(0, own_ref.shape[2], TILE):
        cut = slice(start, start + TILE)
        for k, ref in enumerate((weight_ref, tangent_ref)):
            part = jnp.dot(rows_ref[...], ref[:, cut], preferred_element_type=F32)
            own_ref[k, :, cut] = part[:half]
            other_ref[k, :, cut] = part[half:].astype(BF16)


def up_parts(normed, weight, tangent):
    rows, width = normed.shape
    half, chunk = rows // 2, weight.shape[1]
    out_shape = (
        jax.ShapeDtypeStruct((2, half, chunk), F32),
        jax.ShapeDtypeStruct((2, half, chunk), BF16),
    )
    held = [pltpu.with_memory_space_constraint(a, pltpu.VMEM) for a in (weight, tangent)]
    return pl.pallas_call(
        up_kernel,
        out_shape=out_shape,
        compiler_params=PARAMS,
        cost_estimate=cost(4 * rows * width * chunk, normed),
        name="up_parts",
    )(normed, *held)


def back_kernel(rows_ref, weight_ref, *refs):
    own_ref, other_ref = refs[-2:]
    half = own_ref.shape[0]
    part = lax.dot_general(
        rows_ref[...], weight_ref[...], (((1,), (1,)), ((), ())), preferred_element_type=F32
    )
    own_ref[...] = part[:half]
    other_ref[...] = part[half:].astype(BF16)


def back_parts(cotangent, weight, start, chunk, *earlier):
    rows, width = cotangent.shape
    half = rows // 2
    first = start // TILE
    out_spec = pl.BlockSpec((half, TILE), lambda i: (0, i))
    out_shape = (
        jax.ShapeDtypeStruct((half, chunk), F32),
        jax.ShapeDtypeStruct((half, chunk), BF16),
    )
    moved = jax.ShapeDtypeStruct((width, chunk), BF16)
    return pl.pallas_call(
        back_kernel,
        grid=(chunk // TILE,),
        in_specs=[whole(cotangent), pl.BlockSpec((TILE, width), lambda i: (first + i, 0))]
        + [pl.BlockSpec(memory_space=pl.ANY)] * len(earlier),
        out_specs=(out_spec, out_spec),
        out_shape=out_shape,
        compiler_params=PARAMS,
        cost_estimate=cost(2 * rows * width * chunk, cotangent, moved),
        name="back_parts",
    )(cotangent, weight, *earlier)


def outer(left, right):
    return lax.dot_general(left, right, (((0,), (0,)), ((), ())), preferred_element_type=F32)


def columns_kernel(column, left_ref, right_ref, *refs):
    out_ref, held, sems = refs[-3:]
    width = right_ref.shape[1]
    copies = []
    for k in range(held.shape[0]):
        held[k] = outer(left_ref[:, k * TILE : (k + 1) * TILE], right_ref[...])
        place = out_ref.at[pl.ds(k * TILE, TILE), pl.ds(column, width)]
        copies.append(pltpu.make_async_copy(held.at[k], place, sems.at[k]))
        copies[-1].start()
    for copy in copies:
        copy.wait()


def outer_columns(left, right, shape, column, so_far):
    tiles = left.shape[1] // TILE
    moved = jax.ShapeDtypeStruct((left.shape[1], right.shape[1]), F32)
    vmem, anywhere = pl.BlockSpec(memory_space=pltpu.VMEM), pl.BlockSpec(memory_space=pl.ANY)
    more = [] if so_far is None else [so_far]
    return pl.pallas_call(
        functools.partial(columns_kernel, column),
        in_specs=[vmem, vmem] + [anywhere] * len(more),
        out_specs=anywhere,
        out_shape=jax.ShapeDtypeStruct(shape, F32),
        scratch_shapes=[
            pltpu.VMEM((tiles, TILE, right.shape[1]), F32),
            pltpu.SemaphoreType.DMA((tiles,)),
        ],
        input_output_aliases={2: 0} if more else {},
        compiler_params=PARAMS,
        cost_estimate=cost(2 * left.size * right.shape[1], left, right, moved),
        name="outer_columns",
    )(left, right, *more)


def rows_kernel(count, *refs):
    left_refs, right_ref = refs[:count], refs[count]
    out_ref, held, sems = refs[-3:]
    slots = held.shape[0]
    copies = []
    for left_ref in left_refs:
        for start in range(0, left_ref.shape[1], TILE):
            k = len(copies)
            slot = k % slots
            if k >= slots:
                copies[k - slots].wait()
            held[slot] = outer(left_ref[:, start : start + TILE], right_ref[...])
            place = out_ref.at[pl.ds(k * TILE, TILE)]
            copies.append(pltpu.make_async_copy(held.at[slot], place, sems.at[slot]))
            copies[k].start()
    for copy in copies[-slots:]:
        copy.wait()


def outer_rows(lefts, right, shape, *earlier):
    slots = min(SLOTS, shape[0] // TILE)
    vmem = pl.BlockSpec(memory_space=pltpu.VMEM)
    moved = jax.ShapeDtypeStruct(shape, F32)
    return pl.pallas_call(
        functools.partial(rows_kernel, len(lefts)),
        in_specs=[vmem] * (len(lefts) + 1) + [pl.BlockSpec(memory_space=pl.ANY)] * len(earlier),
        out_specs=pl.BlockSpec(memory_space=pl.ANY),
        out_shape=moved,
        scratch_shapes=[
            pltpu.VMEM((slots, TILE, shape[1]), F32),
            pltpu.SemaphoreType.DMA((slots,)),
        ],
        compiler_params=PARAMS,
        cost_estimate=cost(2 * right.size * shape[0], right, moved),
        name="outer_rows",
    )(*lefts, right, *earlier)


def row_sum(values):
    return jnp.sum(values, axis=1, keepdims=True)


def put_columns(ref, values):
    lane = lax.broadcasted_iota(jnp.int32, ref.shape, 1)
    total = jnp.zeros(ref.shape, F32)
    for k, value in enumerate(values):
        total = jnp.where(lane == k, value, total)
    ref[...] = total


def get_columns(refs, count):
    found = []
    for flip, ref in enumerate(refs):
        values = ref[...]
        if flip & 1:
            values = swap_rows(values)
        found.append([values[:, k : k + 1] for k in range(count)])
    return found


def swap_if(flag, values):
    return jnp.where(flag == 1, swap_rows(values), values)


def stats_in_kernel(odd_ref, given_ref, tokens_ref, stats_ref):
    tokens_ref[...] = swap_if(odd_ref[0], given_ref[...])
    source = tokens_ref[...].astype(F32)
    mean = row_sum(source) / source.shape[1]
    put_columns(stats_ref, [mean, row_sum(jnp.square(source - mean))])


def norm_in_kernel(tokens_ref, gain_ref, shift_ref, *refs):
    source = tokens_ref[...].astype(F32)
    width = source.shape[1]
    stats = get_columns(refs[:-1], 2)
    center = sum(s[0] for s in stats) / len(stats)
    spread = sum(s[1] + width * jnp.square(s[0] - center) for s in stats) / D
    inverse = lax.rsqrt(spread + epsilon)
    refs[-1][...] = ((source - center) * inverse * gain_ref[...] + shift_ref[...]).astype(BF16)


def stats_out_kernel(tokens_ref, gain_ref, curvature_ref, *refs):
    *terms, output_ref, tangent_ref, stats_ref = refs
    rows, width = output_ref.shape
    total = sum(term[...].astype(F32) for term in terms)
    output = tokens_ref[...].astype(F32) + total[:rows]
    tangent = total[rows:]
    output_ref[...] = output
    tangent_ref[...] = tangent
    factor = gain_ref[...] * gain_ref[...] * curvature_ref[...]
    output_mean, tangent_mean = row_sum(output) / width, row_sum(tangent) / width
    output_off, tangent_off = output - output_mean, tangent - tangent_mean
    factor_output = factor * output_off
    put_columns(
        stats_ref,
        [
            output_mean,
            tangent_mean,
            row_sum(output_off * output_off),
            row_sum(output_off * tangent_off),
            row_sum(factor),
            row_sum(factor_output),
            row_sum(factor * tangent_off),
            row_sum(factor_output * output_off),
            row_sum(factor_output * tangent_off),
        ],
    )


def cotangent_kernel(output_ref, tangent_ref, gain_ref, curvature_ref, *refs):
    output, tangent = output_ref[...], tangent_ref[...]
    width = output.shape[1]
    stats = get_columns(refs[:-1], 9)
    center = sum(s[0] for s in stats) / len(stats)
    center_tangent = sum(s[1] for s in stats) / len(stats)
    square = cross = f_output = f_tangent = f_square = f_cross = 0.0
    for mean_o, mean_t, oo, ot, f, fo, ft, foo, fot in stats:
        a, b = mean_o - center, mean_t - center_tangent
        square += oo + width * a * a
        cross += ot + width * a * b
        f_output += fo + a * f
        f_tangent += ft + b * f
        f_square += foo + a * (2.0 * fo + a * f)
        f_cross += fot + a * ft + b * (fo + a * f)
    inverse = lax.rsqrt(square / D + epsilon)
    tangent_dot = cross * inverse / D
    weight_mean = (f_tangent - tangent_dot * inverse * f_output) * inverse / D
    weight_dot = (f_cross - tangent_dot * inverse * f_square) * inverse * inverse / D
    normal = (output - center) * inverse
    factor = gain_ref[...] * gain_ref[...] * curvature_ref[...]
    weighted = factor * ((tangent - center_tangent - normal * tangent_dot) * inverse)
    refs[-1][...] = ((weighted - weight_mean - normal * weight_dot) * inverse).astype(BF16)


def in_vmem(kernel, out_shape, *operands):
    return pl.pallas_call(
        kernel,
        out_shape=out_shape,
        compiler_params=PARAMS,
        cost_estimate=cost(0, *operands),
        name=kernel.__name__,
    )(*operands)


def peers(value):
    return [value] + [swap_tensor(value, flip) for flip in range(1, lax.axis_size("tensor"))]


def over_tensor(total, *earlier):
    flip = 2
    while flip < lax.axis_size("tensor"):
        received = swap_tensor(total.astype(BF16), flip)
        if earlier:
            received = after(received, *earlier)
        total = total + received.astype(F32)
        flip *= 2
    return total


def chunks_of(units):
    part = units // 6
    sizes = [part, 2 * part, 2 * part, part] if part % TILE == 0 else [units]
    return [sum(sizes[:k]) for k in range(len(sizes))], sizes


def on_device(
    tokens,
    gain_in,
    shift_in,
    up_weight,
    up_bias,
    down_weight,
    gain_out,
    curvature,
    up_tangent,
    down_tangent,
):
    rows, width = tokens.shape
    hidden_units = up_weight.shape[1]
    starts, sizes = chunks_of(hidden_units)
    odd = lax.axis_index("tensor") & 1
    curvature = swap_if(odd, curvature)
    gain_in, shift_in, gain_out = gain_in[None], shift_in[None], gain_out[None]
    stats_shape = jax.ShapeDtypeStruct((rows, LANES), F32)
    rows_bf16 = jax.ShapeDtypeStruct((rows, width), BF16)
    rows_f32 = jax.ShapeDtypeStruct((rows, width), F32)

    tokens, stats = pl.pallas_call(
        stats_in_kernel,
        in_specs=[
            pl.BlockSpec(memory_space=pltpu.SMEM),
            pl.BlockSpec(memory_space=pltpu.VMEM),
        ],
        out_shape=(rows_bf16, stats_shape),
        compiler_params=PARAMS,
        cost_estimate=cost(0, tokens),
        name="stats_in_kernel",
    )(odd.astype(jnp.int32)[None], tokens)
    stats = peers(stats)
    normed = in_vmem(norm_in_kernel, rows_bf16, tokens, gain_in, shift_in, *stats)
    all_normed, weights = gather_rows(
        normed,
        lambda early: load_columns((after(up_weight, early), up_tangent), starts[0], sizes[0]),
    )

    totals, owns, own = [], [], None
    for j, (start, chunk) in enumerate(zip(starts, sizes)):
        if j:
            weights = load_columns((after(up_weight, own), up_tangent), start, chunk, totals[-1])
        lhs = after(all_normed, totals[-1], *weights) if j else all_normed
        own, other = up_parts(lhs, *weights)
        totals.append(own + swap_tensor(other, 1).astype(F32))
        owns.append(own)

    slopes, hiddens, done = [], [], [()]
    primal = tangent = None
    for j, (start, chunk) in enumerate(zip(starts, sizes)):
        total = over_tensor(totals[j], *([both if j == len(starts) - 1 else mine, *done[j - 1]] if j else owns[1:2]))
        if j:
            total = after(total, totals[min(j + 2, len(totals) - 1)])
        pre = total[0] + up_bias[start : start + chunk]
        cumulative = 0.5 * (1.0 + lax.erf(pre * root_half))
        slope = cumulative + pre * jnp.exp(-0.5 * pre * pre) * inv_root_two_pi
        slopes.append(slope.astype(BF16))
        mine = jnp.stack([(pre * cumulative).astype(BF16), (slope * total[1]).astype(BF16)])
        both = jnp.concatenate([mine, swap_tensor(mine, 1)], axis=1)
        hidden, hidden_tangent = both[0], both[1]
        hiddens.append(hidden)
        weight = down_weight[start : start + chunk]
        primal_part = jnp.dot(hidden, weight, preferred_element_type=F32)
        tangent_part = jnp.dot(hidden_tangent, weight, preferred_element_type=F32) + jnp.dot(
            hidden, down_tangent[start : start + chunk], preferred_element_type=F32
        )
        primal = primal_part if primal is None else primal + primal_part
        tangent = tangent_part if tangent is None else tangent + tangent_part
        done.append((primal, tangent))

    terms = scatter_rows([primal, tangent], rows)
    output, output_tangent, stats = in_vmem(
        stats_out_kernel,
        (rows_f32, rows_f32, stats_shape),
        tokens,
        gain_out,
        curvature,
        *terms,
    )
    cotangent = in_vmem(
        cotangent_kernel,
        rows_bf16,
        output,
        output_tangent,
        gain_out,
        curvature,
        *peers(stats),
    )
    all_cotangent, _ = gather_rows(cotangent)

    merged = 2 if len(starts) > 2 else 1
    slopes = [jnp.concatenate(slopes[:merged], axis=1)] + slopes[merged:]
    sizes = [sum(sizes[:merged])] + sizes[merged:]
    starts = [0] + starts[merged:]
    totals, lhs = [], all_cotangent
    for start, chunk in zip(starts, sizes):
        own, other = back_parts(lhs, down_weight, start, chunk, *totals[:-1])
        totals.append(own + swap_tensor(other, 1).astype(F32))
        lhs = after(all_cotangent, own)
    down_product = outer_rows(hiddens, all_cotangent, down_weight.shape, *totals)

    made = [down_product]
    for j, (start, chunk) in enumerate(zip(starts, sizes)):
        total = over_tensor(totals[j], made[max(0, j - 1)])
        grad = (total * slopes[j].astype(F32)).astype(BF16)
        grad = jnp.concatenate([grad, swap_tensor(grad, 1)], axis=0)
        so_far = made[-1] if j else None
        made.append(outer_columns(all_normed, grad, up_weight.shape, start, so_far))
    up_product = made[-1]
    return (up_product, down_product)


def solution(mesh):
    return jax.shard_map(
        on_device,
        mesh=mesh,
        in_specs=(
            P("dp", "tensor"),
            P("tensor"),
            P("tensor"),
            P("tensor", "dp"),
            P("dp"),
            P("dp", "tensor"),
            P("tensor"),
            P("dp", "tensor"),
            P("tensor", "dp"),
            P("dp", "tensor"),
        ),
        out_specs=(P("tensor", "dp"), P("dp", "tensor")),
        check_vma=False,
    )
```

time: 412 us -> 161 us (0.39)
  waiting for transfers between devices: 241 us -> 61.2 us
  blocking collectives: 91.6 us -> 0 us
  starting transfers between devices: 0.16 us -> 41.1 us
  matrix products: 49.9 us -> 9.46 us
  Pallas kernels: 0 us -> 37.9 us
  between operations: 13.9 us -> 1.84 us
  other arithmetic: 12.5 us -> 3.77 us
    psum x1 -> x0, waiting for transfers between devices: 120 us -> none  [on_device(): pre_total, tangent_total = lax.psum((pre_part, tangent_part), 'tensor')]
    reduce_scatter x2 -> x0, waiting for transfers between devices: 109 us -> none  [the longest x1 74 us: on_device(): lax.psum_scatter(jnp.concatenate([primal, tangent], axis=1), 'dp', scatte...]
    all_gather x2 -> x0, blocking collectives: 65 us -> none  [the longest x1 32.7 us: on_device(): all_normed = lax.all_gather(normed, 'dp', axis=0, tiled=True)]
    ppermute x0 -> x48, waiting for transfers between devices: none -> 61.2 us  [the longest x21 34.8 us: swap_dp(): return lax.ppermute(value, 'dp', [(i, i ^ flip) for i in range(size)])]
    ppermute x0 -> x48, starting transfers between devices: none -> 41.1 us  [the longest x21 25.5 us: swap_dp(): return lax.ppermute(value, 'dp', [(i, i ^ flip) for i in range(size)])]
    dot_general x8 -> x12, matrix products: 49.9 us -> 9.46 us  [the longest x4 3.24 us: on_device(): jnp.dot(hidden, down_tangent[start:start + chunk], preferred_element_type...]
    pallas_call x0 -> x19, Pallas kernels: none -> 37.9 us  [the longest x4 9.79 us: load_columns(): pl.pallas_call(functools.partial(load_kernel, start, len(arrays)), in_spe...]
    psum x4 -> x0, blocking collectives: 26.6 us -> none  [the longest x1 8.37 us: on_device(): lax.psum((row_total(source), row_total(source * source)), 'tensor')]
  transfers between devices with their start and end apart: 4 -> 48, of which waited for: 4 -> 22; matrix products, arithmetic and copies ran while one was open for 2% -> 8% of each run, Pallas kernels for 0% -> 19%
where the time goes in v1:
time: 161 us; the launch traced here: 160 us
  waiting for transfers between devices  61.2 us (38%)
  starting transfers between devices  41.1 us (26%)
  Pallas kernels  37.9 us (24%)
  matrix products  9.46 us (6%)
  local copies, waits for them, and re-layouts  5.17 us (3%)
  other arithmetic  3.77 us (2%)
  between operations  1.84 us (1%)
    ppermute x21, waiting for transfers between devices, swap_dp(): return lax.ppermute(value, 'dp', [(i, i ^ flip) for i in range(size)])  34.8 us
    ppermute x27, waiting for transfers between devices, swap_tensor(): return lax.ppermute(value, 'tensor', [(t, t ^ flip) for t in range(size)])  26.4 us
    ppermute x21, starting transfers between devices, swap_dp(): return lax.ppermute(value, 'dp', [(i, i ^ flip) for i in range(size)])  25.5 us
    ppermute x27, starting transfers between devices, swap_tensor(): return lax.ppermute(value, 'tensor', [(t, t ^ flip) for t in range(size)])  15.5 us
    pallas_call x4, Pallas kernels, load_columns(): pl.pallas_call(functools.partial(load_kernel, start, len(arrays)), in_spe...  9.79 us
    pallas_call x3, Pallas kernels, outer_columns(): pl.pallas_call(functools.partial(columns_kernel, column), in_specs=[vmem,...  9.11 us
    pallas_call x1, Pallas kernels, outer_rows(): pl.pallas_call(functools.partial(rows_kernel, len(lefts)), in_specs=[vmem...  6.92 us
    pallas_call x4, Pallas kernels, up_parts(): pl.pallas_call(up_kernel, out_shape=out_shape, compiler_params=PARAMS, co...  5.53 us
  transfers between devices with their start and end apart: 48, of which 22 were waited for; matrix products, arithmetic and copies ran while one was open for 8% of the time, Pallas kernels for 19%

profile of v1, /device:TPU:0, one launch (start us, length us, event | category | flops | bytes accessed | tf_op | source)
XLA Modules:
  0.0 160.4 jit_solution(16823096102351018326)
XLA Ops:
  1.7 2.4 %collective-permute-start.2 = (f32[32,128]{1,0:T(8,128)S(1)}, f32[32,128]{1,0:T(8,128)S(1)}, u32[]{:S(2)}, u32[]{:S(2)}) collective-permute-start(f32[32,128]{1,0:T(8,128)S(1)} %get-tuple-element.55.refs_0_), channel_id=1, source_target_pairs={{0,3},{1,2},{2,1},{3,0},{4,7},{5,6},{6,5},{7,4},{8,11},{9,10},{10,... | collective-permute-start | bytes 49160 | tf_op jit(solution)/shard_map/ppermute | solution.py:28
  8.1 2.7 %collective-permute-start.6 = (bf16[32,1536]{1,0:T(8,128)(2,1)S(1)}, bf16[32,1536]{1,0:T(8,128)(2,1)S(1)}, u32[]{:S(2)}, u32[]{:S(2)}) collective-permute-start(bf16[32,1536]{1,0:T(8,128)(2,1)S(1)} %norm_in_kernel.1), channel_id=1, source_target_pairs={{0,16},{4,20},{8,24},{12,28},{16,0},{20,4},{24,8},{28,12},{1,17},{... | collective-permute-start | bytes 294920 | tf_op jit(solution)/shard_map/ppermute | solution.py:33
  10.7 1.6 collective-permute-start.4
  12.3 1.5 collective-permute-start.3
  13.8 1.8 %collective-permute-done.6 = bf16[32,1536]{1,0:T(8,128)(2,1)S(1)} collective-permute-done((bf16[32,1536]{1,0:T(8,128)(2,1)S(1)}, bf16[32,1536]{1,0:T(8,128)(2,1)S(1)}, u32[]{:S(2)}, u32[]{:S(2)}) %collective-permute-start.6) | collective-permute-done | bytes 98336 | tf_op jit(solution)/shard_map/ppermute | solution.py:33
  16.3 1.5 collective-permute-start.7
  18.4 1.9 %collective-permute-done.8 = bf16[32,1536]{1,0:T(8,128)(2,1)S(1)} collective-permute-done((bf16[32,1536]{1,0:T(8,128)(2,1)S(1)}, bf16[32,1536]{1,0:T(8,128)(2,1)S(1)}, u32[]{:S(2)}, u32[]{:S(2)}) %collective-permute-start.8) | collective-permute-done | bytes 98336 | tf_op jit(solution)/shard_map/ppermute | solution.py:33
  20.3 1.5 collective-permute-start.9
  21.7 2.3 %collective-permute-done.5 = bf16[32,1536]{1,0:T(8,128)(2,1)S(1)} collective-permute-done((bf16[32,1536]{1,0:T(8,128)(2,1)S(1)}, bf16[32,1536]{1,0:T(8,128)(2,1)S(1)}, u32[]{:S(2)}, u32[]{:S(2)}) %collective-permute-start.5) | collective-permute-done | bytes 98336 | tf_op jit(solution)/shard_map/ppermute | solution.py:33
  24.1 1.9 %load_columns.4 = (bf16[1536,512]{1,0:T(8,128)(2,1)S(1)}, bf16[1536,512]{1,0:T(8,128)(2,1)S(1)}) custom-call(bf16[1536,3072]{1,0:T(8,128)(2,1)} %refs_0_.3, bf16[1536,3072]{1,0:T(8,128)(2,1)} %refs_1_.7), custom_call_target="tpu_custom_call" | custom-call | bytes 3145 | tf_op jit(solution)/shard_map/load_columns/pallas_call | solution.py:124
  27.3 1.5 collective-permute-done.10
  28.9 1.5 collective-permute-start.11
  30.4 2.9 %load_columns.5 = (bf16[1536,1024]{1,0:T(8,128)(2,1)S(1)}, bf16[1536,1024]{1,0:T(8,128)(2,1)S(1)}) custom-call(bf16[1536,3072]{1,0:T(8,128)(2,1)} %refs_0_.3, bf16[1536,3072]{1,0:T(8,128)(2,1)} %refs_1_.7, f32[2,128,512]{2,1,0:T(8,128)S(1)} %get-tuple-element.119.refs_2_), custom_call_target="tpu_custom_call" | custom-call | bytes 6291 | tf_op jit(solution)/shard_map/load_columns/pallas_call | solution.py:124
  33.3 1.8 %up_parts.5 = (f32[2,128,1024]{2,1,0:T(8,128)S(1)}, bf16[2,128,1024]{2,1,0:T(8,128)(2,1)S(1)}) custom-call(bf16[256,1536]{1,0:T(8,128)(2,1)S(1)} %constant_dynamic-update-slice_fusion.rows_ref.left_ref, bf16[1536,1024]{1,0:T(8,128)(2,1)S(1)} %get-tuple-element.63.weight_ref, bf16[1536,1024]{1,0:T(8,128)(2,1)S(1)} %get-tuple-element.64.tangent_ref), custom_call_target="tpu_custom_call" | custom-call | flops 1610612 | bytes 786 | tf_op jit(solution)/shard_map/up_parts/pallas_call | solution.py:154
  35.2 2.1 %collective-permute-done.11 = bf16[2,128,512]{2,1,0:T(8,128)(2,1)S(1)} collective-permute-done((bf16[2,128,512]{2,1,0:T(8,128)(2,1)S(1)}, bf16[2,128,512]{2,1,0:T(8,128)(2,1)S(1)}, u32[]{:S(2)}, u32[]{:S(2)}) %collective-permute-start.11) | collective-permute-done | bytes 262176 | tf_op jit(solution)/shard_map/ppermute | solution.py:28
  38.0 1.5 collective-permute-start.14
  39.5 3.0 %load_columns.6 = (bf16[1536,1024]{1,0:T(8,128)(2,1)S(1)}, bf16[1536,1024]{1,0:T(8,128)(2,1)S(1)}) custom-call(bf16[1536,3072]{1,0:T(8,128)(2,1)} %refs_0_.3, bf16[1536,3072]{1,0:T(8,128)(2,1)} %refs_1_.7, f32[2,128,1024]{2,1,0:T(8,128)S(1)} %get-tuple-element.117.refs_2_), custom_call_target="tpu_custom_call" | custom-call | bytes 6291 | tf_op jit(solution)/shard_map/load_columns/pallas_call | solution.py:124
  42.6 1.8 %up_parts.6 = (f32[2,128,1024]{2,1,0:T(8,128)S(1)}, bf16[2,128,1024]{2,1,0:T(8,128)(2,1)S(1)}) custom-call(bf16[256,1536]{1,0:T(8,128)(2,1)S(1)} %constant_dynamic-update-slice_fusion.rows_ref.left_ref, bf16[1536,1024]{1,0:T(8,128)(2,1)S(1)} %get-tuple-element.71.weight_ref, bf16[1536,1024]{1,0:T(8,128)(2,1)S(1)} %get-tuple-element.72.tangent_ref), custom_call_target="tpu_custom_call" | custom-call | flops 1610612 | bytes 786 | tf_op jit(solution)/shard_map/up_parts/pallas_call | solution.py:154
  47.9 4.5 %collective-permute-done.14 = bf16[2,128,1024]{2,1,0:T(8,128)(2,1)S(1)} collective-permute-done((bf16[2,128,1024]{2,1,0:T(8,128)(2,1)S(1)}, bf16[2,128,1024]{2,1,0:T(8,128)(2,1)S(1)}, u32[]{:S(2)}, u32[]{:S(2)}) %collective-permute-start.14) | collective-permute-done | bytes 524320 | tf_op jit(solution)/shard_map/ppermute | solution.py:28
  52.6 1.5 collective-permute-start.18
  54.1 1.9 %load_columns.7 = (bf16[1536,512]{1,0:T(8,128)(2,1)S(1)}, bf16[1536,512]{1,0:T(8,128)(2,1)S(1)}) custom-call(bf16[1536,3072]{1,0:T(8,128)(2,1)} %refs_0_.3, bf16[1536,3072]{1,0:T(8,128)(2,1)} %refs_1_.7, f32[2,128,1024]{2,1,0:T(8,128)S(1)} %get-tuple-element.115.refs_2_), custom_call_target="tpu_custom_call" | custom-call | bytes 3145 | tf_op jit(solution)/shard_map/load_columns/pallas_call | solution.py:124
  60.0 7.5 %collective-permute-done.18 = bf16[2,128,1024]{2,1,0:T(8,128)(2,1)S(1)} collective-permute-done((bf16[2,128,1024]{2,1,0:T(8,128)(2,1)S(1)}, bf16[2,128,1024]{2,1,0:T(8,128)(2,1)S(1)}, u32[]{:S(2)}, u32[]{:S(2)}) %collective-permute-start.18) | collective-permute-done | bytes 524320 | tf_op jit(solution)/shard_map/ppermute | solution.py:28
  77.3 1.4 collective-permute-start.22
  78.8 5.7 %collective-permute-done.22 = bf16[64,1536]{1,0:T(8,128)(2,1)S(1)} collective-permute-done((bf16[64,1536]{1,0:T(8,128)(2,1)S(1)}, bf16[64,1536]{1,0:T(8,128)(2,1)S(1)}, u32[]{:S(2)}, u32[]{:S(2)}) %collective-permute-start.22) | collective-permute-done | bytes 196640 | tf_op jit(solution)/shard_map/ppermute | solution.py:33
  84.5 1.3 collective-permute-start.23
  86.0 1.5 collective-permute-start.27
  87.5 4.8 %collective-permute-done.23 = bf16[64,1536]{1,0:T(8,128)(2,1)S(1)} collective-permute-done((bf16[64,1536]{1,0:T(8,128)(2,1)S(1)}, bf16[64,1536]{1,0:T(8,128)(2,1)S(1)}, u32[]{:S(2)}, u32[]{:S(2)}) %collective-permute-start.23) | collective-permute-done | bytes 196640 | tf_op jit(solution)/shard_map/ppermute | solution.py:33
  92.3 1.3 collective-permute-start.24
  93.7 3.4 %collective-permute-start.26 = (bf16[64,1536]{1,0:T(8,128)(2,1)S(1)}, bf16[64,1536]{1,0:T(8,128)(2,1)S(1)}, u32[]{:S(2)}, u32[]{:S(2)}) collective-permute-start(bf16[64,1536]{1,0:T(8,128)(2,1)S(1)} %fusion.51), channel_id=1, source_target_pairs={{0,16},{4,20},{8,24},{12,28},{16,0},{20,4},{24,8},{28,12},{1,17},{... | collective-permute-start | bytes 589832 | tf_op jit(solution)/shard_map/ppermute | solution.py:33
  97.5 1.8 %collective-permute-done.24.refs_1_ = bf16[64,1536]{1,0:T(8,128)(2,1)S(1)} collective-permute-done((bf16[64,1536]{1,0:T(8,128)(2,1)S(1)}, bf16[64,1536]{1,0:T(8,128)(2,1)S(1)}, u32[]{:S(2)}, u32[]{:S(2)}) %collective-permute-start.24) | collective-permute-done | bytes 196640 | tf_op jit(solution)/shard_map/ppermute | solution.py:33
  99.3 6.1 %collective-permute-done.28.refs_3_ = bf16[64,1536]{1,0:T(8,128)(2,1)S(1)} collective-permute-done((bf16[64,1536]{1,0:T(8,128)(2,1)S(1)}, bf16[64,1536]{1,0:T(8,128)(2,1)S(1)}, u32[]{:S(2)}, u32[]{:S(2)}) %collective-permute-start.28) | collective-permute-done | bytes 196640 | tf_op jit(solution)/shard_map/ppermute | solution.py:33
  105.8 1.5 collective-permute-start.30
  107.7 1.4 collective-permute-done.31.refs_3_
  110.8 1.6 %collective-permute-start.33 = (bf16[32,1536]{1,0:T(8,128)(2,1)S(1)}, bf16[32,1536]{1,0:T(8,128)(2,1)S(1)}, u32[]{:S(2)}, u32[]{:S(2)}) collective-permute-start(bf16[32,1536]{1,0:T(8,128)(2,1)S(1)} %cotangent_kernel.1), channel_id=1, source_target_pairs={{0,8},{4,12},{8,0},{12,4},{16,24},{20,28},{24,16},{28,20},{1,9},{5... | collective-permute-start | bytes 294920 | tf_op jit(solution)/shard_map/ppermute | solution.py:33
  112.4 1.3 collective-permute-start.32
  113.8 4.0 %collective-permute-done.35 = bf16[32,1536]{1,0:T(8,128)(2,1)S(1)} collective-permute-done((bf16[32,1536]{1,0:T(8,128)(2,1)S(1)}, bf16[32,1536]{1,0:T(8,128)(2,1)S(1)}, u32[]{:S(2)}, u32[]{:S(2)}) %collective-permute-start.35) | collective-permute-done | bytes 98336 | tf_op jit(solution)/shard_map/ppermute | solution.py:33
  119.8 2.7 %collective-permute-done.37 = bf16[32,1536]{1,0:T(8,128)(2,1)S(1)} collective-permute-done((bf16[32,1536]{1,0:T(8,128)(2,1)S(1)}, bf16[32,1536]{1,0:T(8,128)(2,1)S(1)}, u32[]{:S(2)}, u32[]{:S(2)}) %collective-permute-start.37) | collective-permute-done | bytes 98336 | tf_op jit(solution)/shard_map/ppermute | solution.py:33
  123.4 1.4 collective-permute-done.34
  124.9 2.2 %collective-permute-done.38 = bf16[32,1536]{1,0:T(8,128)(2,1)S(1)} collective-permute-done((bf16[32,1536]{1,0:T(8,128)(2,1)S(1)}, bf16[32,1536]{1,0:T(8,128)(2,1)S(1)}, u32[]{:S(2)}, u32[]{:S(2)}) %collective-permute-start.38) | collective-permute-done | bytes 98336 | tf_op jit(solution)/shard_map/ppermute | solution.py:33
  127.2 2.5 %back_parts.3 = (f32[128,1536]{1,0:T(8,128)S(1)}, bf16[128,1536]{1,0:T(8,128)(2,1)S(1)}) custom-call(bf16[256,1536]{1,0:T(8,128)(2,1)S(1)} %constant_dynamic-update-slice_fusion.16.rows_ref.refs_4_, bf16[3072,1536]{1,0:T(8,128)(2,1)S(1)} %bitcast.54), custom_call_target="tpu_custom_call" | custom-call | flops 1207959 | bytes 5505 | tf_op jit(solution)/shard_map/back_parts/pallas_call | solution.py:183
  129.9 1.7 %back_parts.4 = (f32[128,1024]{1,0:T(8,128)S(1)}, bf16[128,1024]{1,0:T(8,128)(2,1)S(1)}) custom-call(bf16[256,1536]{1,0:T(8,128)(2,1)S(1)} %constant_dynamic-update-slice_fusion.16.rows_ref.refs_4_, bf16[3072,1536]{1,0:T(8,128)(2,1)S(1)} %bitcast.54), custom_call_target="tpu_custom_call" | custom-call | flops 805306 | bytes 3932 | tf_op jit(solution)/shard_map/back_parts/pallas_call | solution.py:183
  133.9 1.6 collective-permute-start.46
  135.5 6.9 %outer_rows.1 = f32[3072,1536]{1,0:T(8,128)} custom-call(bf16[256,512]{1,0:T(8,128)(2,1)S(1)} %slice_bitcast_fusion.11.refs_0_, bf16[256,1024]{1,0:T(8,128)(2,1)S(1)} %slice_bitcast_fusion.5.refs_1_, bf16[256,1024]{1,0:T(8,128)(2,1)S(1)} %slice_bitcast_fusion.4.refs_2_, bf16[256,512]{1,0:T(8,128)(2,1)S(1)} %slice_bitcast_fusion.8.refs_3_, ...), custom_call_target="tpu_custom_call" | custom-call | flops 2415919 | bytes 19660 | tf_op jit(solution)/shard_map/outer_rows/pallas_call | solution.py:257
  142.4 1.9 %collective-permute-done.42 = bf16[128,1536]{1,0:T(8,128)(2,1)S(1)} collective-permute-done((bf16[128,1536]{1,0:T(8,128)(2,1)S(1)}, bf16[128,1536]{1,0:T(8,128)(2,1)S(1)}, u32[]{:S(2)}, u32[]{:S(2)}) %collective-permute-start.42) | collective-permute-done | bytes 393248 | tf_op jit(solution)/shard_map/ppermute | solution.py:28
  145.1 4.8 %collective-permute-done.46 = bf16[128,1024]{1,0:T(8,128)(2,1)S(1)} collective-permute-done((bf16[128,1024]{1,0:T(8,128)(2,1)S(1)}, bf16[128,1024]{1,0:T(8,128)(2,1)S(1)}, u32[]{:S(2)}, u32[]{:S(2)}) %collective-permute-start.46) | collective-permute-done | bytes 262176 | tf_op jit(solution)/shard_map/ppermute | solution.py:28
  150.4 4.1 %outer_columns.3.refs_0_ = f32[1536,3072]{1,0:T(8,128)} custom-call(bf16[256,1536]{1,0:T(8,128)(2,1)S(1)} %constant_dynamic-update-slice_fusion.rows_ref.left_ref, bf16[256,1536]{1,0:T(8,128)(2,1)S(1)} %pad_maximum_fusion.2.right_ref), custom_call_target="tpu_custom_call" | custom-call | flops 1207959 | bytes 11010 | tf_op jit(solution)/shard_map/outer_columns/pallas_call | solution.py:218
  155.2 3.0 %outer_columns.4.refs_0_ = f32[1536,3072]{1,0:T(8,128)} custom-call(bf16[256,1536]{1,0:T(8,128)(2,1)S(1)} %constant_dynamic-update-slice_fusion.rows_ref.left_ref, bf16[256,1024]{1,0:T(8,128)(2,1)S(1)} %pad_maximum_fusion.7.right_ref, f32[1536,3072]{1,0:T(8,128)} %outer_columns.3.refs_0_), custom_call_target="tpu_custom_call", output_to_operand_aliasing={{}: (2, {})} | custom-call | flops 805306 | bytes 7602 | tf_op jit(solution)/shard_map/outer_columns/pallas_call | solution.py:218
  158.3 2.0 %outer_columns.5 = f32[1536,3072]{1,0:T(8,128)} custom-call(bf16[256,1536]{1,0:T(8,128)(2,1)S(1)} %constant_dynamic-update-slice_fusion.rows_ref.left_ref, bf16[256,512]{1,0:T(8,128)(2,1)S(1)} %pad_maximum_fusion.11.right_ref, f32[1536,3072]{1,0:T(8,128)} %outer_columns.4.refs_0_), custom_call_target="tpu_custom_call", output_to_operand_aliasing={{}: (2, {})} | custom-call | flops 402653 | bytes 4194 | tf_op jit(solution)/shard_map/outer_columns/pallas_call | solution.py:218
  (185 shorter events, 35.8 us)
Async XLA Ops:
  1.7 5.5 %collective-permute-start.2 = (f32[32,128]{1,0:T(8,128)S(1)}, f32[32,128]{1,0:T(8,128)S(1)}, u32[]{:S(2)}, u32[]{:S(2)}) collective-permute-start(f32[32,128]{1,0:T(8,128)S(1)} %get-tuple-element.55.refs_0_), channel_id=1, source_target_pairs={{0,3},{1,2},{2,1},{3,0},{4,7},{5,6},{6,5},{7,4},{8,11},{9,10},{10,... | collective-permute-start | bytes 49160 | tf_op jit(solution)/shard_map/ppermute | solution.py:28
  4.1 3.7 %collective-permute-start.1 = (f32[32,128]{1,0:T(8,128)S(1)}, f32[32,128]{1,0:T(8,128)S(1)}, u32[]{:S(2)}, u32[]{:S(2)}) collective-permute-start(f32[32,128]{1,0:T(8,128)S(1)} %get-tuple-element.55.refs_0_), channel_id=1, source_target_pairs={{0,2},{1,3},{2,0},{3,1},{4,6},{5,7},{6,4},{7,5},{8,10},{9,11},{10,... | collective-permute-start | bytes 49160 | tf_op jit(solution)/shard_map/ppermute | solution.py:28
  4.8 3.1 %collective-permute-start = (f32[32,128]{1,0:T(8,128)S(1)}, f32[32,128]{1,0:T(8,128)S(1)}, u32[]{:S(2)}, u32[]{:S(2)}) collective-permute-start(f32[32,128]{1,0:T(8,128)S(1)} %get-tuple-element.55.refs_0_), channel_id=1, source_target_pairs={{0,1},{1,0},{2,3},{3,2},{4,5},{5,4},{6,7},{7,6},{8,9},{9,8},{10,11... | collective-permute-start | bytes 49160 | tf_op jit(solution)/shard_map/ppermute | solution.py:28
  8.1 7.6 %collective-permute-start.6 = (bf16[32,1536]{1,0:T(8,128)(2,1)S(1)}, bf16[32,1536]{1,0:T(8,128)(2,1)S(1)}, u32[]{:S(2)}, u32[]{:S(2)}) collective-permute-start(bf16[32,1536]{1,0:T(8,128)(2,1)S(1)} %norm_in_kernel.1), channel_id=1, source_target_pairs={{0,16},{4,20},{8,24},{12,28},{16,0},{20,4},{24,8},{28,12},{1,17},{... | collective-permute-start | bytes 294920 | tf_op jit(solution)/shard_map/ppermute | solution.py:33
  10.7 7.1 %collective-permute-start.4 = (bf16[32,1536]{1,0:T(8,128)(2,1)S(1)}, bf16[32,1536]{1,0:T(8,128)(2,1)S(1)}, u32[]{:S(2)}, u32[]{:S(2)}) collective-permute-start(bf16[32,1536]{1,0:T(8,128)(2,1)S(1)} %norm_in_kernel.1), channel_id=1, source_target_pairs={{0,8},{4,12},{8,0},{12,4},{16,24},{20,28},{24,16},{28,20},{1,9},{5... | collective-permute-start | bytes 294920 | tf_op jit(solution)/shard_map/ppermute | solution.py:33
  12.3 6.0 %collective-permute-start.3 = (bf16[32,1536]{1,0:T(8,128)(2,1)S(1)}, bf16[32,1536]{1,0:T(8,128)(2,1)S(1)}, u32[]{:S(2)}, u32[]{:S(2)}) collective-permute-start(bf16[32,1536]{1,0:T(8,128)(2,1)S(1)} %norm_in_kernel.1), channel_id=1, source_target_pairs={{0,4},{4,0},{8,12},{12,8},{16,20},{20,16},{24,28},{28,24},{1,5},{5... | collective-permute-start | bytes 294920 | tf_op jit(solution)/shard_map/ppermute | solution.py:33
  15.6 4.6 %collective-permute-start.8 = (bf16[32,1536]{1,0:T(8,128)(2,1)S(1)}, bf16[32,1536]{1,0:T(8,128)(2,1)S(1)}, u32[]{:S(2)}, u32[]{:S(2)}) collective-permute-start(bf16[32,1536]{1,0:T(8,128)(2,1)S(1)} %collective-permute-done.6), channel_id=1, source_target_pairs={{0,8},{4,12},{8,0},{12,4},{16,24},{20,28},{24,16},{28,20},{1,9},{5... | collective-permute-start | bytes 294920 | tf_op jit(solution)/shard_map/ppermute | solution.py:33
  16.3 7.7 %collective-permute-start.7 = (bf16[32,1536]{1,0:T(8,128)(2,1)S(1)}, bf16[32,1536]{1,0:T(8,128)(2,1)S(1)}, u32[]{:S(2)}, u32[]{:S(2)}) collective-permute-start(bf16[32,1536]{1,0:T(8,128)(2,1)S(1)} %collective-permute-done.6), channel_id=1, source_target_pairs={{0,4},{4,0},{8,12},{12,8},{16,20},{20,16},{24,28},{28,24},{1,5},{5... | collective-permute-start | bytes 294920 | tf_op jit(solution)/shard_map/ppermute | solution.py:33
  17.8 6.2 %collective-permute-start.5 = (bf16[32,1536]{1,0:T(8,128)(2,1)S(1)}, bf16[32,1536]{1,0:T(8,128)(2,1)S(1)}, u32[]{:S(2)}, u32[]{:S(2)}) collective-permute-start(bf16[32,1536]{1,0:T(8,128)(2,1)S(1)} %collective-permute-done.4), channel_id=1, source_target_pairs={{0,4},{4,0},{8,12},{12,8},{16,20},{20,16},{24,28},{28,24},{1,5},{5... | collective-permute-start | bytes 294920 | tf_op jit(solution)/shard_map/ppermute | solution.py:33
  20.3 5.8 %collective-permute-start.9 = (bf16[32,1536]{1,0:T(8,128)(2,1)S(1)}, bf16[32,1536]{1,0:T(8,128)(2,1)S(1)}, u32[]{:S(2)}, u32[]{:S(2)}) collective-permute-start(bf16[32,1536]{1,0:T(8,128)(2,1)S(1)} %collective-permute-done.8), channel_id=1, source_target_pairs={{0,4},{4,0},{8,12},{12,8},{16,20},{20,16},{24,28},{28,24},{1,5},{5... | collective-permute-start | bytes 294920 | tf_op jit(solution)/shard_map/ppermute | solution.py:33
  27.2 1.6 collective-permute-start.10
  28.9 8.4 %collective-permute-start.11 = (bf16[2,128,512]{2,1,0:T(8,128)(2,1)S(1)}, bf16[2,128,512]{2,1,0:T(8,128)(2,1)S(1)}, u32[]{:S(2)}, u32[]{:S(2)}) collective-permute-start(bf16[2,128,512]{2,1,0:T(8,128)(2,1)S(1)} %get-tuple-element.118), channel_id=1, source_target_pairs={{0,2},{1,3},{2,0},{3,1},{4,6},{5,7},{6,4},{7,5},{8,10},{9,11},{10,... | collective-permute-start | bytes 786440 | tf_op jit(solution)/shard_map/ppermute | solution.py:28
  35.1 2.7 %collective-permute-start.13 = (bf16[2,128,1024]{2,1,0:T(8,128)(2,1)S(1)}, bf16[2,128,1024]{2,1,0:T(8,128)(2,1)S(1)}, u32[]{:S(2)}, u32[]{:S(2)}) collective-permute-start(bf16[2,128,1024]{2,1,0:T(8,128)(2,1)S(1)} %get-tuple-element.68), channel_id=1, source_target_pairs={{0,1},{1,0},{2,3},{3,2},{4,5},{5,4},{6,7},{7,6},{8,9},{9,8},{10,11... | collective-permute-start | bytes 1572872 | tf_op jit(solution)/shard_map/ppermute | solution.py:28
  37.6 7.1 %collective-permute-start.12 = (bf16[2,128,512]{2,1,0:T(8,128)(2,1)S(1)}, bf16[2,128,512]{2,1,0:T(8,128)(2,1)S(1)}, u32[]{:S(2)}, u32[]{:S(2)}) collective-permute-start(bf16[2,128,512]{2,1,0:T(8,128)(2,1)S(1)} %pad_maximum_fusion.9), channel_id=1, source_target_pairs={{0,1},{1,0},{2,3},{3,2},{4,5},{5,4},{6,7},{7,6},{8,9},{9,8},{10,11... | collective-permute-start | bytes 786440 | tf_op jit(solution)/shard_map/ppermute | solution.py:28
  38.0 14.4 %collective-permute-start.14 = (bf16[2,128,1024]{2,1,0:T(8,128)(2,1)S(1)}, bf16[2,128,1024]{2,1,0:T(8,128)(2,1)S(1)}, u32[]{:S(2)}, u32[]{:S(2)}) collective-permute-start(bf16[2,128,1024]{2,1,0:T(8,128)(2,1)S(1)} %get-tuple-element.116), channel_id=1, source_target_pairs={{0,2},{1,3},{2,0},{3,1},{4,6},{5,7},{6,4},{7,5},{8,10},{9,11},{10,... | collective-permute-start | bytes 1572872 | tf_op jit(solution)/shard_map/ppermute | solution.py:28
  44.4 8.0 %collective-permute-start.15 = (bf16[2,128,1024]{2,1,0:T(8,128)(2,1)S(1)}, bf16[2,128,1024]{2,1,0:T(8,128)(2,1)S(1)}, u32[]{:S(2)}, u32[]{:S(2)}) collective-permute-start(bf16[2,128,1024]{2,1,0:T(8,128)(2,1)S(1)} %get-tuple-element.75), channel_id=1, source_target_pairs={{0,1},{1,0},{2,3},{3,2},{4,5},{5,4},{6,7},{7,6},{8,9},{9,8},{10,11... | collective-permute-start | bytes 1572872 | tf_op jit(solution)/shard_map/ppermute | solution.py:28
  52.6 14.9 %collective-permute-start.18 = (bf16[2,128,1024]{2,1,0:T(8,128)(2,1)S(1)}, bf16[2,128,1024]{2,1,0:T(8,128)(2,1)S(1)}, u32[]{:S(2)}, u32[]{:S(2)}) collective-permute-start(bf16[2,128,1024]{2,1,0:T(8,128)(2,1)S(1)} %get-tuple-element.114), channel_id=1, source_target_pairs={{0,2},{1,3},{2,0},{3,1},{4,6},{5,7},{6,4},{7,5},{8,10},{9,11},{10,... | collective-permute-start | bytes 1572872 | tf_op jit(solution)/shard_map/ppermute | solution.py:28
  57.1 1.6 collective-permute-start.16
  58.8 13.7 %collective-permute-start.20 = (bf16[2,128,512]{2,1,0:T(8,128)(2,1)S(1)}, bf16[2,128,512]{2,1,0:T(8,128)(2,1)S(1)}, u32[]{:S(2)}, u32[]{:S(2)}) collective-permute-start(bf16[2,128,512]{2,1,0:T(8,128)(2,1)S(1)} %get-tuple-element.112), channel_id=1, source_target_pairs={{0,2},{1,3},{2,0},{3,1},{4,6},{5,7},{6,4},{7,5},{8,10},{9,11},{10,... | collective-permute-start | bytes 786440 | tf_op jit(solution)/shard_map/ppermute | solution.py:28
  59.7 8.4 %collective-permute-start.17 = (bf16[2,128,1024]{2,1,0:T(8,128)(2,1)S(1)}, bf16[2,128,1024]{2,1,0:T(8,128)(2,1)S(1)}, u32[]{:S(2)}, u32[]{:S(2)}) collective-permute-start(bf16[2,128,1024]{2,1,0:T(8,128)(2,1)S(1)} %pad_maximum_fusion.4), channel_id=1, source_target_pairs={{0,1},{1,0},{2,3},{3,2},{4,5},{5,4},{6,7},{7,6},{8,9},{9,8},{10,11... | collective-permute-start | bytes 1572872 | tf_op jit(solution)/shard_map/ppermute | solution.py:28
  68.1 3.1 %collective-permute-start.19 = (bf16[2,128,1024]{2,1,0:T(8,128)(2,1)S(1)}, bf16[2,128,1024]{2,1,0:T(8,128)(2,1)S(1)}, u32[]{:S(2)}, u32[]{:S(2)}) collective-permute-start(bf16[2,128,1024]{2,1,0:T(8,128)(2,1)S(1)} %pad_maximum_fusion.5), channel_id=1, source_target_pairs={{0,1},{1,0},{2,3},{3,2},{4,5},{5,4},{6,7},{7,6},{8,9},{9,8},{10,11... | collective-permute-start | bytes 1572872 | tf_op jit(solution)/shard_map/ppermute | solution.py:28
  72.7 1.7 %collective-permute-start.21 = (bf16[2,128,512]{2,1,0:T(8,128)(2,1)S(1)}, bf16[2,128,512]{2,1,0:T(8,128)(2,1)S(1)}, u32[]{:S(2)}, u32[]{:S(2)}) collective-permute-start(bf16[2,128,512]{2,1,0:T(8,128)(2,1)S(1)} %pad_maximum_fusion.10), channel_id=1, source_target_pairs={{0,1},{1,0},{2,3},{3,2},{4,5},{5,4},{6,7},{7,6},{8,9},{9,8},{10,11... | collective-permute-start | bytes 786440 | tf_op jit(solution)/shard_map/ppermute | solution.py:28
  77.3 7.2 %collective-permute-start.22 = (bf16[64,1536]{1,0:T(8,128)(2,1)S(1)}, bf16[64,1536]{1,0:T(8,128)(2,1)S(1)}, u32[]{:S(2)}, u32[]{:S(2)}) collective-permute-start(bf16[64,1536]{1,0:T(8,128)(2,1)S(1)} %pad_maximum_fusion.13), channel_id=1, source_target_pairs={{0,4},{4,0},{8,12},{12,8},{16,20},{20,16},{24,28},{28,24},{1,5},{5... | collective-permute-start | bytes 589832 | tf_op jit(solution)/shard_map/ppermute | solution.py:33
  84.5 7.8 %collective-permute-start.23 = (bf16[64,1536]{1,0:T(8,128)(2,1)S(1)}, bf16[64,1536]{1,0:T(8,128)(2,1)S(1)}, u32[]{:S(2)}, u32[]{:S(2)}) collective-permute-start(bf16[64,1536]{1,0:T(8,128)(2,1)S(1)} %get-tuple-element.87), channel_id=1, source_target_pairs={{0,4},{4,0},{8,12},{12,8},{16,20},{20,16},{24,28},{28,24},{1,5},{5... | collective-permute-start | bytes 589832 | tf_op jit(solution)/shard_map/ppermute | solution.py:33
  85.9 7.8 %collective-permute-start.25 = (bf16[64,1536]{1,0:T(8,128)(2,1)S(1)}, bf16[64,1536]{1,0:T(8,128)(2,1)S(1)}, u32[]{:S(2)}, u32[]{:S(2)}) collective-permute-start(bf16[64,1536]{1,0:T(8,128)(2,1)S(1)} %fusion.52), channel_id=1, source_target_pairs={{0,8},{4,12},{8,0},{12,4},{16,24},{20,28},{24,16},{28,20},{1,9},{5... | collective-permute-start | bytes 589832 | tf_op jit(solution)/shard_map/ppermute | solution.py:33
  86.0 11.2 %collective-permute-start.27 = (bf16[64,1536]{1,0:T(8,128)(2,1)S(1)}, bf16[64,1536]{1,0:T(8,128)(2,1)S(1)}, u32[]{:S(2)}, u32[]{:S(2)}) collective-permute-start(bf16[64,1536]{1,0:T(8,128)(2,1)S(1)} %get-tuple-element.90), channel_id=1, source_target_pairs={{0,4},{4,0},{8,12},{12,8},{16,20},{20,16},{24,28},{28,24},{1,5},{5... | collective-permute-start | bytes 589832 | tf_op jit(solution)/shard_map/ppermute | solution.py:33
  92.3 7.0 %collective-permute-start.24 = (bf16[64,1536]{1,0:T(8,128)(2,1)S(1)}, bf16[64,1536]{1,0:T(8,128)(2,1)S(1)}, u32[]{:S(2)}, u32[]{:S(2)}) collective-permute-start(bf16[64,1536]{1,0:T(8,128)(2,1)S(1)} %pad_maximum_fusion.12), channel_id=1, source_target_pairs={{0,4},{4,0},{8,12},{12,8},{16,20},{20,16},{24,28},{28,24},{1,5},{5... | collective-permute-start | bytes 589832 | tf_op jit(solution)/shard_map/ppermute | solution.py:33
  93.7 11.6 %collective-permute-start.26 = (bf16[64,1536]{1,0:T(8,128)(2,1)S(1)}, bf16[64,1536]{1,0:T(8,128)(2,1)S(1)}, u32[]{:S(2)}, u32[]{:S(2)}) collective-permute-start(bf16[64,1536]{1,0:T(8,128)(2,1)S(1)} %fusion.51), channel_id=1, source_target_pairs={{0,16},{4,20},{8,24},{12,28},{16,0},{20,4},{24,8},{28,12},{1,17},{... | collective-permute-start | bytes 589832 | tf_op jit(solution)/shard_map/ppermute | solution.py:33
  97.2 8.1 %collective-permute-start.28 = (bf16[64,1536]{1,0:T(8,128)(2,1)S(1)}, bf16[64,1536]{1,0:T(8,128)(2,1)S(1)}, u32[]{:S(2)}, u32[]{:S(2)}) collective-permute-start(bf16[64,1536]{1,0:T(8,128)(2,1)S(1)} %fusion.53), channel_id=1, source_target_pairs={{0,8},{4,12},{8,0},{12,4},{16,24},{20,28},{24,16},{28,20},{1,9},{5... | collective-permute-start | bytes 589832 | tf_op jit(solution)/shard_map/ppermute | solution.py:33
  105.7 3.4 %collective-permute-start.31 = (f32[32,128]{1,0:T(8,128)S(1)}, f32[32,128]{1,0:T(8,128)S(1)}, u32[]{:S(2)}, u32[]{:S(2)}) collective-permute-start(f32[32,128]{1,0:T(8,128)S(1)} %get-tuple-element.94.refs_0_), channel_id=1, source_target_pairs={{0,3},{1,2},{2,1},{3,0},{4,7},{5,6},{6,5},{7,4},{8,11},{9,10},{10,... | collective-permute-start | bytes 49160 | tf_op jit(solution)/shard_map/ppermute | solution.py:28
  105.8 3.8 %collective-permute-start.30 = (f32[32,128]{1,0:T(8,128)S(1)}, f32[32,128]{1,0:T(8,128)S(1)}, u32[]{:S(2)}, u32[]{:S(2)}) collective-permute-start(f32[32,128]{1,0:T(8,128)S(1)} %get-tuple-element.94.refs_0_), channel_id=1, source_target_pairs={{0,2},{1,3},{2,0},{3,1},{4,6},{5,7},{6,4},{7,5},{8,10},{9,11},{10,... | collective-permute-start | bytes 49160 | tf_op jit(solution)/shard_map/ppermute | solution.py:28
  107.3 2.3 %collective-permute-start.29 = (f32[32,128]{1,0:T(8,128)S(1)}, f32[32,128]{1,0:T(8,128)S(1)}, u32[]{:S(2)}, u32[]{:S(2)}) collective-permute-start(f32[32,128]{1,0:T(8,128)S(1)} %get-tuple-element.94.refs_0_), channel_id=1, source_target_pairs={{0,1},{1,0},{2,3},{3,2},{4,5},{5,4},{6,7},{7,6},{8,9},{9,8},{10,11... | collective-permute-start | bytes 49160 | tf_op jit(solution)/shard_map/ppermute | solution.py:28
  110.4 7.4 %collective-permute-start.35 = (bf16[32,1536]{1,0:T(8,128)(2,1)S(1)}, bf16[32,1536]{1,0:T(8,128)(2,1)S(1)}, u32[]{:S(2)}, u32[]{:S(2)}) collective-permute-start(bf16[32,1536]{1,0:T(8,128)(2,1)S(1)} %cotangent_kernel.1), channel_id=1, source_target_pairs={{0,16},{4,20},{8,24},{12,28},{16,0},{20,4},{24,8},{28,12},{1,17},{... | collective-permute-start | bytes 294920 | tf_op jit(solution)/shard_map/ppermute | solution.py:33
  110.8 7.9 %collective-permute-start.33 = (bf16[32,1536]{1,0:T(8,128)(2,1)S(1)}, bf16[32,1536]{1,0:T(8,128)(2,1)S(1)}, u32[]{:S(2)}, u32[]{:S(2)}) collective-permute-start(bf16[32,1536]{1,0:T(8,128)(2,1)S(1)} %cotangent_kernel.1), channel_id=1, source_target_pairs={{0,8},{4,12},{8,0},{12,4},{16,24},{20,28},{24,16},{28,20},{1,9},{5... | collective-permute-start | bytes 294920 | tf_op jit(solution)/shard_map/ppermute | solution.py:33
  112.4 7.3 %collective-permute-start.32 = (bf16[32,1536]{1,0:T(8,128)(2,1)S(1)}, bf16[32,1536]{1,0:T(8,128)(2,1)S(1)}, u32[]{:S(2)}, u32[]{:S(2)}) collective-permute-start(bf16[32,1536]{1,0:T(8,128)(2,1)S(1)} %cotangent_kernel.1), channel_id=1, source_target_pairs={{0,4},{4,0},{8,12},{12,8},{16,20},{20,16},{24,28},{28,24},{1,5},{5... | collective-permute-start | bytes 294920 | tf_op jit(solution)/shard_map/ppermute | solution.py:33
  117.7 4.8 %collective-permute-start.37 = (bf16[32,1536]{1,0:T(8,128)(2,1)S(1)}, bf16[32,1536]{1,0:T(8,128)(2,1)S(1)}, u32[]{:S(2)}, u32[]{:S(2)}) collective-permute-start(bf16[32,1536]{1,0:T(8,128)(2,1)S(1)} %collective-permute-done.35), channel_id=1, source_target_pairs={{0,8},{4,12},{8,0},{12,4},{16,24},{20,28},{24,16},{28,20},{1,9},{5... | collective-permute-start | bytes 294920 | tf_op jit(solution)/shard_map/ppermute | solution.py:33
  117.7 7.1 %collective-permute-start.36 = (bf16[32,1536]{1,0:T(8,128)(2,1)S(1)}, bf16[32,1536]{1,0:T(8,128)(2,1)S(1)}, u32[]{:S(2)}, u32[]{:S(2)}) collective-permute-start(bf16[32,1536]{1,0:T(8,128)(2,1)S(1)} %collective-permute-done.35), channel_id=1, source_target_pairs={{0,4},{4,0},{8,12},{12,8},{16,20},{20,16},{24,28},{28,24},{1,5},{5... | collective-permute-start | bytes 294920 | tf_op jit(solution)/shard_map/ppermute | solution.py:33
  118.7 6.1 %collective-permute-start.34 = (bf16[32,1536]{1,0:T(8,128)(2,1)S(1)}, bf16[32,1536]{1,0:T(8,128)(2,1)S(1)}, u32[]{:S(2)}, u32[]{:S(2)}) collective-permute-start(bf16[32,1536]{1,0:T(8,128)(2,1)S(1)} %collective-permute-done.33), channel_id=1, source_target_pairs={{0,4},{4,0},{8,12},{12,8},{16,20},{20,16},{24,28},{28,24},{1,5},{5... | collective-permute-start | bytes 294920 | tf_op jit(solution)/shard_map/ppermute | solution.py:33
  122.5 4.6 %collective-permute-start.38 = (bf16[32,1536]{1,0:T(8,128)(2,1)S(1)}, bf16[32,1536]{1,0:T(8,128)(2,1)S(1)}, u32[]{:S(2)}, u32[]{:S(2)}) collective-permute-start(bf16[32,1536]{1,0:T(8,128)(2,1)S(1)} %collective-permute-done.37), channel_id=1, source_target_pairs={{0,4},{4,0},{8,12},{12,8},{16,20},{20,16},{24,28},{28,24},{1,5},{5... | collective-permute-start | bytes 294920 | tf_op jit(solution)/shard_map/ppermute | solution.py:33
  129.8 2.4 %collective-permute-start.39 = (bf16[128,1536]{1,0:T(8,128)(2,1)S(1)}, bf16[128,1536]{1,0:T(8,128)(2,1)S(1)}, u32[]{:S(2)}, u32[]{:S(2)}) collective-permute-start(bf16[128,1536]{1,0:T(8,128)(2,1)S(1)} %get-tuple-element.99), channel_id=1, source_target_pairs={{0,1},{1,0},{2,3},{3,2},{4,5},{5,4},{6,7},{7,6},{8,9},{9,8},{10,11... | collective-permute-start | bytes 1179656 | tf_op jit(solution)/shard_map/ppermute | solution.py:28
  131.6 2.2 %collective-permute-start.43 = (bf16[128,1024]{1,0:T(8,128)(2,1)S(1)}, bf16[128,1024]{1,0:T(8,128)(2,1)S(1)}, u32[]{:S(2)}, u32[]{:S(2)}) collective-permute-start(bf16[128,1024]{1,0:T(8,128)(2,1)S(1)} %get-tuple-element.102), channel_id=1, source_target_pairs={{0,1},{1,0},{2,3},{3,2},{4,5},{5,4},{6,7},{7,6},{8,9},{9,8},{10,11... | collective-permute-start | bytes 786440 | tf_op jit(solution)/shard_map/ppermute | solution.py:28
  132.3 12.0 %collective-permute-start.42 = (bf16[128,1536]{1,0:T(8,128)(2,1)S(1)}, bf16[128,1536]{1,0:T(8,128)(2,1)S(1)}, u32[]{:S(2)}, u32[]{:S(2)}) collective-permute-start(bf16[128,1536]{1,0:T(8,128)(2,1)S(1)} %get-tuple-element.108), channel_id=1, source_target_pairs={{0,2},{1,3},{2,0},{3,1},{4,6},{5,7},{6,4},{7,5},{8,10},{9,11},{10,... | collective-permute-start | bytes 1179656 | tf_op jit(solution)/shard_map/ppermute | solution.py:28
  133.7 1.8 %collective-permute-start.40 = (bf16[128,512]{1,0:T(8,128)(2,1)S(1)}, bf16[128,512]{1,0:T(8,128)(2,1)S(1)}, u32[]{:S(2)}, u32[]{:S(2)}) collective-permute-start(bf16[128,512]{1,0:T(8,128)(2,1)S(1)} %get-tuple-element.101), channel_id=1, source_target_pairs={{0,1},{1,0},{2,3},{3,2},{4,5},{5,4},{6,7},{7,6},{8,9},{9,8},{10,11... | collective-permute-start | bytes 393224 | tf_op jit(solution)/shard_map/ppermute | solution.py:28
  133.9 16.1 %collective-permute-start.46 = (bf16[128,1024]{1,0:T(8,128)(2,1)S(1)}, bf16[128,1024]{1,0:T(8,128)(2,1)S(1)}, u32[]{:S(2)}, u32[]{:S(2)}) collective-permute-start(bf16[128,1024]{1,0:T(8,128)(2,1)S(1)} %get-tuple-element.106), channel_id=1, source_target_pairs={{0,2},{1,3},{2,0},{3,1},{4,6},{5,7},{6,4},{7,5},{8,10},{9,11},{10,... | collective-permute-start | bytes 786440 | tf_op jit(solution)/shard_map/ppermute | solution.py:28
  144.4 5.8 %collective-permute-start.44 = (bf16[128,1536]{1,0:T(8,128)(2,1)S(1)}, bf16[128,1536]{1,0:T(8,128)(2,1)S(1)}, u32[]{:S(2)}, u32[]{:S(2)}) collective-permute-start(bf16[128,1536]{1,0:T(8,128)(2,1)S(1)} %multiply_convert_fusion), channel_id=1, source_target_pairs={{0,1},{1,0},{2,3},{3,2},{4,5},{5,4},{6,7},{7,6},{8,9},{9,8},{10,11... | collective-permute-start | bytes 1179656 | tf_op jit(solution)/shard_map/ppermute | solution.py:28
  144.5 9.9 %collective-permute-start.41 = (bf16[128,512]{1,0:T(8,128)(2,1)S(1)}, bf16[128,512]{1,0:T(8,128)(2,1)S(1)}, u32[]{:S(2)}, u32[]{:S(2)}) collective-permute-start(bf16[128,512]{1,0:T(8,128)(2,1)S(1)} %get-tuple-element.110), channel_id=1, source_target_pairs={{0,2},{1,3},{2,0},{3,1},{4,6},{5,7},{6,4},{7,5},{8,10},{9,11},{10,... | collective-permute-start | bytes 393224 | tf_op jit(solution)/shard_map/ppermute | solution.py:28
  150.2 5.0 %collective-permute-start.47 = (bf16[128,1024]{1,0:T(8,128)(2,1)S(1)}, bf16[128,1024]{1,0:T(8,128)(2,1)S(1)}, u32[]{:S(2)}, u32[]{:S(2)}) collective-permute-start(bf16[128,1024]{1,0:T(8,128)(2,1)S(1)} %multiply_convert_fusion.1), channel_id=1, source_target_pairs={{0,1},{1,0},{2,3},{3,2},{4,5},{5,4},{6,7},{7,6},{8,9},{9,8},{10,11... | collective-permute-start | bytes 786440 | tf_op jit(solution)/shard_map/ppermute | solution.py:28
  154.6 3.6 %collective-permute-start.45 = (bf16[128,512]{1,0:T(8,128)(2,1)S(1)}, bf16[128,512]{1,0:T(8,128)(2,1)S(1)}, u32[]{:S(2)}, u32[]{:S(2)}) collective-permute-start(bf16[128,512]{1,0:T(8,128)(2,1)S(1)} %multiply_convert_fusion.4), channel_id=1, source_target_pairs={{0,1},{1,0},{2,3},{3,2},{4,5},{5,4},{6,7},{7,6},{8,9},{9,8},{10,11... | collective-permute-start | bytes 393224 | tf_op jit(solution)/shard_map/ppermute | solution.py:28
  (10 other events, 42.6 us)

commit v2 on v1

--- a/solution.py
+++ b/solution.py
@@ -77,8 +77,8 @@
     terms = {}
     for k, far in enumerate(order):
         sent = block(far + 1).astype(BF16)
-        if k >= 1:
-            sent = after(sent, *[terms[o][1] for o in order[: max(1, k - 1)]])
+        if k >= 2:
+            sent = after(sent, *[terms[o][1] for o in order[: k - 1]])
         terms[far] = [block(far), swap_dp(sent, 1)]
     pending = [(far, bit) for bit in far_bits() for far in order if far & bit and far & (bit - 1) < 2]
     pending.sort(key=lambda step: [-step[0], step[1]])
@@ -88,11 +88,7 @@
         total = after(total, *last) if last else total
         last = [total]
         terms[far ^ bit].append(swap_dp(total, bit))
-    return terms[0]
-
-
-def whole(array):
-    return pl.BlockSpec(array.shape, lambda *_: (0,) * array.ndim)
+    return terms[0], last[0]
 
 
 def cost(flops, *arrays):
@@ -133,6 +129,61 @@
     )(*[pltpu.with_memory_space_constraint(a, pltpu.HBM) for a in arrays], *earlier)
 
 
+def load_rows(array, start, height, *earlier):
+    def kernel(given_ref, *refs):
+        held, sems = refs[-2:]
+        step = height // LOADS
+        copies = []
+        for n in range(LOADS):
+            place = given_ref.at[pl.ds(start + n * step, step)]
+            copies.append(pltpu.make_async_copy(place, held.at[pl.ds(n * step, step)], sems.at[n]))
+            copies[n].start()
+        for copy in copies:
+            copy.wait()
+
+    return pl.pallas_call(
+        kernel,
+        in_specs=[pl.BlockSpec(memory_space=pl.ANY)] * (1 + len(earlier)),
+        out_specs=pl.BlockSpec(memory_space=pltpu.VMEM),
+        out_shape=pltpu.VMEM((height, array.shape[1]), array.dtype),
+        scratch_shapes=[pltpu.SemaphoreType.DMA((LOADS,))],
+        compiler_params=PARAMS,
+        cost_estimate=cost(0, array),
+        name="load_rows",
+    )(pltpu.with_memory_space_constraint(array, pltpu.HBM), *earlier)
+
+
+def back_kernel(first, rows_ref, weight_ref, *refs):
+    own_ref, other_ref = refs[-2:]
+    half, chunk = own_ref.shape
+    for start in range(0, chunk, TILE):
+        part = lax.dot_general(
+            rows_ref[...],
+            weight_ref[first + start : first + start + TILE],
+            (((1,), (1,)), ((), ())),
+            preferred_element_type=F32,
+        )
+        own_ref[:, start : start + TILE] = part[:half]
+        other_ref[:, start : start + TILE] = part[half:].astype(BF16)
+
+
+def back_parts(cotangent, weight, start, chunk, *earlier):
+    rows, width = cotangent.shape
+    half = rows // 2
+    vmem, anywhere = pl.BlockSpec(memory_space=pltpu.VMEM), pl.BlockSpec(memory_space=pl.ANY)
+    return pl.pallas_call(
+        functools.partial(back_kernel, start),
+        in_specs=[vmem, vmem] + [anywhere] * len(earlier),
+        out_shape=(
+            jax.ShapeDtypeStruct((half, chunk), F32),
+            jax.ShapeDtypeStruct((half, chunk), BF16),
+        ),
+        compiler_params=PARAMS,
+        cost_estimate=cost(2 * rows * width * chunk, cotangent),
+        name="back_parts",
+    )(cotangent, pltpu.with_memory_space_constraint(weight, pltpu.VMEM), *earlier)
+
+
 def up_kernel(rows_ref, weight_ref, tangent_ref, own_ref, other_ref):
     half = own_ref.shape[1]
     for start in range(0, own_ref.shape[2], TILE):
@@ -158,39 +209,6 @@
         cost_estimate=cost(4 * rows * width * chunk, normed),
         name="up_parts",
     )(normed, *held)
-
-
-def back_kernel(rows_ref, weight_ref, *refs):
-    own_ref, other_ref = refs[-2:]
-    half = own_ref.shape[0]
-    part = lax.dot_general(
-        rows_ref[...], weight_ref[...], (((1,), (1,)), ((), ())), preferred_element_type=F32
-    )
-    own_ref[...] = part[:half]
-    other_ref[...] = part[half:].astype(BF16)
-
-
-def back_parts(cotangent, weight, start, chunk, *earlier):
-    rows, width = cotangent.shape
-    half = rows // 2
-    first = start // TILE
-    out_spec = pl.BlockSpec((half, TILE), lambda i: (0, i))
-    out_shape = (
-        jax.ShapeDtypeStruct((half, chunk), F32),
-        jax.ShapeDtypeStruct((half, chunk), BF16),
-    )
-    moved = jax.ShapeDtypeStruct((width, chunk), BF16)
-    return pl.pallas_call(
-        back_kernel,
-        grid=(chunk // TILE,),
-        in_specs=[whole(cotangent), pl.BlockSpec((TILE, width), lambda i: (first + i, 0))]
-        + [pl.BlockSpec(memory_space=pl.ANY)] * len(earlier),
-        out_specs=(out_spec, out_spec),
-        out_shape=out_shape,
-        compiler_params=PARAMS,
-        cost_estimate=cost(2 * rows * width * chunk, cotangent, moved),
-        name="back_parts",
-    )(cotangent, weight, *earlier)
 
 
 def outer(left, right):
@@ -312,8 +330,9 @@
     refs[-1][...] = ((source - center) * inverse * gain_ref[...] + shift_ref[...]).astype(BF16)
 
 
-def stats_out_kernel(tokens_ref, gain_ref, curvature_ref, *refs):
-    *terms, output_ref, tangent_ref, stats_ref = refs
+def stats_out_kernel(count, tokens_ref, gain_ref, curvature_ref, *refs):
+    terms = refs[:count]
+    output_ref, tangent_ref, stats_ref = refs[-3:]
     rows, width = output_ref.shape
     total = sum(term[...].astype(F32) for term in terms)
     output = tokens_ref[...].astype(F32) + total[:rows]
@@ -468,15 +487,18 @@
         tangent = tangent_part if tangent is None else tangent + tangent_part
         done.append((primal, tangent))
 
-    terms = scatter_rows([primal, tangent], rows)
-    output, output_tangent, stats = in_vmem(
-        stats_out_kernel,
-        (rows_f32, rows_f32, stats_shape),
-        tokens,
-        gain_out,
-        curvature,
-        *terms,
-    )
+    terms, step = scatter_rows([primal, tangent], rows)
+    held = load_rows(down_weight, 0, hidden_units, step)
+    operands = [tokens, gain_out, curvature, *terms]
+    vmem = pl.BlockSpec(memory_space=pltpu.VMEM)
+    output, output_tangent, stats = pl.pallas_call(
+        functools.partial(stats_out_kernel, len(terms)),
+        in_specs=[vmem] * len(operands) + [pl.BlockSpec(memory_space=pl.ANY)],
+        out_shape=(rows_f32, rows_f32, stats_shape),
+        compiler_params=PARAMS,
+        cost_estimate=cost(0, *operands),
+        name="stats_out_kernel",
+    )(*operands, held)
     cotangent = in_vmem(
         cotangent_kernel,
         rows_bf16,
@@ -494,7 +516,7 @@
     starts = [0] + starts[merged:]
     totals, lhs = [], all_cotangent
     for start, chunk in zip(starts, sizes):
-        own, other = back_parts(lhs, down_weight, start, chunk, *totals[:-1])
+        own, other = back_parts(lhs, held, start, chunk, *totals[:-1])
         totals.append(own + swap_tensor(other, 1).astype(F32))
         lhs = after(all_cotangent, own)
     down_product = outer_rows(hiddens, all_cotangent, down_weight.shape, *totals)

time: 161 us -> 158 us (0.981)
  waiting for transfers between devices: 61.2 us -> 56.2 us
  Pallas kernels: 37.9 us -> 39.9 us
    ppermute x21, waiting for transfers between devices: 34.8 us -> 29.5 us  [swap_dp(): return lax.ppermute(value, 'dp', [(i, i ^ flip) for i in range(size)])]
    pallas_call x3 -> x5, Pallas kernels: 5.07 us -> 7.13 us  [the longest x1 3.8 us: load_rows(): pl.pallas_call(kernel, in_specs=[pl.BlockSpec(memory_space=pl.ANY)] * (1...]
  transfers between devices with their start and end apart: 48 -> 48, of which waited for: 22 -> 23; matrix products, arithmetic and copies ran while one was open for 8% -> 8% of each run, Pallas kernels for 19% -> 22%
where the time goes in v2:
time: 158 us
  waiting for transfers between devices  56.2 us (36%)
  starting transfers between devices  41.2 us (26%)
  Pallas kernels  39.9 us (25%)
  matrix products  9.52 us (6%)
  local copies, waits for them, and re-layouts  5.17 us (3%)
  other arithmetic  3.78 us (2%)
  between operations  1.86 us (1%)
    ppermute x21, waiting for transfers between devices, swap_dp(): return lax.ppermute(value, 'dp', [(i, i ^ flip) for i in range(size)])  29.5 us
    ppermute x27, waiting for transfers between devices, swap_tensor(): return lax.ppermute(value, 'tensor', [(t, t ^ flip) for t in range(size)])  26.7 us
    ppermute x21, starting transfers between devices, swap_dp(): return lax.ppermute(value, 'dp', [(i, i ^ flip) for i in range(size)])  25.8 us
    ppermute x27, starting transfers between devices, swap_tensor(): return lax.ppermute(value, 'tensor', [(t, t ^ flip) for t in range(size)])  15.5 us
    pallas_call x4, Pallas kernels, load_columns(): pl.pallas_call(functools.partial(load_kernel, start, len(arrays)), in_spe...  9.79 us
    pallas_call x3, Pallas kernels, outer_columns(): pl.pallas_call(functools.partial(columns_kernel, column), in_specs=[vmem,...  9.35 us
    pallas_call x1, Pallas kernels, outer_rows(): pl.pallas_call(functools.partial(rows_kernel, len(lefts)), in_specs=[vmem...  6.92 us
    pallas_call x4, Pallas kernels, up_parts(): pl.pallas_call(up_kernel, out_shape=out_shape, compiler_params=PARAMS, co...  5.54 us
  transfers between devices with their start and end apart: 48, of which 23 were waited for; matrix products, arithmetic and copies ran while one was open for 8% of the time, Pallas kernels for 22%

profile of v2, /device:TPU:0, one launch (start us, length us, event | category | flops | bytes accessed | tf_op | source)
XLA Modules:
  0.0 157.7 jit_solution(4492220413733927932)
XLA Ops:
  1.7 2.4 %collective-permute-start.2 = (f32[32,128]{1,0:T(8,128)S(1)}, f32[32,128]{1,0:T(8,128)S(1)}, u32[]{:S(2)}, u32[]{:S(2)}) collective-permute-start(f32[32,128]{1,0:T(8,128)S(1)} %get-tuple-element.54.refs_0_), channel_id=1, source_target_pairs={{0,3},{1,2},{2,1},{3,0},{4,7},{5,6},{6,5},{7,4},{8,11},{9,10},{10,... | collective-permute-start | bytes 49160 | tf_op jit(solution)/shard_map/ppermute | solution.py:28
  8.1 2.7 %collective-permute-start.6 = (bf16[32,1536]{1,0:T(8,128)(2,1)S(1)}, bf16[32,1536]{1,0:T(8,128)(2,1)S(1)}, u32[]{:S(2)}, u32[]{:S(2)}) collective-permute-start(bf16[32,1536]{1,0:T(8,128)(2,1)S(1)} %norm_in_kernel.1), channel_id=1, source_target_pairs={{0,16},{4,20},{8,24},{12,28},{16,0},{20,4},{24,8},{28,12},{1,17},{... | collective-permute-start | bytes 294920 | tf_op jit(solution)/shard_map/ppermute | solution.py:33
  10.7 1.6 collective-permute-start.4
  12.3 1.5 collective-permute-start.3
  13.8 1.8 %collective-permute-done.6 = bf16[32,1536]{1,0:T(8,128)(2,1)S(1)} collective-permute-done((bf16[32,1536]{1,0:T(8,128)(2,1)S(1)}, bf16[32,1536]{1,0:T(8,128)(2,1)S(1)}, u32[]{:S(2)}, u32[]{:S(2)}) %collective-permute-start.6) | collective-permute-done | bytes 98336 | tf_op jit(solution)/shard_map/ppermute | solution.py:33
  16.3 1.5 collective-permute-start.7
  18.4 1.9 %collective-permute-done.8 = bf16[32,1536]{1,0:T(8,128)(2,1)S(1)} collective-permute-done((bf16[32,1536]{1,0:T(8,128)(2,1)S(1)}, bf16[32,1536]{1,0:T(8,128)(2,1)S(1)}, u32[]{:S(2)}, u32[]{:S(2)}) %collective-permute-start.8) | collective-permute-done | bytes 98336 | tf_op jit(solution)/shard_map/ppermute | solution.py:33
  20.3 1.5 collective-permute-start.9
  21.7 2.3 %collective-permute-done.5 = bf16[32,1536]{1,0:T(8,128)(2,1)S(1)} collective-permute-done((bf16[32,1536]{1,0:T(8,128)(2,1)S(1)}, bf16[32,1536]{1,0:T(8,128)(2,1)S(1)}, u32[]{:S(2)}, u32[]{:S(2)}) %collective-permute-start.5) | collective-permute-done | bytes 98336 | tf_op jit(solution)/shard_map/ppermute | solution.py:33
  24.1 1.9 %load_columns.4 = (bf16[1536,512]{1,0:T(8,128)(2,1)S(1)}, bf16[1536,512]{1,0:T(8,128)(2,1)S(1)}) custom-call(bf16[1536,3072]{1,0:T(8,128)(2,1)} %refs_0_.3, bf16[1536,3072]{1,0:T(8,128)(2,1)} %refs_1_.7), custom_call_target="tpu_custom_call" | custom-call | bytes 3145 | tf_op jit(solution)/shard_map/load_columns/pallas_call | solution.py:120
  27.3 1.5 collective-permute-done.10
  28.9 1.5 collective-permute-start.11
  30.4 2.9 %load_columns.5 = (bf16[1536,1024]{1,0:T(8,128)(2,1)S(1)}, bf16[1536,1024]{1,0:T(8,128)(2,1)S(1)}) custom-call(bf16[1536,3072]{1,0:T(8,128)(2,1)} %refs_0_.3, bf16[1536,3072]{1,0:T(8,128)(2,1)} %refs_1_.7, f32[2,128,512]{2,1,0:T(8,128)S(1)} %get-tuple-element.117.refs_2_), custom_call_target="tpu_custom_call" | custom-call | bytes 6291 | tf_op jit(solution)/shard_map/load_columns/pallas_call | solution.py:120
  33.3 1.8 %up_parts.5 = (f32[2,128,1024]{2,1,0:T(8,128)S(1)}, bf16[2,128,1024]{2,1,0:T(8,128)(2,1)S(1)}) custom-call(bf16[256,1536]{1,0:T(8,128)(2,1)S(1)} %constant_dynamic-update-slice_fusion.rows_ref.left_ref, bf16[1536,1024]{1,0:T(8,128)(2,1)S(1)} %get-tuple-element.62.weight_ref, bf16[1536,1024]{1,0:T(8,128)(2,1)S(1)} %get-tuple-element.63.tangent_ref), custom_call_target="tpu_custom_call" | custom-call | flops 1610612 | bytes 786 | tf_op jit(solution)/shard_map/up_parts/pallas_call | solution.py:205
  35.2 2.1 %collective-permute-done.11 = bf16[2,128,512]{2,1,0:T(8,128)(2,1)S(1)} collective-permute-done((bf16[2,128,512]{2,1,0:T(8,128)(2,1)S(1)}, bf16[2,128,512]{2,1,0:T(8,128)(2,1)S(1)}, u32[]{:S(2)}, u32[]{:S(2)}) %collective-permute-start.11) | collective-permute-done | bytes 262176 | tf_op jit(solution)/shard_map/ppermute | solution.py:28
  38.0 1.5 collective-permute-start.14
  39.5 3.0 %load_columns.6 = (bf16[1536,1024]{1,0:T(8,128)(2,1)S(1)}, bf16[1536,1024]{1,0:T(8,128)(2,1)S(1)}) custom-call(bf16[1536,3072]{1,0:T(8,128)(2,1)} %refs_0_.3, bf16[1536,3072]{1,0:T(8,128)(2,1)} %refs_1_.7, f32[2,128,1024]{2,1,0:T(8,128)S(1)} %get-tuple-element.115.refs_2_), custom_call_target="tpu_custom_call" | custom-call | bytes 6291 | tf_op jit(solution)/shard_map/load_columns/pallas_call | solution.py:120
  42.6 1.8 %up_parts.6 = (f32[2,128,1024]{2,1,0:T(8,128)S(1)}, bf16[2,128,1024]{2,1,0:T(8,128)(2,1)S(1)}) custom-call(bf16[256,1536]{1,0:T(8,128)(2,1)S(1)} %constant_dynamic-update-slice_fusion.rows_ref.left_ref, bf16[1536,1024]{1,0:T(8,128)(2,1)S(1)} %get-tuple-element.70.weight_ref, bf16[1536,1024]{1,0:T(8,128)(2,1)S(1)} %get-tuple-element.71.tangent_ref), custom_call_target="tpu_custom_call" | custom-call | flops 1610612 | bytes 786 | tf_op jit(solution)/shard_map/up_parts/pallas_call | solution.py:205
  47.9 4.5 %collective-permute-done.14 = bf16[2,128,1024]{2,1,0:T(8,128)(2,1)S(1)} collective-permute-done((bf16[2,128,1024]{2,1,0:T(8,128)(2,1)S(1)}, bf16[2,128,1024]{2,1,0:T(8,128)(2,1)S(1)}, u32[]{:S(2)}, u32[]{:S(2)}) %collective-permute-start.14) | collective-permute-done | bytes 524320 | tf_op jit(solution)/shard_map/ppermute | solution.py:28
  52.6 1.5 collective-permute-start.18
  54.1 1.9 %load_columns.7 = (bf16[1536,512]{1,0:T(8,128)(2,1)S(1)}, bf16[1536,512]{1,0:T(8,128)(2,1)S(1)}) custom-call(bf16[1536,3072]{1,0:T(8,128)(2,1)} %refs_0_.3, bf16[1536,3072]{1,0:T(8,128)(2,1)} %refs_1_.7, f32[2,128,1024]{2,1,0:T(8,128)S(1)} %get-tuple-element.113.refs_2_), custom_call_target="tpu_custom_call" | custom-call | bytes 3145 | tf_op jit(solution)/shard_map/load_columns/pallas_call | solution.py:120
  57.3 1.3 collective-permute-done.16
  60.0 7.5 %collective-permute-done.18 = bf16[2,128,1024]{2,1,0:T(8,128)(2,1)S(1)} collective-permute-done((bf16[2,128,1024]{2,1,0:T(8,128)(2,1)S(1)}, bf16[2,128,1024]{2,1,0:T(8,128)(2,1)S(1)}, u32[]{:S(2)}, u32[]{:S(2)}) %collective-permute-start.18) | collective-permute-done | bytes 524320 | tf_op jit(solution)/shard_map/ppermute | solution.py:28
  77.3 1.4 collective-permute-start.22
  79.6 5.5 %collective-permute-done.22 = bf16[64,1536]{1,0:T(8,128)(2,1)S(1)} collective-permute-done((bf16[64,1536]{1,0:T(8,128)(2,1)S(1)}, bf16[64,1536]{1,0:T(8,128)(2,1)S(1)}, u32[]{:S(2)}, u32[]{:S(2)}) %collective-permute-start.22) | collective-permute-done | bytes 196640 | tf_op jit(solution)/shard_map/ppermute | solution.py:33
  86.6 2.6 %collective-permute-done.23 = bf16[64,1536]{1,0:T(8,128)(2,1)S(1)} collective-permute-done((bf16[64,1536]{1,0:T(8,128)(2,1)S(1)}, bf16[64,1536]{1,0:T(8,128)(2,1)S(1)}, u32[]{:S(2)}, u32[]{:S(2)}) %collective-permute-start.23) | collective-permute-done | bytes 196640 | tf_op jit(solution)/shard_map/ppermute | solution.py:33
  89.3 1.3 collective-permute-start.24
  91.1 3.7 %collective-permute-start.26 = (bf16[64,1536]{1,0:T(8,128)(2,1)S(1)}, bf16[64,1536]{1,0:T(8,128)(2,1)S(1)}, u32[]{:S(2)}, u32[]{:S(2)}) collective-permute-start(bf16[64,1536]{1,0:T(8,128)(2,1)S(1)} %fusion.51), channel_id=1, source_target_pairs={{0,16},{4,20},{8,24},{12,28},{16,0},{20,4},{24,8},{28,12},{1,17},{... | collective-permute-start | bytes 589832 | tf_op jit(solution)/shard_map/ppermute | solution.py:33
  95.3 3.8 %load_rows.1.refs_4_.weight_ref = bf16[3072,1536]{1,0:T(8,128)(2,1)S(1)} custom-call(bf16[3072,1536]{1,0:T(8,128)(2,1)} %given_ref.3, bf16[64,1536]{1,0:T(8,128)(2,1)S(1)} %fusion.53.refs_0_), custom_call_target="tpu_custom_call" | custom-call | bytes 9437 | tf_op jit(solution)/shard_map/load_rows/pallas_call | solution.py:144
  99.1 5.0 %collective-permute-done.28.refs_3_ = bf16[64,1536]{1,0:T(8,128)(2,1)S(1)} collective-permute-done((bf16[64,1536]{1,0:T(8,128)(2,1)S(1)}, bf16[64,1536]{1,0:T(8,128)(2,1)S(1)}, u32[]{:S(2)}, u32[]{:S(2)}) %collective-permute-start.28) | collective-permute-done | bytes 196640 | tf_op jit(solution)/shard_map/ppermute | solution.py:33
  104.6 1.5 collective-permute-start.30
  106.5 1.4 collective-permute-done.31.refs_3_
  109.3 1.9 %collective-permute-start.33 = (bf16[32,1536]{1,0:T(8,128)(2,1)S(1)}, bf16[32,1536]{1,0:T(8,128)(2,1)S(1)}, u32[]{:S(2)}, u32[]{:S(2)}) collective-permute-start(bf16[32,1536]{1,0:T(8,128)(2,1)S(1)} %cotangent_kernel.1), channel_id=1, source_target_pairs={{0,8},{4,12},{8,0},{12,4},{16,24},{20,28},{24,16},{28,20},{1,9},{5... | collective-permute-start | bytes 294920 | tf_op jit(solution)/shard_map/ppermute | solution.py:33
  111.1 1.6 %collective-permute-start.32 = (bf16[32,1536]{1,0:T(8,128)(2,1)S(1)}, bf16[32,1536]{1,0:T(8,128)(2,1)S(1)}, u32[]{:S(2)}, u32[]{:S(2)}) collective-permute-start(bf16[32,1536]{1,0:T(8,128)(2,1)S(1)} %cotangent_kernel.1), channel_id=1, source_target_pairs={{0,4},{4,0},{8,12},{12,8},{16,20},{20,16},{24,28},{28,24},{1,5},{5... | collective-permute-start | bytes 294920 | tf_op jit(solution)/shard_map/ppermute | solution.py:33
  112.7 3.7 %collective-permute-done.35 = bf16[32,1536]{1,0:T(8,128)(2,1)S(1)} collective-permute-done((bf16[32,1536]{1,0:T(8,128)(2,1)S(1)}, bf16[32,1536]{1,0:T(8,128)(2,1)S(1)}, u32[]{:S(2)}, u32[]{:S(2)}) %collective-permute-start.35) | collective-permute-done | bytes 98336 | tf_op jit(solution)/shard_map/ppermute | solution.py:33
  116.5 1.2 collective-permute-start.36
  118.5 2.7 %collective-permute-done.37 = bf16[32,1536]{1,0:T(8,128)(2,1)S(1)} collective-permute-done((bf16[32,1536]{1,0:T(8,128)(2,1)S(1)}, bf16[32,1536]{1,0:T(8,128)(2,1)S(1)}, u32[]{:S(2)}, u32[]{:S(2)}) %collective-permute-start.37) | collective-permute-done | bytes 98336 | tf_op jit(solution)/shard_map/ppermute | solution.py:33
  121.2 1.2 collective-permute-start.38
  122.4 1.2 collective-permute-done.34
  123.6 2.2 %collective-permute-done.38 = bf16[32,1536]{1,0:T(8,128)(2,1)S(1)} collective-permute-done((bf16[32,1536]{1,0:T(8,128)(2,1)S(1)}, bf16[32,1536]{1,0:T(8,128)(2,1)S(1)}, u32[]{:S(2)}, u32[]{:S(2)}) %collective-permute-start.38) | collective-permute-done | bytes 98336 | tf_op jit(solution)/shard_map/ppermute | solution.py:33
  126.0 1.4 back_parts.3
  130.6 1.6 %collective-permute-start.46 = (bf16[128,1024]{1,0:T(8,128)(2,1)S(1)}, bf16[128,1024]{1,0:T(8,128)(2,1)S(1)}, u32[]{:S(2)}, u32[]{:S(2)}) collective-permute-start(bf16[128,1024]{1,0:T(8,128)(2,1)S(1)} %get-tuple-element.104), channel_id=1, source_target_pairs={{0,2},{1,3},{2,0},{3,1},{4,6},{5,7},{6,4},{7,5},{8,10},{9,11},{10,... | collective-permute-start | bytes 786440 | tf_op jit(solution)/shard_map/ppermute | solution.py:28
  132.3 6.9 %outer_rows.1 = f32[3072,1536]{1,0:T(8,128)} custom-call(bf16[256,512]{1,0:T(8,128)(2,1)S(1)} %slice_bitcast_fusion.11.refs_0_, bf16[256,1024]{1,0:T(8,128)(2,1)S(1)} %slice_bitcast_fusion.5.refs_1_, bf16[256,1024]{1,0:T(8,128)(2,1)S(1)} %slice_bitcast_fusion.4.refs_2_, bf16[256,512]{1,0:T(8,128)(2,1)S(1)} %slice_bitcast_fusion.8.refs_3_, ...), custom_call_target="tpu_custom_call" | custom-call | flops 2415919 | bytes 19660 | tf_op jit(solution)/shard_map/outer_rows/pallas_call | solution.py:275
  139.2 2.1 %collective-permute-done.42 = bf16[128,1536]{1,0:T(8,128)(2,1)S(1)} collective-permute-done((bf16[128,1536]{1,0:T(8,128)(2,1)S(1)}, bf16[128,1536]{1,0:T(8,128)(2,1)S(1)}, u32[]{:S(2)}, u32[]{:S(2)}) %collective-permute-start.42) | collective-permute-done | bytes 393248 | tf_op jit(solution)/shard_map/ppermute | solution.py:28
  142.0 4.9 %collective-permute-done.46 = bf16[128,1024]{1,0:T(8,128)(2,1)S(1)} collective-permute-done((bf16[128,1024]{1,0:T(8,128)(2,1)S(1)}, bf16[128,1024]{1,0:T(8,128)(2,1)S(1)}, u32[]{:S(2)}, u32[]{:S(2)}) %collective-permute-start.46) | collective-permute-done | bytes 262176 | tf_op jit(solution)/shard_map/ppermute | solution.py:28
  147.4 4.3 %outer_columns.3.refs_0_ = f32[1536,3072]{1,0:T(8,128)} custom-call(bf16[256,1536]{1,0:T(8,128)(2,1)S(1)} %constant_dynamic-update-slice_fusion.rows_ref.left_ref, bf16[256,1536]{1,0:T(8,128)(2,1)S(1)} %pad_maximum_fusion.2.right_ref), custom_call_target="tpu_custom_call" | custom-call | flops 1207959 | bytes 11010 | tf_op jit(solution)/shard_map/outer_columns/pallas_call | solution.py:236
  152.4 3.0 %outer_columns.4.refs_0_ = f32[1536,3072]{1,0:T(8,128)} custom-call(bf16[256,1536]{1,0:T(8,128)(2,1)S(1)} %constant_dynamic-update-slice_fusion.rows_ref.left_ref, bf16[256,1024]{1,0:T(8,128)(2,1)S(1)} %pad_maximum_fusion.7.right_ref, f32[1536,3072]{1,0:T(8,128)} %outer_columns.3.refs_0_), custom_call_target="tpu_custom_call", output_to_operand_aliasing={{}: (2, {})} | custom-call | flops 805306 | bytes 7602 | tf_op jit(solution)/shard_map/outer_columns/pallas_call | solution.py:236
  155.5 2.0 %outer_columns.5 = f32[1536,3072]{1,0:T(8,128)} custom-call(bf16[256,1536]{1,0:T(8,128)(2,1)S(1)} %constant_dynamic-update-slice_fusion.rows_ref.left_ref, bf16[256,512]{1,0:T(8,128)(2,1)S(1)} %pad_maximum_fusion.11.right_ref, f32[1536,3072]{1,0:T(8,128)} %outer_columns.4.refs_0_), custom_call_target="tpu_custom_call", output_to_operand_aliasing={{}: (2, {})} | custom-call | flops 402653 | bytes 4194 | tf_op jit(solution)/shard_map/outer_columns/pallas_call | solution.py:236
  (186 shorter events, 35.5 us)
Async XLA Ops:
  1.7 5.5 %collective-permute-start.2 = (f32[32,128]{1,0:T(8,128)S(1)}, f32[32,128]{1,0:T(8,128)S(1)}, u32[]{:S(2)}, u32[]{:S(2)}) collective-permute-start(f32[32,128]{1,0:T(8,128)S(1)} %get-tuple-element.54.refs_0_), channel_id=1, source_target_pairs={{0,3},{1,2},{2,1},{3,0},{4,7},{5,6},{6,5},{7,4},{8,11},{9,10},{10,... | collective-permute-start | bytes 49160 | tf_op jit(solution)/shard_map/ppermute | solution.py:28
  4.1 3.7 %collective-permute-start.1 = (f32[32,128]{1,0:T(8,128)S(1)}, f32[32,128]{1,0:T(8,128)S(1)}, u32[]{:S(2)}, u32[]{:S(2)}) collective-permute-start(f32[32,128]{1,0:T(8,128)S(1)} %get-tuple-element.54.refs_0_), channel_id=1, source_target_pairs={{0,2},{1,3},{2,0},{3,1},{4,6},{5,7},{6,4},{7,5},{8,10},{9,11},{10,... | collective-permute-start | bytes 49160 | tf_op jit(solution)/shard_map/ppermute | solution.py:28
  4.8 3.1 %collective-permute-start = (f32[32,128]{1,0:T(8,128)S(1)}, f32[32,128]{1,0:T(8,128)S(1)}, u32[]{:S(2)}, u32[]{:S(2)}) collective-permute-start(f32[32,128]{1,0:T(8,128)S(1)} %get-tuple-element.54.refs_0_), channel_id=1, source_target_pairs={{0,1},{1,0},{2,3},{3,2},{4,5},{5,4},{6,7},{7,6},{8,9},{9,8},{10,11... | collective-permute-start | bytes 49160 | tf_op jit(solution)/shard_map/ppermute | solution.py:28
  8.1 7.6 %collective-permute-start.6 = (bf16[32,1536]{1,0:T(8,128)(2,1)S(1)}, bf16[32,1536]{1,0:T(8,128)(2,1)S(1)}, u32[]{:S(2)}, u32[]{:S(2)}) collective-permute-start(bf16[32,1536]{1,0:T(8,128)(2,1)S(1)} %norm_in_kernel.1), channel_id=1, source_target_pairs={{0,16},{4,20},{8,24},{12,28},{16,0},{20,4},{24,8},{28,12},{1,17},{... | collective-permute-start | bytes 294920 | tf_op jit(solution)/shard_map/ppermute | solution.py:33
  10.7 7.1 %collective-permute-start.4 = (bf16[32,1536]{1,0:T(8,128)(2,1)S(1)}, bf16[32,1536]{1,0:T(8,128)(2,1)S(1)}, u32[]{:S(2)}, u32[]{:S(2)}) collective-permute-start(bf16[32,1536]{1,0:T(8,128)(2,1)S(1)} %norm_in_kernel.1), channel_id=1, source_target_pairs={{0,8},{4,12},{8,0},{12,4},{16,24},{20,28},{24,16},{28,20},{1,9},{5... | collective-permute-start | bytes 294920 | tf_op jit(solution)/shard_map/ppermute | solution.py:33
  12.3 6.0 %collective-permute-start.3 = (bf16[32,1536]{1,0:T(8,128)(2,1)S(1)}, bf16[32,1536]{1,0:T(8,128)(2,1)S(1)}, u32[]{:S(2)}, u32[]{:S(2)}) collective-permute-start(bf16[32,1536]{1,0:T(8,128)(2,1)S(1)} %norm_in_kernel.1), channel_id=1, source_target_pairs={{0,4},{4,0},{8,12},{12,8},{16,20},{20,16},{24,28},{28,24},{1,5},{5... | collective-permute-start | bytes 294920 | tf_op jit(solution)/shard_map/ppermute | solution.py:33
  15.6 4.6 %collective-permute-start.8 = (bf16[32,1536]{1,0:T(8,128)(2,1)S(1)}, bf16[32,1536]{1,0:T(8,128)(2,1)S(1)}, u32[]{:S(2)}, u32[]{:S(2)}) collective-permute-start(bf16[32,1536]{1,0:T(8,128)(2,1)S(1)} %collective-permute-done.6), channel_id=1, source_target_pairs={{0,8},{4,12},{8,0},{12,4},{16,24},{20,28},{24,16},{28,20},{1,9},{5... | collective-permute-start | bytes 294920 | tf_op jit(solution)/shard_map/ppermute | solution.py:33
  16.3 7.7 %collective-permute-start.7 = (bf16[32,1536]{1,0:T(8,128)(2,1)S(1)}, bf16[32,1536]{1,0:T(8,128)(2,1)S(1)}, u32[]{:S(2)}, u32[]{:S(2)}) collective-permute-start(bf16[32,1536]{1,0:T(8,128)(2,1)S(1)} %collective-permute-done.6), channel_id=1, source_target_pairs={{0,4},{4,0},{8,12},{12,8},{16,20},{20,16},{24,28},{28,24},{1,5},{5... | collective-permute-start | bytes 294920 | tf_op jit(solution)/shard_map/ppermute | solution.py:33
  17.8 6.2 %collective-permute-start.5 = (bf16[32,1536]{1,0:T(8,128)(2,1)S(1)}, bf16[32,1536]{1,0:T(8,128)(2,1)S(1)}, u32[]{:S(2)}, u32[]{:S(2)}) collective-permute-start(bf16[32,1536]{1,0:T(8,128)(2,1)S(1)} %collective-permute-done.4), channel_id=1, source_target_pairs={{0,4},{4,0},{8,12},{12,8},{16,20},{20,16},{24,28},{28,24},{1,5},{5... | collective-permute-start | bytes 294920 | tf_op jit(solution)/shard_map/ppermute | solution.py:33
  20.3 5.8 %collective-permute-start.9 = (bf16[32,1536]{1,0:T(8,128)(2,1)S(1)}, bf16[32,1536]{1,0:T(8,128)(2,1)S(1)}, u32[]{:S(2)}, u32[]{:S(2)}) collective-permute-start(bf16[32,1536]{1,0:T(8,128)(2,1)S(1)} %collective-permute-done.8), channel_id=1, source_target_pairs={{0,4},{4,0},{8,12},{12,8},{16,20},{20,16},{24,28},{28,24},{1,5},{5... | collective-permute-start | bytes 294920 | tf_op jit(solution)/shard_map/ppermute | solution.py:33
  27.2 1.6 %collective-permute-start.10 = (bf16[2,128,512]{2,1,0:T(8,128)(2,1)S(1)}, bf16[2,128,512]{2,1,0:T(8,128)(2,1)S(1)}, u32[]{:S(2)}, u32[]{:S(2)}) collective-permute-start(bf16[2,128,512]{2,1,0:T(8,128)(2,1)S(1)} %get-tuple-element.60), channel_id=1, source_target_pairs={{0,1},{1,0},{2,3},{3,2},{4,5},{5,4},{6,7},{7,6},{8,9},{9,8},{10,11... | collective-permute-start | bytes 786440 | tf_op jit(solution)/shard_map/ppermute | solution.py:28
  28.9 8.4 %collective-permute-start.11 = (bf16[2,128,512]{2,1,0:T(8,128)(2,1)S(1)}, bf16[2,128,512]{2,1,0:T(8,128)(2,1)S(1)}, u32[]{:S(2)}, u32[]{:S(2)}) collective-permute-start(bf16[2,128,512]{2,1,0:T(8,128)(2,1)S(1)} %get-tuple-element.116), channel_id=1, source_target_pairs={{0,2},{1,3},{2,0},{3,1},{4,6},{5,7},{6,4},{7,5},{8,10},{9,11},{10,... | collective-permute-start | bytes 786440 | tf_op jit(solution)/shard_map/ppermute | solution.py:28
  35.1 2.6 %collective-permute-start.13 = (bf16[2,128,1024]{2,1,0:T(8,128)(2,1)S(1)}, bf16[2,128,1024]{2,1,0:T(8,128)(2,1)S(1)}, u32[]{:S(2)}, u32[]{:S(2)}) collective-permute-start(bf16[2,128,1024]{2,1,0:T(8,128)(2,1)S(1)} %get-tuple-element.67), channel_id=1, source_target_pairs={{0,1},{1,0},{2,3},{3,2},{4,5},{5,4},{6,7},{7,6},{8,9},{9,8},{10,11... | collective-permute-start | bytes 1572872 | tf_op jit(solution)/shard_map/ppermute | solution.py:28
  37.6 7.1 %collective-permute-start.12 = (bf16[2,128,512]{2,1,0:T(8,128)(2,1)S(1)}, bf16[2,128,512]{2,1,0:T(8,128)(2,1)S(1)}, u32[]{:S(2)}, u32[]{:S(2)}) collective-permute-start(bf16[2,128,512]{2,1,0:T(8,128)(2,1)S(1)} %pad_maximum_fusion.9), channel_id=1, source_target_pairs={{0,1},{1,0},{2,3},{3,2},{4,5},{5,4},{6,7},{7,6},{8,9},{9,8},{10,11... | collective-permute-start | bytes 786440 | tf_op jit(solution)/shard_map/ppermute | solution.py:28
  38.0 14.4 %collective-permute-start.14 = (bf16[2,128,1024]{2,1,0:T(8,128)(2,1)S(1)}, bf16[2,128,1024]{2,1,0:T(8,128)(2,1)S(1)}, u32[]{:S(2)}, u32[]{:S(2)}) collective-permute-start(bf16[2,128,1024]{2,1,0:T(8,128)(2,1)S(1)} %get-tuple-element.114), channel_id=1, source_target_pairs={{0,2},{1,3},{2,0},{3,1},{4,6},{5,7},{6,4},{7,5},{8,10},{9,11},{10,... | collective-permute-start | bytes 1572872 | tf_op jit(solution)/shard_map/ppermute | solution.py:28
  44.4 8.0 %collective-permute-start.15 = (bf16[2,128,1024]{2,1,0:T(8,128)(2,1)S(1)}, bf16[2,128,1024]{2,1,0:T(8,128)(2,1)S(1)}, u32[]{:S(2)}, u32[]{:S(2)}) collective-permute-start(bf16[2,128,1024]{2,1,0:T(8,128)(2,1)S(1)} %get-tuple-element.74), channel_id=1, source_target_pairs={{0,1},{1,0},{2,3},{3,2},{4,5},{5,4},{6,7},{7,6},{8,9},{9,8},{10,11... | collective-permute-start | bytes 1572872 | tf_op jit(solution)/shard_map/ppermute | solution.py:28
  52.6 14.9 %collective-permute-start.18 = (bf16[2,128,1024]{2,1,0:T(8,128)(2,1)S(1)}, bf16[2,128,1024]{2,1,0:T(8,128)(2,1)S(1)}, u32[]{:S(2)}, u32[]{:S(2)}) collective-permute-start(bf16[2,128,1024]{2,1,0:T(8,128)(2,1)S(1)} %get-tuple-element.112), channel_id=1, source_target_pairs={{0,2},{1,3},{2,0},{3,1},{4,6},{5,7},{6,4},{7,5},{8,10},{9,11},{10,... | collective-permute-start | bytes 1572872 | tf_op jit(solution)/shard_map/ppermute | solution.py:28
  57.1 1.6 %collective-permute-start.16 = (bf16[2,128,512]{2,1,0:T(8,128)(2,1)S(1)}, bf16[2,128,512]{2,1,0:T(8,128)(2,1)S(1)}, u32[]{:S(2)}, u32[]{:S(2)}) collective-permute-start(bf16[2,128,512]{2,1,0:T(8,128)(2,1)S(1)} %get-tuple-element.80), channel_id=1, source_target_pairs={{0,1},{1,0},{2,3},{3,2},{4,5},{5,4},{6,7},{7,6},{8,9},{9,8},{10,11... | collective-permute-start | bytes 786440 | tf_op jit(solution)/shard_map/ppermute | solution.py:28
  58.7 13.7 %collective-permute-start.20 = (bf16[2,128,512]{2,1,0:T(8,128)(2,1)S(1)}, bf16[2,128,512]{2,1,0:T(8,128)(2,1)S(1)}, u32[]{:S(2)}, u32[]{:S(2)}) collective-permute-start(bf16[2,128,512]{2,1,0:T(8,128)(2,1)S(1)} %get-tuple-element.110), channel_id=1, source_target_pairs={{0,2},{1,3},{2,0},{3,1},{4,6},{5,7},{6,4},{7,5},{8,10},{9,11},{10,... | collective-permute-start | bytes 786440 | tf_op jit(solution)/shard_map/ppermute | solution.py:28
  59.7 8.4 %collective-permute-start.17 = (bf16[2,128,1024]{2,1,0:T(8,128)(2,1)S(1)}, bf16[2,128,1024]{2,1,0:T(8,128)(2,1)S(1)}, u32[]{:S(2)}, u32[]{:S(2)}) collective-permute-start(bf16[2,128,1024]{2,1,0:T(8,128)(2,1)S(1)} %pad_maximum_fusion.4), channel_id=1, source_target_pairs={{0,1},{1,0},{2,3},{3,2},{4,5},{5,4},{6,7},{7,6},{8,9},{9,8},{10,11... | collective-permute-start | bytes 1572872 | tf_op jit(solution)/shard_map/ppermute | solution.py:28
  68.0 3.2 %collective-permute-start.19 = (bf16[2,128,1024]{2,1,0:T(8,128)(2,1)S(1)}, bf16[2,128,1024]{2,1,0:T(8,128)(2,1)S(1)}, u32[]{:S(2)}, u32[]{:S(2)}) collective-permute-start(bf16[2,128,1024]{2,1,0:T(8,128)(2,1)S(1)} %pad_maximum_fusion.5), channel_id=1, source_target_pairs={{0,1},{1,0},{2,3},{3,2},{4,5},{5,4},{6,7},{7,6},{8,9},{9,8},{10,11... | collective-permute-start | bytes 1572872 | tf_op jit(solution)/shard_map/ppermute | solution.py:28
  72.7 1.7 %collective-permute-start.21 = (bf16[2,128,512]{2,1,0:T(8,128)(2,1)S(1)}, bf16[2,128,512]{2,1,0:T(8,128)(2,1)S(1)}, u32[]{:S(2)}, u32[]{:S(2)}) collective-permute-start(bf16[2,128,512]{2,1,0:T(8,128)(2,1)S(1)} %pad_maximum_fusion.10), channel_id=1, source_target_pairs={{0,1},{1,0},{2,3},{3,2},{4,5},{5,4},{6,7},{7,6},{8,9},{9,8},{10,11... | collective-permute-start | bytes 786440 | tf_op jit(solution)/shard_map/ppermute | solution.py:28
  77.3 7.8 %collective-permute-start.22 = (bf16[64,1536]{1,0:T(8,128)(2,1)S(1)}, bf16[64,1536]{1,0:T(8,128)(2,1)S(1)}, u32[]{:S(2)}, u32[]{:S(2)}) collective-permute-start(bf16[64,1536]{1,0:T(8,128)(2,1)S(1)} %pad_maximum_fusion.13), channel_id=1, source_target_pairs={{0,4},{4,0},{8,12},{12,8},{16,20},{20,16},{24,28},{28,24},{1,5},{5... | collective-permute-start | bytes 589832 | tf_op jit(solution)/shard_map/ppermute | solution.py:33
  78.7 10.6 %collective-permute-start.23 = (bf16[64,1536]{1,0:T(8,128)(2,1)S(1)}, bf16[64,1536]{1,0:T(8,128)(2,1)S(1)}, u32[]{:S(2)}, u32[]{:S(2)}) collective-permute-start(bf16[64,1536]{1,0:T(8,128)(2,1)S(1)} %pad_maximum_fusion.14), channel_id=1, source_target_pairs={{0,4},{4,0},{8,12},{12,8},{16,20},{20,16},{24,28},{28,24},{1,5},{5... | collective-permute-start | bytes 589832 | tf_op jit(solution)/shard_map/ppermute | solution.py:33
  85.1 5.9 %collective-permute-start.25 = (bf16[64,1536]{1,0:T(8,128)(2,1)S(1)}, bf16[64,1536]{1,0:T(8,128)(2,1)S(1)}, u32[]{:S(2)}, u32[]{:S(2)}) collective-permute-start(bf16[64,1536]{1,0:T(8,128)(2,1)S(1)} %fusion.52), channel_id=1, source_target_pairs={{0,8},{4,12},{8,0},{12,4},{16,24},{20,28},{24,16},{28,20},{1,9},{5... | collective-permute-start | bytes 589832 | tf_op jit(solution)/shard_map/ppermute | solution.py:33
  86.0 8.8 %collective-permute-start.27 = (bf16[64,1536]{1,0:T(8,128)(2,1)S(1)}, bf16[64,1536]{1,0:T(8,128)(2,1)S(1)}, u32[]{:S(2)}, u32[]{:S(2)}) collective-permute-start(bf16[64,1536]{1,0:T(8,128)(2,1)S(1)} %get-tuple-element.88), channel_id=1, source_target_pairs={{0,4},{4,0},{8,12},{12,8},{16,20},{20,16},{24,28},{28,24},{1,5},{5... | collective-permute-start | bytes 589832 | tf_op jit(solution)/shard_map/ppermute | solution.py:33
  89.3 9.8 %collective-permute-start.24 = (bf16[64,1536]{1,0:T(8,128)(2,1)S(1)}, bf16[64,1536]{1,0:T(8,128)(2,1)S(1)}, u32[]{:S(2)}, u32[]{:S(2)}) collective-permute-start(bf16[64,1536]{1,0:T(8,128)(2,1)S(1)} %get-tuple-element.86), channel_id=1, source_target_pairs={{0,4},{4,0},{8,12},{12,8},{16,20},{20,16},{24,28},{28,24},{1,5},{5... | collective-permute-start | bytes 589832 | tf_op jit(solution)/shard_map/ppermute | solution.py:33
  91.1 13.1 %collective-permute-start.26 = (bf16[64,1536]{1,0:T(8,128)(2,1)S(1)}, bf16[64,1536]{1,0:T(8,128)(2,1)S(1)}, u32[]{:S(2)}, u32[]{:S(2)}) collective-permute-start(bf16[64,1536]{1,0:T(8,128)(2,1)S(1)} %fusion.51), channel_id=1, source_target_pairs={{0,16},{4,20},{8,24},{12,28},{16,0},{20,4},{24,8},{28,12},{1,17},{... | collective-permute-start | bytes 589832 | tf_op jit(solution)/shard_map/ppermute | solution.py:33
  94.9 9.3 %collective-permute-start.28 = (bf16[64,1536]{1,0:T(8,128)(2,1)S(1)}, bf16[64,1536]{1,0:T(8,128)(2,1)S(1)}, u32[]{:S(2)}, u32[]{:S(2)}) collective-permute-start(bf16[64,1536]{1,0:T(8,128)(2,1)S(1)} %fusion.53.refs_0_), channel_id=1, source_target_pairs={{0,8},{4,12},{8,0},{12,4},{16,24},{20,28},{24,16},{28,20},{1,9},{5... | collective-permute-start | bytes 589832 | tf_op jit(solution)/shard_map/ppermute | solution.py:33
  104.5 3.4 %collective-permute-start.31 = (f32[32,128]{1,0:T(8,128)S(1)}, f32[32,128]{1,0:T(8,128)S(1)}, u32[]{:S(2)}, u32[]{:S(2)}) collective-permute-start(f32[32,128]{1,0:T(8,128)S(1)} %get-tuple-element.92.refs_0_), channel_id=1, source_target_pairs={{0,3},{1,2},{2,1},{3,0},{4,7},{5,6},{6,5},{7,4},{8,11},{9,10},{10,... | collective-permute-start | bytes 49160 | tf_op jit(solution)/shard_map/ppermute | solution.py:28
  104.6 3.8 %collective-permute-start.30 = (f32[32,128]{1,0:T(8,128)S(1)}, f32[32,128]{1,0:T(8,128)S(1)}, u32[]{:S(2)}, u32[]{:S(2)}) collective-permute-start(f32[32,128]{1,0:T(8,128)S(1)} %get-tuple-element.92.refs_0_), channel_id=1, source_target_pairs={{0,2},{1,3},{2,0},{3,1},{4,6},{5,7},{6,4},{7,5},{8,10},{9,11},{10,... | collective-permute-start | bytes 49160 | tf_op jit(solution)/shard_map/ppermute | solution.py:28
  106.1 2.3 %collective-permute-start.29 = (f32[32,128]{1,0:T(8,128)S(1)}, f32[32,128]{1,0:T(8,128)S(1)}, u32[]{:S(2)}, u32[]{:S(2)}) collective-permute-start(f32[32,128]{1,0:T(8,128)S(1)} %get-tuple-element.92.refs_0_), channel_id=1, source_target_pairs={{0,1},{1,0},{2,3},{3,2},{4,5},{5,4},{6,7},{7,6},{8,9},{9,8},{10,11... | collective-permute-start | bytes 49160 | tf_op jit(solution)/shard_map/ppermute | solution.py:28
  109.2 7.3 %collective-permute-start.35 = (bf16[32,1536]{1,0:T(8,128)(2,1)S(1)}, bf16[32,1536]{1,0:T(8,128)(2,1)S(1)}, u32[]{:S(2)}, u32[]{:S(2)}) collective-permute-start(bf16[32,1536]{1,0:T(8,128)(2,1)S(1)} %cotangent_kernel.1), channel_id=1, source_target_pairs={{0,16},{4,20},{8,24},{12,28},{16,0},{20,4},{24,8},{28,12},{1,17},{... | collective-permute-start | bytes 294920 | tf_op jit(solution)/shard_map/ppermute | solution.py:33
  109.3 8.5 %collective-permute-start.33 = (bf16[32,1536]{1,0:T(8,128)(2,1)S(1)}, bf16[32,1536]{1,0:T(8,128)(2,1)S(1)}, u32[]{:S(2)}, u32[]{:S(2)}) collective-permute-start(bf16[32,1536]{1,0:T(8,128)(2,1)S(1)} %cotangent_kernel.1), channel_id=1, source_target_pairs={{0,8},{4,12},{8,0},{12,4},{16,24},{20,28},{24,16},{28,20},{1,9},{5... | collective-permute-start | bytes 294920 | tf_op jit(solution)/shard_map/ppermute | solution.py:33
  111.1 7.4 %collective-permute-start.32 = (bf16[32,1536]{1,0:T(8,128)(2,1)S(1)}, bf16[32,1536]{1,0:T(8,128)(2,1)S(1)}, u32[]{:S(2)}, u32[]{:S(2)}) collective-permute-start(bf16[32,1536]{1,0:T(8,128)(2,1)S(1)} %cotangent_kernel.1), channel_id=1, source_target_pairs={{0,4},{4,0},{8,12},{12,8},{16,20},{20,16},{24,28},{28,24},{1,5},{5... | collective-permute-start | bytes 294920 | tf_op jit(solution)/shard_map/ppermute | solution.py:33
  116.5 4.8 %collective-permute-start.37 = (bf16[32,1536]{1,0:T(8,128)(2,1)S(1)}, bf16[32,1536]{1,0:T(8,128)(2,1)S(1)}, u32[]{:S(2)}, u32[]{:S(2)}) collective-permute-start(bf16[32,1536]{1,0:T(8,128)(2,1)S(1)} %collective-permute-done.35), channel_id=1, source_target_pairs={{0,8},{4,12},{8,0},{12,4},{16,24},{20,28},{24,16},{28,20},{1,9},{5... | collective-permute-start | bytes 294920 | tf_op jit(solution)/shard_map/ppermute | solution.py:33
  116.5 7.1 %collective-permute-start.36 = (bf16[32,1536]{1,0:T(8,128)(2,1)S(1)}, bf16[32,1536]{1,0:T(8,128)(2,1)S(1)}, u32[]{:S(2)}, u32[]{:S(2)}) collective-permute-start(bf16[32,1536]{1,0:T(8,128)(2,1)S(1)} %collective-permute-done.35), channel_id=1, source_target_pairs={{0,4},{4,0},{8,12},{12,8},{16,20},{20,16},{24,28},{28,24},{1,5},{5... | collective-permute-start | bytes 294920 | tf_op jit(solution)/shard_map/ppermute | solution.py:33
  117.7 5.9 %collective-permute-start.34 = (bf16[32,1536]{1,0:T(8,128)(2,1)S(1)}, bf16[32,1536]{1,0:T(8,128)(2,1)S(1)}, u32[]{:S(2)}, u32[]{:S(2)}) collective-permute-start(bf16[32,1536]{1,0:T(8,128)(2,1)S(1)} %collective-permute-done.33), channel_id=1, source_target_pairs={{0,4},{4,0},{8,12},{12,8},{16,20},{20,16},{24,28},{28,24},{1,5},{5... | collective-permute-start | bytes 294920 | tf_op jit(solution)/shard_map/ppermute | solution.py:33
  121.2 4.6 %collective-permute-start.38 = (bf16[32,1536]{1,0:T(8,128)(2,1)S(1)}, bf16[32,1536]{1,0:T(8,128)(2,1)S(1)}, u32[]{:S(2)}, u32[]{:S(2)}) collective-permute-start(bf16[32,1536]{1,0:T(8,128)(2,1)S(1)} %collective-permute-done.37), channel_id=1, source_target_pairs={{0,4},{4,0},{8,12},{12,8},{16,20},{20,16},{24,28},{28,24},{1,5},{5... | collective-permute-start | bytes 294920 | tf_op jit(solution)/shard_map/ppermute | solution.py:33
  127.4 1.8 %collective-permute-start.39 = (bf16[128,1536]{1,0:T(8,128)(2,1)S(1)}, bf16[128,1536]{1,0:T(8,128)(2,1)S(1)}, u32[]{:S(2)}, u32[]{:S(2)}) collective-permute-start(bf16[128,1536]{1,0:T(8,128)(2,1)S(1)} %get-tuple-element.97), channel_id=1, source_target_pairs={{0,1},{1,0},{2,3},{3,2},{4,5},{5,4},{6,7},{7,6},{8,9},{9,8},{10,11... | collective-permute-start | bytes 1179656 | tf_op jit(solution)/shard_map/ppermute | solution.py:28
  128.5 1.9 %collective-permute-start.43 = (bf16[128,1024]{1,0:T(8,128)(2,1)S(1)}, bf16[128,1024]{1,0:T(8,128)(2,1)S(1)}, u32[]{:S(2)}, u32[]{:S(2)}) collective-permute-start(bf16[128,1024]{1,0:T(8,128)(2,1)S(1)} %get-tuple-element.100), channel_id=1, source_target_pairs={{0,1},{1,0},{2,3},{3,2},{4,5},{5,4},{6,7},{7,6},{8,9},{9,8},{10,11... | collective-permute-start | bytes 786440 | tf_op jit(solution)/shard_map/ppermute | solution.py:28
  129.3 12.0 %collective-permute-start.42 = (bf16[128,1536]{1,0:T(8,128)(2,1)S(1)}, bf16[128,1536]{1,0:T(8,128)(2,1)S(1)}, u32[]{:S(2)}, u32[]{:S(2)}) collective-permute-start(bf16[128,1536]{1,0:T(8,128)(2,1)S(1)} %get-tuple-element.106), channel_id=1, source_target_pairs={{0,2},{1,3},{2,0},{3,1},{4,6},{5,7},{6,4},{7,5},{8,10},{9,11},{10,... | collective-permute-start | bytes 1179656 | tf_op jit(solution)/shard_map/ppermute | solution.py:28
  130.4 1.8 %collective-permute-start.40 = (bf16[128,512]{1,0:T(8,128)(2,1)S(1)}, bf16[128,512]{1,0:T(8,128)(2,1)S(1)}, u32[]{:S(2)}, u32[]{:S(2)}) collective-permute-start(bf16[128,512]{1,0:T(8,128)(2,1)S(1)} %get-tuple-element.99), channel_id=1, source_target_pairs={{0,1},{1,0},{2,3},{3,2},{4,5},{5,4},{6,7},{7,6},{8,9},{9,8},{10,11... | collective-permute-start | bytes 393224 | tf_op jit(solution)/shard_map/ppermute | solution.py:28
  130.6 16.3 %collective-permute-start.46 = (bf16[128,1024]{1,0:T(8,128)(2,1)S(1)}, bf16[128,1024]{1,0:T(8,128)(2,1)S(1)}, u32[]{:S(2)}, u32[]{:S(2)}) collective-permute-start(bf16[128,1024]{1,0:T(8,128)(2,1)S(1)} %get-tuple-element.104), channel_id=1, source_target_pairs={{0,2},{1,3},{2,0},{3,1},{4,6},{5,7},{6,4},{7,5},{8,10},{9,11},{10,... | collective-permute-start | bytes 786440 | tf_op jit(solution)/shard_map/ppermute | solution.py:28
  141.4 5.8 %collective-permute-start.44 = (bf16[128,1536]{1,0:T(8,128)(2,1)S(1)}, bf16[128,1536]{1,0:T(8,128)(2,1)S(1)}, u32[]{:S(2)}, u32[]{:S(2)}) collective-permute-start(bf16[128,1536]{1,0:T(8,128)(2,1)S(1)} %multiply_convert_fusion), channel_id=1, source_target_pairs={{0,1},{1,0},{2,3},{3,2},{4,5},{5,4},{6,7},{7,6},{8,9},{9,8},{10,11... | collective-permute-start | bytes 1179656 | tf_op jit(solution)/shard_map/ppermute | solution.py:28
  141.5 10.2 %collective-permute-start.41 = (bf16[128,512]{1,0:T(8,128)(2,1)S(1)}, bf16[128,512]{1,0:T(8,128)(2,1)S(1)}, u32[]{:S(2)}, u32[]{:S(2)}) collective-permute-start(bf16[128,512]{1,0:T(8,128)(2,1)S(1)} %get-tuple-element.108), channel_id=1, source_target_pairs={{0,2},{1,3},{2,0},{3,1},{4,6},{5,7},{6,4},{7,5},{8,10},{9,11},{10,... | collective-permute-start | bytes 393224 | tf_op jit(solution)/shard_map/ppermute | solution.py:28
  147.2 5.2 %collective-permute-start.47 = (bf16[128,1024]{1,0:T(8,128)(2,1)S(1)}, bf16[128,1024]{1,0:T(8,128)(2,1)S(1)}, u32[]{:S(2)}, u32[]{:S(2)}) collective-permute-start(bf16[128,1024]{1,0:T(8,128)(2,1)S(1)} %multiply_convert_fusion.1), channel_id=1, source_target_pairs={{0,1},{1,0},{2,3},{3,2},{4,5},{5,4},{6,7},{7,6},{8,9},{9,8},{10,11... | collective-permute-start | bytes 786440 | tf_op jit(solution)/shard_map/ppermute | solution.py:28
  151.8 3.6 %collective-permute-start.45 = (bf16[128,512]{1,0:T(8,128)(2,1)S(1)}, bf16[128,512]{1,0:T(8,128)(2,1)S(1)}, u32[]{:S(2)}, u32[]{:S(2)}) collective-permute-start(bf16[128,512]{1,0:T(8,128)(2,1)S(1)} %multiply_convert_fusion.4), channel_id=1, source_target_pairs={{0,1},{1,0},{2,3},{3,2},{4,5},{5,4},{6,7},{7,6},{8,9},{9,8},{10,11... | collective-permute-start | bytes 393224 | tf_op jit(solution)/shard_map/ppermute | solution.py:28
  (10 other events, 42.6 us)

commit v3 on v2

--- a/solution.py
+++ b/solution.py
@@ -410,8 +410,8 @@
 
 
 def chunks_of(units):
-    part = units // 6
-    sizes = [part, 2 * part, 2 * part, part] if part % TILE == 0 else [units]
+    part = units // 12
+    sizes = [2 * part, 3 * part, 4 * part, 3 * part] if part % TILE == 0 else [units]
     return [sum(sizes[:k]) for k in range(len(sizes))], sizes
 
 

time: 158 us -> 158 us (level)
  starting transfers between devices: 41.2 us -> 42.8 us
    ppermute x21, waiting for transfers between devices: 29.5 us -> 26.8 us  [swap_dp(): return lax.ppermute(value, 'dp', [(i, i ^ flip) for i in range(size)])]
    ppermute x27, waiting for transfers between devices: 26.7 us -> 29.2 us  [swap_tensor(): return lax.ppermute(value, 'tensor', [(t, t ^ flip) for t in range(size)])]
  transfers between devices with their start and end apart: 48 -> 48, of which waited for: 23 -> 22; matrix products, arithmetic and copies ran while one was open for 8% -> 7% of each run, Pallas kernels for 22% -> 21%
where the time goes in v3:
time: 158 us
  waiting for transfers between devices  56 us (35%)
  starting transfers between devices  42.8 us (27%)
  Pallas kernels  39.8 us (25%)
  matrix products  9.64 us (6%)
  local copies, waits for them, and re-layouts  4.08 us (3%)
  other arithmetic  3.46 us (2%)
  between operations  1.87 us (1%)
    ppermute x27, waiting for transfers between devices, swap_tensor(): return lax.ppermute(value, 'tensor', [(t, t ^ flip) for t in range(size)])  29.2 us
    ppermute x21, starting transfers between devices, swap_dp(): return lax.ppermute(value, 'dp', [(i, i ^ flip) for i in range(size)])  27.1 us
    ppermute x21, waiting for transfers between devices, swap_dp(): return lax.ppermute(value, 'dp', [(i, i ^ flip) for i in range(size)])  26.8 us
    ppermute x27, starting transfers between devices, swap_tensor(): return lax.ppermute(value, 'tensor', [(t, t ^ flip) for t in range(size)])  15.7 us
    pallas_call x4, Pallas kernels, load_columns(): pl.pallas_call(functools.partial(load_kernel, start, len(arrays)), in_spe...  9.79 us
    pallas_call x3, Pallas kernels, outer_columns(): pl.pallas_call(functools.partial(columns_kernel, column), in_specs=[vmem,...  9.21 us
    pallas_call x1, Pallas kernels, outer_rows(): pl.pallas_call(functools.partial(rows_kernel, len(lefts)), in_specs=[vmem...  6.92 us
    pallas_call x4, Pallas kernels, up_parts(): pl.pallas_call(up_kernel, out_shape=out_shape, compiler_params=PARAMS, co...  5.54 us
  transfers between devices with their start and end apart: 48, of which 22 were waited for; matrix products, arithmetic and copies ran while one was open for 7% of the time, Pallas kernels for 21%

profile of v3, /device:TPU:0, one launch (start us, length us, event | category | flops | bytes accessed | tf_op | source)
XLA Modules:
  0.0 157.6 jit_solution(10826581860766089158)
XLA Ops:
  1.7 2.4 %collective-permute-start.2 = (f32[32,128]{1,0:T(8,128)S(1)}, f32[32,128]{1,0:T(8,128)S(1)}, u32[]{:S(2)}, u32[]{:S(2)}) collective-permute-start(f32[32,128]{1,0:T(8,128)S(1)} %get-tuple-element.54.refs_0_), channel_id=1, source_target_pairs={{0,3},{1,2},{2,1},{3,0},{4,7},{5,6},{6,5},{7,4},{8,11},{9,10},{10,... | collective-permute-start | bytes 49160 | tf_op jit(solution)/shard_map/ppermute | solution.py:28
  6.2 1.7 %collective-permute-done.1.refs_2_ = f32[32,128]{1,0:T(8,128)S(1)} collective-permute-done((f32[32,128]{1,0:T(8,128)S(1)}, f32[32,128]{1,0:T(8,128)S(1)}, u32[]{:S(2)}, u32[]{:S(2)}) %collective-permute-start.1) | collective-permute-done | bytes 16416 | tf_op jit(solution)/shard_map/ppermute | solution.py:28
  8.1 2.7 %collective-permute-start.6 = (bf16[32,1536]{1,0:T(8,128)(2,1)S(1)}, bf16[32,1536]{1,0:T(8,128)(2,1)S(1)}, u32[]{:S(2)}, u32[]{:S(2)}) collective-permute-start(bf16[32,1536]{1,0:T(8,128)(2,1)S(1)} %norm_in_kernel.1), channel_id=1, source_target_pairs={{0,16},{4,20},{8,24},{12,28},{16,0},{20,4},{24,8},{28,12},{1,17},{... | collective-permute-start | bytes 294920 | tf_op jit(solution)/shard_map/ppermute | solution.py:33
  10.7 1.6 %collective-permute-start.4 = (bf16[32,1536]{1,0:T(8,128)(2,1)S(1)}, bf16[32,1536]{1,0:T(8,128)(2,1)S(1)}, u32[]{:S(2)}, u32[]{:S(2)}) collective-permute-start(bf16[32,1536]{1,0:T(8,128)(2,1)S(1)} %norm_in_kernel.1), channel_id=1, source_target_pairs={{0,8},{4,12},{8,0},{12,4},{16,24},{20,28},{24,16},{28,20},{1,9},{5... | collective-permute-start | bytes 294920 | tf_op jit(solution)/shard_map/ppermute | solution.py:33
  12.3 1.5 collective-permute-start.3
  13.8 1.7 %collective-permute-done.6 = bf16[32,1536]{1,0:T(8,128)(2,1)S(1)} collective-permute-done((bf16[32,1536]{1,0:T(8,128)(2,1)S(1)}, bf16[32,1536]{1,0:T(8,128)(2,1)S(1)}, u32[]{:S(2)}, u32[]{:S(2)}) %collective-permute-start.6) | collective-permute-done | bytes 98336 | tf_op jit(solution)/shard_map/ppermute | solution.py:33
  16.0 1.5 collective-permute-start.7
  18.1 2.0 %collective-permute-done.8 = bf16[32,1536]{1,0:T(8,128)(2,1)S(1)} collective-permute-done((bf16[32,1536]{1,0:T(8,128)(2,1)S(1)}, bf16[32,1536]{1,0:T(8,128)(2,1)S(1)}, u32[]{:S(2)}, u32[]{:S(2)}) %collective-permute-start.8) | collective-permute-done | bytes 98336 | tf_op jit(solution)/shard_map/ppermute | solution.py:33
  20.1 1.5 collective-permute-start.9
  21.6 1.5 collective-permute-done.5
  23.1 1.9 %load_columns.4 = (bf16[1536,512]{1,0:T(8,128)(2,1)S(1)}, bf16[1536,512]{1,0:T(8,128)(2,1)S(1)}) custom-call(bf16[1536,3072]{1,0:T(8,128)(2,1)} %refs_0_.3, bf16[1536,3072]{1,0:T(8,128)(2,1)} %refs_1_.7), custom_call_target="tpu_custom_call" | custom-call | bytes 3145 | tf_op jit(solution)/shard_map/load_columns/pallas_call | solution.py:120
  26.3 1.5 collective-permute-done.10
  27.9 1.1 collective-permute-start.11
  29.1 2.4 %load_columns.5 = (bf16[1536,768]{1,0:T(8,128)(2,1)S(1)}, bf16[1536,768]{1,0:T(8,128)(2,1)S(1)}) custom-call(bf16[1536,3072]{1,0:T(8,128)(2,1)} %refs_0_.3, bf16[1536,3072]{1,0:T(8,128)(2,1)} %refs_1_.7, f32[2,128,512]{2,1,0:T(8,128)S(1)} %get-tuple-element.117.refs_2_), custom_call_target="tpu_custom_call" | custom-call | bytes 4718 | tf_op jit(solution)/shard_map/load_columns/pallas_call | solution.py:120
  31.5 1.4 up_parts.5
  33.0 3.3 %collective-permute-done.11 = bf16[2,128,512]{2,1,0:T(8,128)(2,1)S(1)} collective-permute-done((bf16[2,128,512]{2,1,0:T(8,128)(2,1)S(1)}, bf16[2,128,512]{2,1,0:T(8,128)(2,1)S(1)}, u32[]{:S(2)}, u32[]{:S(2)}) %collective-permute-start.11) | collective-permute-done | bytes 262176 | tf_op jit(solution)/shard_map/ppermute | solution.py:28
  36.9 1.1 collective-permute-start.14
  38.0 3.0 %load_columns.6 = (bf16[1536,1024]{1,0:T(8,128)(2,1)S(1)}, bf16[1536,1024]{1,0:T(8,128)(2,1)S(1)}) custom-call(bf16[1536,3072]{1,0:T(8,128)(2,1)} %refs_0_.3, bf16[1536,3072]{1,0:T(8,128)(2,1)} %refs_1_.7, f32[2,128,768]{2,1,0:T(8,128)S(1)} %get-tuple-element.115.refs_2_), custom_call_target="tpu_custom_call" | custom-call | bytes 6291 | tf_op jit(solution)/shard_map/load_columns/pallas_call | solution.py:120
  41.1 1.8 %up_parts.6 = (f32[2,128,1024]{2,1,0:T(8,128)S(1)}, bf16[2,128,1024]{2,1,0:T(8,128)(2,1)S(1)}) custom-call(bf16[256,1536]{1,0:T(8,128)(2,1)S(1)} %constant_dynamic-update-slice_fusion.rows_ref.left_ref, bf16[1536,1024]{1,0:T(8,128)(2,1)S(1)} %get-tuple-element.70.weight_ref, bf16[1536,1024]{1,0:T(8,128)(2,1)S(1)} %get-tuple-element.71.tangent_ref), custom_call_target="tpu_custom_call" | custom-call | flops 1610612 | bytes 786 | tf_op jit(solution)/shard_map/up_parts/pallas_call | solution.py:205
  46.6 2.4 %load_columns.7 = (bf16[1536,768]{1,0:T(8,128)(2,1)S(1)}, bf16[1536,768]{1,0:T(8,128)(2,1)S(1)}) custom-call(bf16[1536,3072]{1,0:T(8,128)(2,1)} %refs_0_.3, bf16[1536,3072]{1,0:T(8,128)(2,1)} %refs_1_.7, f32[2,128,1024]{2,1,0:T(8,128)S(1)} %get-tuple-element.113.refs_2_), custom_call_target="tpu_custom_call" | custom-call | bytes 4718 | tf_op jit(solution)/shard_map/load_columns/pallas_call | solution.py:120
  49.1 1.4 up_parts.7
  51.1 1.1 collective-permute-start.18
  54.4 11.6 %collective-permute-done.18 = bf16[2,128,1024]{2,1,0:T(8,128)(2,1)S(1)} collective-permute-done((bf16[2,128,1024]{2,1,0:T(8,128)(2,1)S(1)}, bf16[2,128,1024]{2,1,0:T(8,128)(2,1)S(1)}, u32[]{:S(2)}, u32[]{:S(2)}) %collective-permute-start.18) | collective-permute-done | bytes 524320 | tf_op jit(solution)/shard_map/ppermute | solution.py:28
  70.1 3.4 %collective-permute-done.20 = bf16[2,128,768]{2,1,0:T(8,128)(2,1)S(1)} collective-permute-done((bf16[2,128,768]{2,1,0:T(8,128)(2,1)S(1)}, bf16[2,128,768]{2,1,0:T(8,128)(2,1)S(1)}, u32[]{:S(2)}, u32[]{:S(2)}) %collective-permute-start.20) | collective-permute-done | bytes 393248 | tf_op jit(solution)/shard_map/ppermute | solution.py:28
  73.9 1.2 fusion.9
  79.2 1.4 collective-permute-start.22
  81.5 5.5 %collective-permute-done.22 = bf16[64,1536]{1,0:T(8,128)(2,1)S(1)} collective-permute-done((bf16[64,1536]{1,0:T(8,128)(2,1)S(1)}, bf16[64,1536]{1,0:T(8,128)(2,1)S(1)}, u32[]{:S(2)}, u32[]{:S(2)}) %collective-permute-start.22) | collective-permute-done | bytes 196640 | tf_op jit(solution)/shard_map/ppermute | solution.py:33
  87.0 1.3 collective-permute-start.25
  88.3 1.6 collective-permute-start.27
  89.9 1.3 collective-permute-done.23
  91.2 1.3 collective-permute-start.24
  92.8 4.5 %collective-permute-start.26 = (bf16[64,1536]{1,0:T(8,128)(2,1)S(1)}, bf16[64,1536]{1,0:T(8,128)(2,1)S(1)}, u32[]{:S(2)}, u32[]{:S(2)}) collective-permute-start(bf16[64,1536]{1,0:T(8,128)(2,1)S(1)} %fusion.60), channel_id=1, source_target_pairs={{0,16},{4,20},{8,24},{12,28},{16,0},{20,4},{24,8},{28,12},{1,17},{... | collective-permute-start | bytes 589832 | tf_op jit(solution)/shard_map/ppermute | solution.py:33
  97.5 3.8 %load_rows.1.refs_4_.weight_ref = bf16[3072,1536]{1,0:T(8,128)(2,1)S(1)} custom-call(bf16[3072,1536]{1,0:T(8,128)(2,1)} %given_ref.3, bf16[64,1536]{1,0:T(8,128)(2,1)S(1)} %fusion.62.refs_0_), custom_call_target="tpu_custom_call" | custom-call | bytes 9437 | tf_op jit(solution)/shard_map/load_rows/pallas_call | solution.py:144
  101.4 4.5 %collective-permute-done.28.refs_3_ = bf16[64,1536]{1,0:T(8,128)(2,1)S(1)} collective-permute-done((bf16[64,1536]{1,0:T(8,128)(2,1)S(1)}, bf16[64,1536]{1,0:T(8,128)(2,1)S(1)}, u32[]{:S(2)}, u32[]{:S(2)}) %collective-permute-start.28) | collective-permute-done | bytes 196640 | tf_op jit(solution)/shard_map/ppermute | solution.py:33
  108.1 1.3 collective-permute-done.31.refs_3_
  111.1 1.6 collective-permute-start.33
  112.7 1.7 %collective-permute-start.32 = (bf16[32,1536]{1,0:T(8,128)(2,1)S(1)}, bf16[32,1536]{1,0:T(8,128)(2,1)S(1)}, u32[]{:S(2)}, u32[]{:S(2)}) collective-permute-start(bf16[32,1536]{1,0:T(8,128)(2,1)S(1)} %cotangent_kernel.1), channel_id=1, source_target_pairs={{0,4},{4,0},{8,12},{12,8},{16,20},{20,16},{24,28},{28,24},{1,5},{5... | collective-permute-start | bytes 294920 | tf_op jit(solution)/shard_map/ppermute | solution.py:33
  114.4 3.9 %collective-permute-done.35 = bf16[32,1536]{1,0:T(8,128)(2,1)S(1)} collective-permute-done((bf16[32,1536]{1,0:T(8,128)(2,1)S(1)}, bf16[32,1536]{1,0:T(8,128)(2,1)S(1)}, u32[]{:S(2)}, u32[]{:S(2)}) %collective-permute-start.35) | collective-permute-done | bytes 98336 | tf_op jit(solution)/shard_map/ppermute | solution.py:33
  120.3 2.7 %collective-permute-done.37 = bf16[32,1536]{1,0:T(8,128)(2,1)S(1)} collective-permute-done((bf16[32,1536]{1,0:T(8,128)(2,1)S(1)}, bf16[32,1536]{1,0:T(8,128)(2,1)S(1)}, u32[]{:S(2)}, u32[]{:S(2)}) %collective-permute-start.37) | collective-permute-done | bytes 98336 | tf_op jit(solution)/shard_map/ppermute | solution.py:33
  124.0 1.3 collective-permute-done.34
  125.4 2.2 %collective-permute-done.38 = bf16[32,1536]{1,0:T(8,128)(2,1)S(1)} collective-permute-done((bf16[32,1536]{1,0:T(8,128)(2,1)S(1)}, bf16[32,1536]{1,0:T(8,128)(2,1)S(1)}, u32[]{:S(2)}, u32[]{:S(2)}) %collective-permute-start.38) | collective-permute-done | bytes 98336 | tf_op jit(solution)/shard_map/ppermute | solution.py:33
  127.7 1.2 back_parts.3
  132.5 1.3 collective-permute-start.46
  133.9 6.9 %outer_rows.1 = f32[3072,1536]{1,0:T(8,128)} custom-call(bf16[256,512]{1,0:T(8,128)(2,1)S(1)} %slice_bitcast_fusion.11.refs_0_, bf16[256,768]{1,0:T(8,128)(2,1)S(1)} %slice_bitcast_fusion.8.refs_1_, bf16[256,1024]{1,0:T(8,128)(2,1)S(1)} %slice_bitcast_fusion.2.refs_2_, bf16[256,768]{1,0:T(8,128)(2,1)S(1)} %slice_bitcast_fusion.5.refs_3_, ...), custom_call_target="tpu_custom_call" | custom-call | flops 2415919 | bytes 19660 | tf_op jit(solution)/shard_map/outer_rows/pallas_call | solution.py:275
  142.4 4.5 %collective-permute-done.46 = bf16[128,1024]{1,0:T(8,128)(2,1)S(1)} collective-permute-done((bf16[128,1024]{1,0:T(8,128)(2,1)S(1)}, bf16[128,1024]{1,0:T(8,128)(2,1)S(1)}, u32[]{:S(2)}, u32[]{:S(2)}) %collective-permute-start.46) | collective-permute-done | bytes 262176 | tf_op jit(solution)/shard_map/ppermute | solution.py:28
  147.3 3.6 %outer_columns.3.refs_0_ = f32[1536,3072]{1,0:T(8,128)} custom-call(bf16[256,1536]{1,0:T(8,128)(2,1)S(1)} %constant_dynamic-update-slice_fusion.rows_ref.left_ref, bf16[256,1280]{1,0:T(8,128)(2,1)S(1)} %pad_maximum_fusion.3.right_ref), custom_call_target="tpu_custom_call" | custom-call | flops 1006632 | bytes 9306 | tf_op jit(solution)/shard_map/outer_columns/pallas_call | solution.py:236
  151.8 3.0 %outer_columns.4.refs_0_ = f32[1536,3072]{1,0:T(8,128)} custom-call(bf16[256,1536]{1,0:T(8,128)(2,1)S(1)} %constant_dynamic-update-slice_fusion.rows_ref.left_ref, bf16[256,1024]{1,0:T(8,128)(2,1)S(1)} %pad_maximum_fusion.6.right_ref, f32[1536,3072]{1,0:T(8,128)} %outer_columns.3.refs_0_), custom_call_target="tpu_custom_call", output_to_operand_aliasing={{}: (2, {})} | custom-call | flops 805306 | bytes 7602 | tf_op jit(solution)/shard_map/outer_columns/pallas_call | solution.py:236
  154.9 2.6 %outer_columns.5 = f32[1536,3072]{1,0:T(8,128)} custom-call(bf16[256,1536]{1,0:T(8,128)(2,1)S(1)} %constant_dynamic-update-slice_fusion.rows_ref.left_ref, bf16[256,768]{1,0:T(8,128)(2,1)S(1)} %pad_maximum_fusion.10.right_ref, f32[1536,3072]{1,0:T(8,128)} %outer_columns.4.refs_0_), custom_call_target="tpu_custom_call", output_to_operand_aliasing={{}: (2, {})} | custom-call | flops 603979 | bytes 5898 | tf_op jit(solution)/shard_map/outer_columns/pallas_call | solution.py:236
  (187 shorter events, 36.2 us)
Async XLA Ops:
  1.7 4.5 %collective-permute-start.2 = (f32[32,128]{1,0:T(8,128)S(1)}, f32[32,128]{1,0:T(8,128)S(1)}, u32[]{:S(2)}, u32[]{:S(2)}) collective-permute-start(f32[32,128]{1,0:T(8,128)S(1)} %get-tuple-element.54.refs_0_), channel_id=1, source_target_pairs={{0,3},{1,2},{2,1},{3,0},{4,7},{5,6},{6,5},{7,4},{8,11},{9,10},{10,... | collective-permute-start | bytes 49160 | tf_op jit(solution)/shard_map/ppermute | solution.py:28
  4.1 3.7 %collective-permute-start.1 = (f32[32,128]{1,0:T(8,128)S(1)}, f32[32,128]{1,0:T(8,128)S(1)}, u32[]{:S(2)}, u32[]{:S(2)}) collective-permute-start(f32[32,128]{1,0:T(8,128)S(1)} %get-tuple-element.54.refs_0_), channel_id=1, source_target_pairs={{0,2},{1,3},{2,0},{3,1},{4,6},{5,7},{6,4},{7,5},{8,10},{9,11},{10,... | collective-permute-start | bytes 49160 | tf_op jit(solution)/shard_map/ppermute | solution.py:28
  4.8 3.1 %collective-permute-start = (f32[32,128]{1,0:T(8,128)S(1)}, f32[32,128]{1,0:T(8,128)S(1)}, u32[]{:S(2)}, u32[]{:S(2)}) collective-permute-start(f32[32,128]{1,0:T(8,128)S(1)} %get-tuple-element.54.refs_0_), channel_id=1, source_target_pairs={{0,1},{1,0},{2,3},{3,2},{4,5},{5,4},{6,7},{7,6},{8,9},{9,8},{10,11... | collective-permute-start | bytes 49160 | tf_op jit(solution)/shard_map/ppermute | solution.py:28
  8.1 7.4 %collective-permute-start.6 = (bf16[32,1536]{1,0:T(8,128)(2,1)S(1)}, bf16[32,1536]{1,0:T(8,128)(2,1)S(1)}, u32[]{:S(2)}, u32[]{:S(2)}) collective-permute-start(bf16[32,1536]{1,0:T(8,128)(2,1)S(1)} %norm_in_kernel.1), channel_id=1, source_target_pairs={{0,16},{4,20},{8,24},{12,28},{16,0},{20,4},{24,8},{28,12},{1,17},{... | collective-permute-start | bytes 294920 | tf_op jit(solution)/shard_map/ppermute | solution.py:33
  10.7 6.8 %collective-permute-start.4 = (bf16[32,1536]{1,0:T(8,128)(2,1)S(1)}, bf16[32,1536]{1,0:T(8,128)(2,1)S(1)}, u32[]{:S(2)}, u32[]{:S(2)}) collective-permute-start(bf16[32,1536]{1,0:T(8,128)(2,1)S(1)} %norm_in_kernel.1), channel_id=1, source_target_pairs={{0,8},{4,12},{8,0},{12,4},{16,24},{20,28},{24,16},{28,20},{1,9},{5... | collective-permute-start | bytes 294920 | tf_op jit(solution)/shard_map/ppermute | solution.py:33
  12.3 5.8 %collective-permute-start.3 = (bf16[32,1536]{1,0:T(8,128)(2,1)S(1)}, bf16[32,1536]{1,0:T(8,128)(2,1)S(1)}, u32[]{:S(2)}, u32[]{:S(2)}) collective-permute-start(bf16[32,1536]{1,0:T(8,128)(2,1)S(1)} %norm_in_kernel.1), channel_id=1, source_target_pairs={{0,4},{4,0},{8,12},{12,8},{16,20},{20,16},{24,28},{28,24},{1,5},{5... | collective-permute-start | bytes 294920 | tf_op jit(solution)/shard_map/ppermute | solution.py:33
  15.5 4.6 %collective-permute-start.8 = (bf16[32,1536]{1,0:T(8,128)(2,1)S(1)}, bf16[32,1536]{1,0:T(8,128)(2,1)S(1)}, u32[]{:S(2)}, u32[]{:S(2)}) collective-permute-start(bf16[32,1536]{1,0:T(8,128)(2,1)S(1)} %collective-permute-done.6), channel_id=1, source_target_pairs={{0,8},{4,12},{8,0},{12,4},{16,24},{20,28},{24,16},{28,20},{1,9},{5... | collective-permute-start | bytes 294920 | tf_op jit(solution)/shard_map/ppermute | solution.py:33
  16.0 7.0 %collective-permute-start.7 = (bf16[32,1536]{1,0:T(8,128)(2,1)S(1)}, bf16[32,1536]{1,0:T(8,128)(2,1)S(1)}, u32[]{:S(2)}, u32[]{:S(2)}) collective-permute-start(bf16[32,1536]{1,0:T(8,128)(2,1)S(1)} %collective-permute-done.6), channel_id=1, source_target_pairs={{0,4},{4,0},{8,12},{12,8},{16,20},{20,16},{24,28},{28,24},{1,5},{5... | collective-permute-start | bytes 294920 | tf_op jit(solution)/shard_map/ppermute | solution.py:33
  17.5 5.5 %collective-permute-start.5 = (bf16[32,1536]{1,0:T(8,128)(2,1)S(1)}, bf16[32,1536]{1,0:T(8,128)(2,1)S(1)}, u32[]{:S(2)}, u32[]{:S(2)}) collective-permute-start(bf16[32,1536]{1,0:T(8,128)(2,1)S(1)} %collective-permute-done.4), channel_id=1, source_target_pairs={{0,4},{4,0},{8,12},{12,8},{16,20},{20,16},{24,28},{28,24},{1,5},{5... | collective-permute-start | bytes 294920 | tf_op jit(solution)/shard_map/ppermute | solution.py:33
  20.1 5.0 %collective-permute-start.9 = (bf16[32,1536]{1,0:T(8,128)(2,1)S(1)}, bf16[32,1536]{1,0:T(8,128)(2,1)S(1)}, u32[]{:S(2)}, u32[]{:S(2)}) collective-permute-start(bf16[32,1536]{1,0:T(8,128)(2,1)S(1)} %collective-permute-done.8), channel_id=1, source_target_pairs={{0,4},{4,0},{8,12},{12,8},{16,20},{20,16},{24,28},{28,24},{1,5},{5... | collective-permute-start | bytes 294920 | tf_op jit(solution)/shard_map/ppermute | solution.py:33
  26.2 1.6 %collective-permute-start.10 = (bf16[2,128,512]{2,1,0:T(8,128)(2,1)S(1)}, bf16[2,128,512]{2,1,0:T(8,128)(2,1)S(1)}, u32[]{:S(2)}, u32[]{:S(2)}) collective-permute-start(bf16[2,128,512]{2,1,0:T(8,128)(2,1)S(1)} %get-tuple-element.60), channel_id=1, source_target_pairs={{0,1},{1,0},{2,3},{3,2},{4,5},{5,4},{6,7},{7,6},{8,9},{9,8},{10,11... | collective-permute-start | bytes 786440 | tf_op jit(solution)/shard_map/ppermute | solution.py:28
  27.9 8.4 %collective-permute-start.11 = (bf16[2,128,512]{2,1,0:T(8,128)(2,1)S(1)}, bf16[2,128,512]{2,1,0:T(8,128)(2,1)S(1)}, u32[]{:S(2)}, u32[]{:S(2)}) collective-permute-start(bf16[2,128,512]{2,1,0:T(8,128)(2,1)S(1)} %get-tuple-element.116), channel_id=1, source_target_pairs={{0,2},{1,3},{2,0},{3,1},{4,6},{5,7},{6,4},{7,5},{8,10},{9,11},{10,... | collective-permute-start | bytes 786440 | tf_op jit(solution)/shard_map/ppermute | solution.py:28
  32.9 3.9 %collective-permute-start.13 = (bf16[2,128,768]{2,1,0:T(8,128)(2,1)S(1)}, bf16[2,128,768]{2,1,0:T(8,128)(2,1)S(1)}, u32[]{:S(2)}, u32[]{:S(2)}) collective-permute-start(bf16[2,128,768]{2,1,0:T(8,128)(2,1)S(1)} %get-tuple-element.67), channel_id=1, source_target_pairs={{0,1},{1,0},{2,3},{3,2},{4,5},{5,4},{6,7},{7,6},{8,9},{9,8},{10,11... | collective-permute-start | bytes 1179656 | tf_op jit(solution)/shard_map/ppermute | solution.py:28
  36.6 6.8 %collective-permute-start.12 = (bf16[2,128,512]{2,1,0:T(8,128)(2,1)S(1)}, bf16[2,128,512]{2,1,0:T(8,128)(2,1)S(1)}, u32[]{:S(2)}, u32[]{:S(2)}) collective-permute-start(bf16[2,128,512]{2,1,0:T(8,128)(2,1)S(1)} %pad_maximum_fusion.11), channel_id=1, source_target_pairs={{0,1},{1,0},{2,3},{3,2},{4,5},{5,4},{6,7},{7,6},{8,9},{9,8},{10,11... | collective-permute-start | bytes 786440 | tf_op jit(solution)/shard_map/ppermute | solution.py:28
  36.9 14.1 %collective-permute-start.14 = (bf16[2,128,768]{2,1,0:T(8,128)(2,1)S(1)}, bf16[2,128,768]{2,1,0:T(8,128)(2,1)S(1)}, u32[]{:S(2)}, u32[]{:S(2)}) collective-permute-start(bf16[2,128,768]{2,1,0:T(8,128)(2,1)S(1)} %get-tuple-element.114), channel_id=1, source_target_pairs={{0,2},{1,3},{2,0},{3,1},{4,6},{5,7},{6,4},{7,5},{8,10},{9,11},{10,... | collective-permute-start | bytes 1179656 | tf_op jit(solution)/shard_map/ppermute | solution.py:28
  42.9 3.6 %collective-permute-start.15 = (bf16[2,128,1024]{2,1,0:T(8,128)(2,1)S(1)}, bf16[2,128,1024]{2,1,0:T(8,128)(2,1)S(1)}, u32[]{:S(2)}, u32[]{:S(2)}) collective-permute-start(bf16[2,128,1024]{2,1,0:T(8,128)(2,1)S(1)} %get-tuple-element.74), channel_id=1, source_target_pairs={{0,1},{1,0},{2,3},{3,2},{4,5},{5,4},{6,7},{7,6},{8,9},{9,8},{10,11... | collective-permute-start | bytes 1572872 | tf_op jit(solution)/shard_map/ppermute | solution.py:28
  50.4 1.9 %collective-permute-start.16 = (bf16[2,128,768]{2,1,0:T(8,128)(2,1)S(1)}, bf16[2,128,768]{2,1,0:T(8,128)(2,1)S(1)}, u32[]{:S(2)}, u32[]{:S(2)}) collective-permute-start(bf16[2,128,768]{2,1,0:T(8,128)(2,1)S(1)} %get-tuple-element.80), channel_id=1, source_target_pairs={{0,1},{1,0},{2,3},{3,2},{4,5},{5,4},{6,7},{7,6},{8,9},{9,8},{10,11... | collective-permute-start | bytes 1179656 | tf_op jit(solution)/shard_map/ppermute | solution.py:28
  51.1 14.9 %collective-permute-start.18 = (bf16[2,128,1024]{2,1,0:T(8,128)(2,1)S(1)}, bf16[2,128,1024]{2,1,0:T(8,128)(2,1)S(1)}, u32[]{:S(2)}, u32[]{:S(2)}) collective-permute-start(bf16[2,128,1024]{2,1,0:T(8,128)(2,1)S(1)} %get-tuple-element.112), channel_id=1, source_target_pairs={{0,2},{1,3},{2,0},{3,1},{4,6},{5,7},{6,4},{7,5},{8,10},{9,11},{10,... | collective-permute-start | bytes 1572872 | tf_op jit(solution)/shard_map/ppermute | solution.py:28
  52.7 13.9 %collective-permute-start.17 = (bf16[2,128,768]{2,1,0:T(8,128)(2,1)S(1)}, bf16[2,128,768]{2,1,0:T(8,128)(2,1)S(1)}, u32[]{:S(2)}, u32[]{:S(2)}) collective-permute-start(bf16[2,128,768]{2,1,0:T(8,128)(2,1)S(1)} %pad_maximum_fusion.7), channel_id=1, source_target_pairs={{0,1},{1,0},{2,3},{3,2},{4,5},{5,4},{6,7},{7,6},{8,9},{9,8},{10,11... | collective-permute-start | bytes 1179656 | tf_op jit(solution)/shard_map/ppermute | solution.py:28
  53.1 20.3 %collective-permute-start.20 = (bf16[2,128,768]{2,1,0:T(8,128)(2,1)S(1)}, bf16[2,128,768]{2,1,0:T(8,128)(2,1)S(1)}, u32[]{:S(2)}, u32[]{:S(2)}) collective-permute-start(bf16[2,128,768]{2,1,0:T(8,128)(2,1)S(1)} %get-tuple-element.110), channel_id=1, source_target_pairs={{0,2},{1,3},{2,0},{3,1},{4,6},{5,7},{6,4},{7,5},{8,10},{9,11},{10,... | collective-permute-start | bytes 1179656 | tf_op jit(solution)/shard_map/ppermute | solution.py:28
  66.5 2.5 %collective-permute-start.19 = (bf16[2,128,1024]{2,1,0:T(8,128)(2,1)S(1)}, bf16[2,128,1024]{2,1,0:T(8,128)(2,1)S(1)}, u32[]{:S(2)}, u32[]{:S(2)}) collective-permute-start(bf16[2,128,1024]{2,1,0:T(8,128)(2,1)S(1)} %pad_maximum_fusion.5), channel_id=1, source_target_pairs={{0,1},{1,0},{2,3},{3,2},{4,5},{5,4},{6,7},{7,6},{8,9},{9,8},{10,11... | collective-permute-start | bytes 1572872 | tf_op jit(solution)/shard_map/ppermute | solution.py:28
  73.8 1.8 %collective-permute-start.21 = (bf16[2,128,768]{2,1,0:T(8,128)(2,1)S(1)}, bf16[2,128,768]{2,1,0:T(8,128)(2,1)S(1)}, u32[]{:S(2)}, u32[]{:S(2)}) collective-permute-start(bf16[2,128,768]{2,1,0:T(8,128)(2,1)S(1)} %pad_maximum_fusion.8), channel_id=1, source_target_pairs={{0,1},{1,0},{2,3},{3,2},{4,5},{5,4},{6,7},{7,6},{8,9},{9,8},{10,11... | collective-permute-start | bytes 1179656 | tf_op jit(solution)/shard_map/ppermute | solution.py:28
  79.2 7.8 %collective-permute-start.22 = (bf16[64,1536]{1,0:T(8,128)(2,1)S(1)}, bf16[64,1536]{1,0:T(8,128)(2,1)S(1)}, u32[]{:S(2)}, u32[]{:S(2)}) collective-permute-start(bf16[64,1536]{1,0:T(8,128)(2,1)S(1)} %pad_maximum_fusion.13), channel_id=1, source_target_pairs={{0,4},{4,0},{8,12},{12,8},{16,20},{20,16},{24,28},{28,24},{1,5},{5... | collective-permute-start | bytes 589832 | tf_op jit(solution)/shard_map/ppermute | solution.py:33
  80.6 10.6 %collective-permute-start.23 = (bf16[64,1536]{1,0:T(8,128)(2,1)S(1)}, bf16[64,1536]{1,0:T(8,128)(2,1)S(1)}, u32[]{:S(2)}, u32[]{:S(2)}) collective-permute-start(bf16[64,1536]{1,0:T(8,128)(2,1)S(1)} %pad_maximum_fusion.14), channel_id=1, source_target_pairs={{0,4},{4,0},{8,12},{12,8},{16,20},{20,16},{24,28},{28,24},{1,5},{5... | collective-permute-start | bytes 589832 | tf_op jit(solution)/shard_map/ppermute | solution.py:33
  87.0 5.7 %collective-permute-start.25 = (bf16[64,1536]{1,0:T(8,128)(2,1)S(1)}, bf16[64,1536]{1,0:T(8,128)(2,1)S(1)}, u32[]{:S(2)}, u32[]{:S(2)}) collective-permute-start(bf16[64,1536]{1,0:T(8,128)(2,1)S(1)} %fusion.61), channel_id=1, source_target_pairs={{0,8},{4,12},{8,0},{12,4},{16,24},{20,28},{24,16},{28,20},{1,9},{5... | collective-permute-start | bytes 589832 | tf_op jit(solution)/shard_map/ppermute | solution.py:33
  88.3 9.1 %collective-permute-start.27 = (bf16[64,1536]{1,0:T(8,128)(2,1)S(1)}, bf16[64,1536]{1,0:T(8,128)(2,1)S(1)}, u32[]{:S(2)}, u32[]{:S(2)}) collective-permute-start(bf16[64,1536]{1,0:T(8,128)(2,1)S(1)} %get-tuple-element.88), channel_id=1, source_target_pairs={{0,4},{4,0},{8,12},{12,8},{16,20},{20,16},{24,28},{28,24},{1,5},{5... | collective-permute-start | bytes 589832 | tf_op jit(solution)/shard_map/ppermute | solution.py:33
  91.2 10.2 %collective-permute-start.24 = (bf16[64,1536]{1,0:T(8,128)(2,1)S(1)}, bf16[64,1536]{1,0:T(8,128)(2,1)S(1)}, u32[]{:S(2)}, u32[]{:S(2)}) collective-permute-start(bf16[64,1536]{1,0:T(8,128)(2,1)S(1)} %get-tuple-element.86), channel_id=1, source_target_pairs={{0,4},{4,0},{8,12},{12,8},{16,20},{20,16},{24,28},{28,24},{1,5},{5... | collective-permute-start | bytes 589832 | tf_op jit(solution)/shard_map/ppermute | solution.py:33
  92.8 13.0 %collective-permute-start.26 = (bf16[64,1536]{1,0:T(8,128)(2,1)S(1)}, bf16[64,1536]{1,0:T(8,128)(2,1)S(1)}, u32[]{:S(2)}, u32[]{:S(2)}) collective-permute-start(bf16[64,1536]{1,0:T(8,128)(2,1)S(1)} %fusion.60), channel_id=1, source_target_pairs={{0,16},{4,20},{8,24},{12,28},{16,0},{20,4},{24,8},{28,12},{1,17},{... | collective-permute-start | bytes 589832 | tf_op jit(solution)/shard_map/ppermute | solution.py:33
  97.4 8.4 %collective-permute-start.28 = (bf16[64,1536]{1,0:T(8,128)(2,1)S(1)}, bf16[64,1536]{1,0:T(8,128)(2,1)S(1)}, u32[]{:S(2)}, u32[]{:S(2)}) collective-permute-start(bf16[64,1536]{1,0:T(8,128)(2,1)S(1)} %fusion.62.refs_0_), channel_id=1, source_target_pairs={{0,8},{4,12},{8,0},{12,4},{16,24},{20,28},{24,16},{28,20},{1,9},{5... | collective-permute-start | bytes 589832 | tf_op jit(solution)/shard_map/ppermute | solution.py:33
  106.2 3.2 %collective-permute-start.31 = (f32[32,128]{1,0:T(8,128)S(1)}, f32[32,128]{1,0:T(8,128)S(1)}, u32[]{:S(2)}, u32[]{:S(2)}) collective-permute-start(f32[32,128]{1,0:T(8,128)S(1)} %get-tuple-element.92.refs_0_), channel_id=1, source_target_pairs={{0,3},{1,2},{2,1},{3,0},{4,7},{5,6},{6,5},{7,4},{8,11},{9,10},{10,... | collective-permute-start | bytes 49160 | tf_op jit(solution)/shard_map/ppermute | solution.py:28
  106.3 3.9 %collective-permute-start.30 = (f32[32,128]{1,0:T(8,128)S(1)}, f32[32,128]{1,0:T(8,128)S(1)}, u32[]{:S(2)}, u32[]{:S(2)}) collective-permute-start(f32[32,128]{1,0:T(8,128)S(1)} %get-tuple-element.92.refs_0_), channel_id=1, source_target_pairs={{0,2},{1,3},{2,0},{3,1},{4,6},{5,7},{6,4},{7,5},{8,10},{9,11},{10,... | collective-permute-start | bytes 49160 | tf_op jit(solution)/shard_map/ppermute | solution.py:28
  107.3 2.9 %collective-permute-start.29 = (f32[32,128]{1,0:T(8,128)S(1)}, f32[32,128]{1,0:T(8,128)S(1)}, u32[]{:S(2)}, u32[]{:S(2)}) collective-permute-start(f32[32,128]{1,0:T(8,128)S(1)} %get-tuple-element.92.refs_0_), channel_id=1, source_target_pairs={{0,1},{1,0},{2,3},{3,2},{4,5},{5,4},{6,7},{7,6},{8,9},{9,8},{10,11... | collective-permute-start | bytes 49160 | tf_op jit(solution)/shard_map/ppermute | solution.py:28
  111.0 7.2 %collective-permute-start.35 = (bf16[32,1536]{1,0:T(8,128)(2,1)S(1)}, bf16[32,1536]{1,0:T(8,128)(2,1)S(1)}, u32[]{:S(2)}, u32[]{:S(2)}) collective-permute-start(bf16[32,1536]{1,0:T(8,128)(2,1)S(1)} %cotangent_kernel.1), channel_id=1, source_target_pairs={{0,16},{4,20},{8,24},{12,28},{16,0},{20,4},{24,8},{28,12},{1,17},{... | collective-permute-start | bytes 294920 | tf_op jit(solution)/shard_map/ppermute | solution.py:33
  111.1 8.2 %collective-permute-start.33 = (bf16[32,1536]{1,0:T(8,128)(2,1)S(1)}, bf16[32,1536]{1,0:T(8,128)(2,1)S(1)}, u32[]{:S(2)}, u32[]{:S(2)}) collective-permute-start(bf16[32,1536]{1,0:T(8,128)(2,1)S(1)} %cotangent_kernel.1), channel_id=1, source_target_pairs={{0,8},{4,12},{8,0},{12,4},{16,24},{20,28},{24,16},{28,20},{1,9},{5... | collective-permute-start | bytes 294920 | tf_op jit(solution)/shard_map/ppermute | solution.py:33
  112.7 7.6 %collective-permute-start.32 = (bf16[32,1536]{1,0:T(8,128)(2,1)S(1)}, bf16[32,1536]{1,0:T(8,128)(2,1)S(1)}, u32[]{:S(2)}, u32[]{:S(2)}) collective-permute-start(bf16[32,1536]{1,0:T(8,128)(2,1)S(1)} %cotangent_kernel.1), channel_id=1, source_target_pairs={{0,4},{4,0},{8,12},{12,8},{16,20},{20,16},{24,28},{28,24},{1,5},{5... | collective-permute-start | bytes 294920 | tf_op jit(solution)/shard_map/ppermute | solution.py:33
  118.2 4.7 %collective-permute-start.37 = (bf16[32,1536]{1,0:T(8,128)(2,1)S(1)}, bf16[32,1536]{1,0:T(8,128)(2,1)S(1)}, u32[]{:S(2)}, u32[]{:S(2)}) collective-permute-start(bf16[32,1536]{1,0:T(8,128)(2,1)S(1)} %collective-permute-done.35), channel_id=1, source_target_pairs={{0,8},{4,12},{8,0},{12,4},{16,24},{20,28},{24,16},{28,20},{1,9},{5... | collective-permute-start | bytes 294920 | tf_op jit(solution)/shard_map/ppermute | solution.py:33
  118.2 7.1 %collective-permute-start.36 = (bf16[32,1536]{1,0:T(8,128)(2,1)S(1)}, bf16[32,1536]{1,0:T(8,128)(2,1)S(1)}, u32[]{:S(2)}, u32[]{:S(2)}) collective-permute-start(bf16[32,1536]{1,0:T(8,128)(2,1)S(1)} %collective-permute-done.35), channel_id=1, source_target_pairs={{0,4},{4,0},{8,12},{12,8},{16,20},{20,16},{24,28},{28,24},{1,5},{5... | collective-permute-start | bytes 294920 | tf_op jit(solution)/shard_map/ppermute | solution.py:33
  119.3 6.0 %collective-permute-start.34 = (bf16[32,1536]{1,0:T(8,128)(2,1)S(1)}, bf16[32,1536]{1,0:T(8,128)(2,1)S(1)}, u32[]{:S(2)}, u32[]{:S(2)}) collective-permute-start(bf16[32,1536]{1,0:T(8,128)(2,1)S(1)} %collective-permute-done.33), channel_id=1, source_target_pairs={{0,4},{4,0},{8,12},{12,8},{16,20},{20,16},{24,28},{28,24},{1,5},{5... | collective-permute-start | bytes 294920 | tf_op jit(solution)/shard_map/ppermute | solution.py:33
  122.9 4.6 %collective-permute-start.38 = (bf16[32,1536]{1,0:T(8,128)(2,1)S(1)}, bf16[32,1536]{1,0:T(8,128)(2,1)S(1)}, u32[]{:S(2)}, u32[]{:S(2)}) collective-permute-start(bf16[32,1536]{1,0:T(8,128)(2,1)S(1)} %collective-permute-done.37), channel_id=1, source_target_pairs={{0,4},{4,0},{8,12},{12,8},{16,20},{20,16},{24,28},{28,24},{1,5},{5... | collective-permute-start | bytes 294920 | tf_op jit(solution)/shard_map/ppermute | solution.py:33
  128.9 1.7 %collective-permute-start.39 = (bf16[128,1280]{1,0:T(8,128)(2,1)S(1)}, bf16[128,1280]{1,0:T(8,128)(2,1)S(1)}, u32[]{:S(2)}, u32[]{:S(2)}) collective-permute-start(bf16[128,1280]{1,0:T(8,128)(2,1)S(1)} %get-tuple-element.97), channel_id=1, source_target_pairs={{0,1},{1,0},{2,3},{3,2},{4,5},{5,4},{6,7},{7,6},{8,9},{9,8},{10,11... | collective-permute-start | bytes 983048 | tf_op jit(solution)/shard_map/ppermute | solution.py:28
  130.1 2.4 %collective-permute-start.43 = (bf16[128,1024]{1,0:T(8,128)(2,1)S(1)}, bf16[128,1024]{1,0:T(8,128)(2,1)S(1)}, u32[]{:S(2)}, u32[]{:S(2)}) collective-permute-start(bf16[128,1024]{1,0:T(8,128)(2,1)S(1)} %get-tuple-element.100), channel_id=1, source_target_pairs={{0,1},{1,0},{2,3},{3,2},{4,5},{5,4},{6,7},{7,6},{8,9},{9,8},{10,11... | collective-permute-start | bytes 786440 | tf_op jit(solution)/shard_map/ppermute | solution.py:28
  130.7 10.6 %collective-permute-start.42 = (bf16[128,1280]{1,0:T(8,128)(2,1)S(1)}, bf16[128,1280]{1,0:T(8,128)(2,1)S(1)}, u32[]{:S(2)}, u32[]{:S(2)}) collective-permute-start(bf16[128,1280]{1,0:T(8,128)(2,1)S(1)} %get-tuple-element.106), channel_id=1, source_target_pairs={{0,2},{1,3},{2,0},{3,1},{4,6},{5,7},{6,4},{7,5},{8,10},{9,11},{10,... | collective-permute-start | bytes 983048 | tf_op jit(solution)/shard_map/ppermute | solution.py:28
  132.3 1.5 collective-permute-start.40
  132.5 14.4 %collective-permute-start.46 = (bf16[128,1024]{1,0:T(8,128)(2,1)S(1)}, bf16[128,1024]{1,0:T(8,128)(2,1)S(1)}, u32[]{:S(2)}, u32[]{:S(2)}) collective-permute-start(bf16[128,1024]{1,0:T(8,128)(2,1)S(1)} %get-tuple-element.104), channel_id=1, source_target_pairs={{0,2},{1,3},{2,0},{3,1},{4,6},{5,7},{6,4},{7,5},{8,10},{9,11},{10,... | collective-permute-start | bytes 786440 | tf_op jit(solution)/shard_map/ppermute | solution.py:28
  141.4 5.9 %collective-permute-start.44 = (bf16[128,1280]{1,0:T(8,128)(2,1)S(1)}, bf16[128,1280]{1,0:T(8,128)(2,1)S(1)}, u32[]{:S(2)}, u32[]{:S(2)}) collective-permute-start(bf16[128,1280]{1,0:T(8,128)(2,1)S(1)} %multiply_convert_fusion), channel_id=1, source_target_pairs={{0,1},{1,0},{2,3},{3,2},{4,5},{5,4},{6,7},{7,6},{8,9},{9,8},{10,11... | collective-permute-start | bytes 983048 | tf_op jit(solution)/shard_map/ppermute | solution.py:28
  141.5 9.5 %collective-permute-start.41 = (bf16[128,768]{1,0:T(8,128)(2,1)S(1)}, bf16[128,768]{1,0:T(8,128)(2,1)S(1)}, u32[]{:S(2)}, u32[]{:S(2)}) collective-permute-start(bf16[128,768]{1,0:T(8,128)(2,1)S(1)} %get-tuple-element.108), channel_id=1, source_target_pairs={{0,2},{1,3},{2,0},{3,1},{4,6},{5,7},{6,4},{7,5},{8,10},{9,11},{10,... | collective-permute-start | bytes 589832 | tf_op jit(solution)/shard_map/ppermute | solution.py:28
  147.2 4.5 %collective-permute-start.47 = (bf16[128,1024]{1,0:T(8,128)(2,1)S(1)}, bf16[128,1024]{1,0:T(8,128)(2,1)S(1)}, u32[]{:S(2)}, u32[]{:S(2)}) collective-permute-start(bf16[128,1024]{1,0:T(8,128)(2,1)S(1)} %multiply_convert_fusion.1), channel_id=1, source_target_pairs={{0,1},{1,0},{2,3},{3,2},{4,5},{5,4},{6,7},{7,6},{8,9},{9,8},{10,11... | collective-permute-start | bytes 786440 | tf_op jit(solution)/shard_map/ppermute | solution.py:28
  151.2 3.6 %collective-permute-start.45 = (bf16[128,768]{1,0:T(8,128)(2,1)S(1)}, bf16[128,768]{1,0:T(8,128)(2,1)S(1)}, u32[]{:S(2)}, u32[]{:S(2)}) collective-permute-start(bf16[128,768]{1,0:T(8,128)(2,1)S(1)} %multiply_convert_fusion.3), channel_id=1, source_target_pairs={{0,1},{1,0},{2,3},{3,2},{4,5},{5,4},{6,7},{7,6},{8,9},{9,8},{10,11... | collective-permute-start | bytes 589832 | tf_op jit(solution)/shard_map/ppermute | solution.py:28
  (10 other events, 42.3 us)
